TPU v7x, 32 devices: a whole 2x2x4 slice. The times are simulated.
32 devices in a mesh: batch: 4 (over y, x), head: 8 (over z, core).
Axes of the slice: x: 2, y: 2, z: 4, core: 2. Of those that a mesh axis runs over, the one named last changes fastest.
Arguments:
- tokens: bfloat16 [8192, 2048], P(('batch', 'head')), may hold values from -6 to 6
- cotangent: bfloat16 [8192, 2048], P(('batch', 'head')), may hold values from -6 to 6
- doc_starts: int32 [4, 4], P('batch'), may hold values from 1 to 2048, as said below
- owner: int32 [16], replicated, may hold values from 0 to 15, each once
- vectors: float32 [6, 2048], replicated, may hold values from -1 to 2
- bias_query: float32 [2048], P('head'), may hold values from -1.75 to 1.75
- bias_value: float32 [128], replicated, may hold values from -1.75 to 1.75
- bias_up: float32 [8192], P('head'), may hold values from -1.75 to 1.75
- w_query: bfloat16 [2048, 2048], P(None, 'head'), may hold values from -0.1875 to 0.1875
- w_key: bfloat16 [2048, 128], replicated, may hold values from -0.125 to 0.125
- w_value: bfloat16 [2048, 128], replicated, may hold values from -0.125 to 0.125
- w_out: bfloat16 [2048, 2048], P('head'), may hold values from -2 to 2
- w_up: bfloat16 [2048, 8192], P(None, 'head'), may hold values from -0.125 to 0.125
- w_down: bfloat16 [8192, 2048], P('head'), may hold values from -0.0625 to 0.0625
- attn_left: float32 [2, 16, 16, 128, 128], P(None, 'batch', 'head')
- attn_right: float32 [2, 16, 16, 128, 128], P(None, 'batch', 'head')
- attn_root_left: float32 [2, 16, 16, 128, 128], P(None, 'batch', 'head')
- attn_root_right: float32 [2, 16, 16, 128, 128], P(None, 'batch', 'head')
- mixer_left: float32 [2, 16, 64, 128, 128], P(None, 'batch', 'head')
- mixer_right: float32 [2, 16, 64, 128, 128], P(None, 'batch', 'head')
- mixer_root_left: float32 [2, 16, 64, 128, 128], P(None, 'batch', 'head')
- mixer_root_right: float32 [2, 16, 64, 128, 128], P(None, 'batch', 'head')
- kv_left: float32 [2, 16, 1, 128, 128], P(None, 'head')
- kv_right: float32 [2, 16, 1, 128, 128], P(None, 'head')
- kv_root_left: float32 [2, 16, 1, 128, 128], P(None, 'head')
- kv_root_right: float32 [2, 16, 1, 128, 128], P(None, 'head')
- vector_second: float32 [6, 2048], replicated
- query_second: float32 [2048], P('head')
- value_second: float32 [128], replicated
- up_second: float32 [8192], P('head')
Outputs:
- output: float32 [8192, 2048], P(('batch', 'head'))
- grad_tokens: float32 [8192, 2048], P(('batch', 'head'))
- vector_grad: float32 [6, 2048], replicated
- vector_second_new: float32 [4, 2048], replicated
- first_norm_second: float32 [2, 2048], replicated
- vector_new: float32 [6, 2048], replicated
- query_bias_grad: float32 [2048], P('head')
- query_second_new: float32 [2048], P('head')
- query_bias_new: float32 [2048], P('head')
- value_bias_grad: float32 [128], replicated
- value_second_new: float32 [128], replicated
- value_bias_new: float32 [128], replicated
- up_bias_grad: float32 [8192], P('head')
- up_second_new: float32 [8192], P('head')
- up_bias_new: float32 [8192], P('head')
- attn_grad: float32 [2, 16, 16, 128, 128], P(None, 'batch', 'head')
- attn_left_new: float32 [2, 16, 16, 128, 128], P(None, 'batch', 'head')
- attn_right_new: float32 [2, 16, 16, 128, 128], P(None, 'batch', 'head')
- attn_weight_new: float32 [2, 16, 16, 128, 128], P(None, 'batch', 'head')
- mixer_grad: float32 [2, 16, 64, 128, 128], P(None, 'batch', 'head')
- mixer_left_new: float32 [2, 16, 64, 128, 128], P(None, 'batch', 'head')
- mixer_right_new: float32 [2, 16, 64, 128, 128], P(None, 'batch', 'head')
- mixer_weight_new: float32 [2, 16, 64, 128, 128], P(None, 'batch', 'head')
- kv_grad: float32 [2, 16, 1, 128, 128], P(None, 'head')
- kv_left_new: float32 [2, 16, 1, 128, 128], P(None, 'head')
- kv_right_new: float32 [2, 16, 1, 128, 128], P(None, 'head')
- kv_weight_new: float32 [2, 16, 1, 128, 128], P(None, 'head')
Inputs may be any that keep to these rules, and one draw needn't show every extreme that they name: `doc_starts`: in every draw one sequence has all its entries equal to 2048, so that it is one document; entries need not be sorted.
All inputs are finite; a program needn't handle non-finite values.
Results may differ from a plain program's by a relative error of at most 0.013.
Values may be sent and summed in bfloat16 or wider, within the bound.
A program may use at most 384 MiB of HBM per device.

v0:
```python
from functools import partial
import math

import jax
import jax.numpy as jnp
from jax import lax
from jax.sharding import PartitionSpec as P

QUERY_ROWS = 512


EPSILON = 1e-05
DECAY_RATE = 0.5
MATRIX_RATE = 0.01
VECTOR_RATE = 0.1
SAFE_ADD = 1e-08
PRECISE = lax.Precision.HIGHEST


def matmul(first_op, second_op):
    return jnp.dot(first_op, second_op, preferred_element_type=jnp.float32)


def matmul_t(first_op, second_op):
    return lax.dot_general(
        first_op, second_op, (((0,), (0,)), ((), ())), preferred_element_type=jnp.float32
    )


def matmul_nt(first_op, second_op):
    return lax.dot_general(
        first_op, second_op, (((1,), (1,)), ((), ())), preferred_element_type=jnp.float32
    )


def norm_stats(rows_in):
    mean_row = jnp.mean(rows_in, axis=-1, keepdims=True)
    centered = rows_in - mean_row
    variance = jnp.mean(centered * centered, axis=-1, keepdims=True)
    inverse = lax.rsqrt(variance + EPSILON)
    return (centered * inverse, inverse)


def norm_back(grad_out, normed, inverse, gain):
    scaled = grad_out * gain
    mean_one = jnp.mean(scaled, axis=-1, keepdims=True)
    mean_two = jnp.mean(scaled * normed, axis=-1, keepdims=True)
    return inverse * (scaled - mean_one - normed * mean_two)


def tile_mask(documents, positions, first_row):
    row_ids = first_row + jnp.arange(QUERY_ROWS, dtype=jnp.int32)
    row_docs = lax.dynamic_slice_in_dim(documents, first_row, QUERY_ROWS, 0)
    return (row_docs[:, None] == documents[None, :]) & (positions[None, :] <= row_ids[:, None])


def attention_forward(queries, key_rows, value_rows, documents, heads_dev):
    seq_len, head_size = key_rows.shape
    tile_count = seq_len // QUERY_ROWS
    score_scale = 1.0 / math.sqrt(head_size)
    shaped = queries.reshape(seq_len, heads_dev, head_size)
    positions = jnp.arange(seq_len, dtype=jnp.int32)

    def one_tile(tile_index):
        first_row = tile_index * QUERY_ROWS
        query_tile = lax.dynamic_slice_in_dim(shaped, first_row, QUERY_ROWS, 0)
        allowed = tile_mask(documents, positions, first_row)
        scores = (
            jnp.einsum("qhd,kd->hqk", query_tile, key_rows, preferred_element_type=jnp.float32)
            * score_scale
        )
        scores = jnp.where(allowed[None], scores, -1e30)
        highest = jnp.max(scores, axis=-1, keepdims=True)
        raised = jnp.exp(scores - highest)
        totals = jnp.sum(raised, axis=-1, keepdims=True)
        attention = (raised / totals).astype(jnp.bfloat16)
        tile_out = jnp.einsum(
            "hqk,kd->qhd", attention, value_rows, preferred_element_type=jnp.float32
        )
        return (
            tile_out.astype(jnp.bfloat16).reshape(QUERY_ROWS, heads_dev * head_size),
            (highest + jnp.log(totals))[..., 0],
        )

    tile_outs, log_totals = lax.map(one_tile, jnp.arange(tile_count, dtype=jnp.int32))
    return (tile_outs.reshape(seq_len, heads_dev * head_size), log_totals)


def attention_backward(
    queries, key_rows, value_rows, documents, log_totals, grad_attended, heads_dev
):
    seq_len, head_size = key_rows.shape
    tile_count = seq_len // QUERY_ROWS
    score_scale = 1.0 / math.sqrt(head_size)
    shaped = queries.reshape(seq_len, heads_dev, head_size)
    grad_shaped = grad_attended.reshape(seq_len, heads_dev, head_size)
    positions = jnp.arange(seq_len, dtype=jnp.int32)

    def one_tile(carry, element):
        grad_keys, grad_values = carry
        tile_index, tile_totals = element
        first_row = tile_index * QUERY_ROWS
        query_tile = lax.dynamic_slice_in_dim(shaped, first_row, QUERY_ROWS, 0)
        grad_tile = lax.dynamic_slice_in_dim(grad_shaped, first_row, QUERY_ROWS, 0)
        allowed = tile_mask(documents, positions, first_row)
        scores = (
            jnp.einsum("qhd,kd->hqk", query_tile, key_rows, preferred_element_type=jnp.float32)
            * score_scale
        )
        scores = jnp.where(allowed[None], scores, -1e30)
        attention = jnp.exp(scores - tile_totals[..., None])
        grad_probs = jnp.einsum(
            "qhd,kd->hqk", grad_tile, value_rows, preferred_element_type=jnp.float32
        )
        inner = jnp.sum(attention * grad_probs, axis=-1, keepdims=True)
        grad_scores = (attention * (grad_probs - inner)).astype(jnp.bfloat16)
        grad_query = (
            jnp.einsum("hqk,kd->qhd", grad_scores, key_rows, preferred_element_type=jnp.float32)
            * score_scale
        )
        grad_keys = (
            grad_keys
            + jnp.einsum("hqk,qhd->kd", grad_scores, query_tile, preferred_element_type=jnp.float32)
            * score_scale
        )
        grad_values = grad_values + jnp.einsum(
            "hqk,qhd->kd",
            attention.astype(jnp.bfloat16),
            grad_tile,
            preferred_element_type=jnp.float32,
        )
        return ((grad_keys, grad_values), grad_query.reshape(QUERY_ROWS, heads_dev * head_size))

    zero_rows = jnp.zeros((seq_len, head_size), jnp.float32)
    (grad_keys, grad_values), grad_queries = lax.scan(
        one_tile, (zero_rows, zero_rows), (jnp.arange(tile_count, dtype=jnp.int32), log_totals)
    )
    return (grad_queries.reshape(seq_len, heads_dev * head_size), grad_keys, grad_values)


def row_tiles(matrix, tile_size):
    return matrix.reshape(
        matrix.shape[0] // tile_size, tile_size, matrix.shape[1] // tile_size, tile_size
    ).transpose(0, 2, 1, 3)


def col_tiles(matrix, tile_size):
    return matrix.reshape(
        matrix.shape[0] // tile_size, tile_size, matrix.shape[1] // tile_size, tile_size
    ).transpose(2, 0, 1, 3)


def shampoo_update(grad_tiles, left_old, right_old, root_left, root_right, weight_tiles):
    outer_left = jnp.einsum("...ij,...kj->...ik", grad_tiles, grad_tiles, precision=PRECISE)
    outer_right = jnp.einsum("...ji,...jk->...ik", grad_tiles, grad_tiles, precision=PRECISE)
    left_new = DECAY_RATE * left_old + (1.0 - DECAY_RATE) * outer_left
    right_new = DECAY_RATE * right_old + (1.0 - DECAY_RATE) * outer_right
    stepped = jnp.einsum("...ij,...jk->...ik", root_left, grad_tiles, precision=PRECISE)
    stepped = jnp.einsum("...ij,...jk->...ik", stepped, root_right, precision=PRECISE)
    return (grad_tiles, left_new, right_new, weight_tiles - MATRIX_RATE * stepped)


def diagonal_update(gradient, second, current):
    second_new = DECAY_RATE * second + (1.0 - DECAY_RATE) * gradient * gradient
    return (
        gradient,
        second_new,
        current - VECTOR_RATE * gradient / (jnp.sqrt(second_new) + SAFE_ADD),
    )


def body(
    tokens,
    cotangent,
    doc_starts,
    owner,
    vectors,
    bias_query,
    bias_value,
    bias_up,
    w_query,
    w_key,
    w_value,
    w_out,
    w_up,
    w_down,
    attn_left,
    attn_right,
    attn_root_left,
    attn_root_right,
    mixer_left,
    mixer_right,
    mixer_root_left,
    mixer_root_right,
    kv_left,
    kv_right,
    kv_root_left,
    kv_root_right,
    vector_second,
    query_second,
    value_second,
    up_second,
):
    tok_dev = tokens.shape[0]
    seq_len = tok_dev * lax.axis_size("head")
    head_index = lax.axis_index("head")
    row_start = head_index * tok_dev
    head_size = w_key.shape[1]
    heads_dev = w_query.shape[1] // head_size
    tile_size = attn_left.shape[-1]
    gain_one = vectors[0]
    shift_one = vectors[1]
    gain_two = vectors[2]
    shift_two = vectors[3]
    bias_attn = vectors[4]
    bias_down = vectors[5]
    positions = jnp.arange(seq_len, dtype=jnp.int32)
    documents = jnp.sum((doc_starts[0][None, :] <= positions[:, None]).astype(jnp.int32), axis=1)
    rows_all = lax.all_gather(tokens, "head", axis=0, tiled=True).astype(jnp.float32)
    normed_all, inverse_all = norm_stats(rows_all)
    normed_one = lax.dynamic_slice_in_dim(normed_all, row_start, tok_dev, 0)
    inverse_one = lax.dynamic_slice_in_dim(inverse_all, row_start, tok_dev, 0)
    normed_in = (normed_all * gain_one + shift_one).astype(jnp.bfloat16)
    queries = (matmul(normed_in, w_query) + bias_query).astype(jnp.bfloat16)
    key_rows = matmul(normed_in, w_key).astype(jnp.bfloat16)
    value_rows = (matmul(normed_in, w_value) + bias_value).astype(jnp.bfloat16)
    attended, log_totals = attention_forward(queries, key_rows, value_rows, documents, heads_dev)
    attn_all = lax.psum(matmul(attended, w_out), "head")
    resid_all = rows_all + attn_all + bias_attn
    normed_all_two, inverse_all_two = norm_stats(resid_all)
    resid_one = lax.dynamic_slice_in_dim(resid_all, row_start, tok_dev, 0)
    normed_two = lax.dynamic_slice_in_dim(normed_all_two, row_start, tok_dev, 0)
    inverse_two = lax.dynamic_slice_in_dim(inverse_all_two, row_start, tok_dev, 0)
    mixer_in = (normed_all_two * gain_two + shift_two).astype(jnp.bfloat16)
    pre_act = matmul(mixer_in, w_up) + bias_up
    hidden_f, gelu_pull = jax.vjp(partial(jax.nn.gelu, approximate=True), pre_act)
    hidden = hidden_f.astype(jnp.bfloat16)
    mix_one = lax.psum_scatter(
        matmul(lax.slice_in_dim(hidden, 0, tok_dev * lax.axis_size("head"), axis=0), w_down),
        "head",
        scatter_dimension=0,
        tiled=True,
    )
    output = resid_one + mix_one + bias_down
    cot_one = cotangent.astype(jnp.float32)
    grad_down_bias = jnp.sum(cot_one, axis=0)
    cot_all = lax.all_gather(cotangent, "head", axis=0, tiled=True)
    grad_w_down = matmul_t(hidden, cot_all)
    grad_hidden = matmul_nt(cot_all, w_down)
    grad_pre = gelu_pull(grad_hidden)[0].astype(jnp.bfloat16)
    grad_up_bias = jnp.sum(grad_pre.astype(jnp.float32), axis=0)
    grad_w_up = matmul_t(mixer_in, grad_pre)
    grad_mixer_in = lax.psum_scatter(
        matmul_nt(grad_pre, w_up), "head", scatter_dimension=0, tiled=True
    )
    grad_gain_two = jnp.sum(grad_mixer_in * normed_two, axis=0)
    grad_shift_two = jnp.sum(grad_mixer_in, axis=0)
    grad_resid = cot_one + norm_back(grad_mixer_in, normed_two, inverse_two, gain_two)
    grad_branch = grad_resid.astype(jnp.bfloat16)
    grad_attn_bias = jnp.sum(grad_branch.astype(jnp.float32), axis=0)
    branch_all = lax.all_gather(grad_branch, "head", axis=0, tiled=True)
    grad_w_out = matmul_t(attended, branch_all)
    grad_attended = matmul_nt(branch_all, w_out).astype(jnp.bfloat16)
    grad_q_f, grad_k_f, grad_v_f = attention_backward(
        queries, key_rows, value_rows, documents, log_totals, grad_attended, heads_dev
    )
    grad_q = grad_q_f.astype(jnp.bfloat16)
    grad_k = grad_k_f.astype(jnp.bfloat16)
    grad_v = grad_v_f.astype(jnp.bfloat16)
    grad_query_bias = jnp.sum(grad_q.astype(jnp.float32), axis=0)
    grad_value_bias = jnp.sum(grad_v.astype(jnp.float32), axis=0)
    grad_w_query = matmul_t(normed_in, grad_q)
    grad_w_key = matmul_t(normed_in, grad_k)
    grad_w_value = matmul_t(normed_in, grad_v)
    grad_normed_in = lax.psum_scatter(
        matmul_nt(grad_q, w_query) + matmul_nt(grad_k, w_key) + matmul_nt(grad_v, w_value),
        "head",
        scatter_dimension=0,
        tiled=True,
    )
    grad_gain_one = jnp.sum(grad_normed_in * normed_one, axis=0)
    grad_shift_one = jnp.sum(grad_normed_in, axis=0)
    grad_tokens = grad_resid + norm_back(grad_normed_in, normed_one, inverse_one, gain_one)
    key_share, value_share = (
        lax.psum_scatter(grad_w_key, "head", scatter_dimension=0, tiled=True),
        lax.psum_scatter(grad_w_value, "head", scatter_dimension=0, tiled=True),
    )
    key_total, value_total, query_bias_total, up_bias_total = lax.psum(
        (key_share, value_share, grad_query_bias, grad_up_bias), "batch"
    )
    vector_part = jnp.stack(
        [
            grad_gain_one,
            grad_shift_one,
            grad_gain_two,
            grad_shift_two,
            grad_attn_bias,
            grad_down_bias,
        ]
    )
    vector_total, value_bias_total = lax.psum((vector_part, grad_value_bias), ("batch", "head"))
    attn_stack = jnp.stack([row_tiles(grad_w_query, tile_size), col_tiles(grad_w_out, tile_size)])
    mixer_stack = jnp.stack([row_tiles(grad_w_up, tile_size), col_tiles(grad_w_down, tile_size)])
    attn_stack = jnp.take(attn_stack, owner, axis=1)
    mixer_stack = jnp.take(mixer_stack, owner, axis=1)
    attn_own, mixer_own = (
        lax.psum_scatter(attn_stack, "batch", scatter_dimension=1, tiled=True),
        lax.psum_scatter(mixer_stack, "batch", scatter_dimension=1, tiled=True),
    )
    owned_count = attn_own.shape[1]
    owned_ids = lax.dynamic_slice_in_dim(
        owner, lax.axis_index("batch") * owned_count, owned_count, 0
    )
    attn_weight = jnp.stack(
        [
            jnp.take(row_tiles(w_query, tile_size), owned_ids, axis=0),
            jnp.take(col_tiles(w_out, tile_size), owned_ids, axis=0),
        ]
    ).astype(jnp.float32)
    mixer_weight = jnp.stack(
        [
            jnp.take(row_tiles(w_up, tile_size), owned_ids, axis=0),
            jnp.take(col_tiles(w_down, tile_size), owned_ids, axis=0),
        ]
    ).astype(jnp.float32)
    kv_count = key_total.shape[0]
    key_slab = lax.dynamic_slice_in_dim(w_key, head_index * kv_count, kv_count, 0)
    value_slab = lax.dynamic_slice_in_dim(w_value, head_index * kv_count, kv_count, 0)
    kv_weight = jnp.stack(
        [row_tiles(key_slab, tile_size), row_tiles(value_slab, tile_size)]
    ).astype(jnp.float32)
    kv_stack = jnp.stack([row_tiles(key_total, tile_size), row_tiles(value_total, tile_size)])
    attn_out = shampoo_update(
        attn_own, attn_left, attn_right, attn_root_left, attn_root_right, attn_weight
    )
    mixer_out = shampoo_update(
        mixer_own, mixer_left, mixer_right, mixer_root_left, mixer_root_right, mixer_weight
    )
    kv_out = shampoo_update(kv_stack, kv_left, kv_right, kv_root_left, kv_root_right, kv_weight)
    vec_out = diagonal_update(vector_total, vector_second, vectors)
    query_out = diagonal_update(query_bias_total, query_second, bias_query)
    value_out = diagonal_update(value_bias_total, value_second, bias_value)
    up_out = diagonal_update(up_bias_total, up_second, bias_up)
    return (
        output,
        grad_tokens,
        vec_out[0],
        vec_out[1][2:],
        vec_out[1][:2],
        vec_out[2],
        query_out[0],
        query_out[1],
        query_out[2],
        value_out[0],
        value_out[1],
        value_out[2],
        up_out[0],
        up_out[1],
        up_out[2],
        attn_out[0],
        attn_out[1],
        attn_out[2],
        attn_out[3],
        mixer_out[0],
        mixer_out[1],
        mixer_out[2],
        mixer_out[3],
        kv_out[0],
        kv_out[1],
        kv_out[2],
        kv_out[3],
    )


def solution(mesh):
    in_specs = (
        P(("batch", "head"), None),
        P(("batch", "head"), None),
        P("batch", None),
        P(),
        P(),
        P("head"),
        P(),
        P("head"),
        P(None, "head"),
        P(),
        P(),
        P("head", None),
        P(None, "head"),
        P("head", None),
        P(None, "batch", "head", None, None),
        P(None, "batch", "head", None, None),
        P(None, "batch", "head", None, None),
        P(None, "batch", "head", None, None),
        P(None, "batch", "head", None, None),
        P(None, "batch", "head", None, None),
        P(None, "batch", "head", None, None),
        P(None, "batch", "head", None, None),
        P(None, "head", None, None, None),
        P(None, "head", None, None, None),
        P(None, "head", None, None, None),
        P(None, "head", None, None, None),
        P(),
        P("head"),
        P(),
        P("head"),
    )
    out_specs = (
        P(("batch", "head"), None),
        P(("batch", "head"), None),
        P(),
        P(),
        P(),
        P(),
        P("head"),
        P("head"),
        P("head"),
        P(),
        P(),
        P(),
        P("head"),
        P("head"),
        P("head"),
        P(None, "batch", "head", None, None),
        P(None, "batch", "head", None, None),
        P(None, "batch", "head", None, None),
        P(None, "batch", "head", None, None),
        P(None, "batch", "head", None, None),
        P(None, "batch", "head", None, None),
        P(None, "batch", "head", None, None),
        P(None, "batch", "head", None, None),
        P(None, "head", None, None, None),
        P(None, "head", None, None, None),
        P(None, "head", None, None, None),
        P(None, "head", None, None, None),
    )
    return jax.shard_map(body, mesh=mesh, in_specs=in_specs, out_specs=out_specs, check_vma=False)
```

profile of v0, /device:TPU:0, one launch (start us, length us, event | category | flops | bytes accessed | tf_op | source)
XLA Modules:
  0.0 1733.9 jit_solution(4903899334301405845)
XLA Ops:
  10.5 83.9 %all-gather.4.cloned.1.call-done = bf16[2048,2048]{1,0:T(8,128)(2,1)} async-done(((bf16[256,2048]{1,0:T(8,128)(2,1)}), bf16[2048,2048]{1,0:T(8,128)(2,1)}) %all-gather.4.cloned.1.call-update) | async-done | bytes 8388624 | tf_op jit(solution)/shard_map/all_gather | solution.py:219
  94.4 4.7 convert_reduce_fusion
  102.6 7.1 fusion.48
  114.3 6.7 convolution_convert_fusion.1
  124.5 47.8 %while.28 = (s32[]{:T(128)}, bf16[4,512,256]{2,1,0:T(8,128)(2,1)}, f32[4,2,512]{2,1,0:T(2,128)S(1)}, s32[4]{0:T(128)S(1)}, s32[2048]{0:T(1024)S(1)}, /*index=5*/...) while((s32[]{:T(128)}, bf16[4,512,256]{2,1,0:T(8,128)(2,1)}, ...), condition=%wide.region_6.7_spmd.clone, body=%wide.region_3.6_spmd.clone.sunk | while | flops 1102183936 | bytes 34130152 | solution.py:85
  172.3 9.3 fusion.98
  182.5 330.7 %all-reduce.6.cloned.1.call-done = f32[2048,2048]{1,0:T(8,128)} async-done(((f32[2048,2048]{1,0:T(8,128)}), f32[2048,2048]{1,0:T(8,128)}) %all-reduce.6.cloned.1.call-update) | async-done | bytes 16777232 | tf_op jit(solution)/shard_map/psum | solution.py:228
  513.2 15.9 fusion.95
  529.1 7.7 multiply_reduce_fusion
  536.8 7.8 subtract_multiply_fusion
  544.6 5.7 copy-done.9
  550.4 11.0 fusion.61
  561.4 35.6 %all-gather.6.cloned.1.call-done = bf16[2048,2048]{1,0:T(8,128)(2,1)} async-done(((bf16[256,2048]{1,0:T(8,128)(2,1)}), bf16[2048,2048]{1,0:T(8,128)(2,1)}) %all-gather.6.cloned.1.call-update) | async-done | bytes 8388624 | tf_op jit(solution)/shard_map/all_gather | solution.py:247
  597.0 20.9 %convert_reduce_fusion.1 = (f32[1024]{0:T(1024)}, bf16[2048,1024]{1,0:T(8,128)(2,1)S(1)}) fusion(f32[2048,1024]{1,0:T(8,128)} %fusion.61, f32[1024]{0:T(1024)S(1)} %copy-done.56, bf16[2048,2048]{1,0:T(8,128)(2,1)} %all-gather.6.cloned.1.call-done, bf16[1024,2048]{1,0:T(8,128)(2,1)} %param.51), kind=kOutput, calls=%fused_computation.89 | convolution fusion | flops 8638168064 | bytes 25174016 | tf_op jit(solution)/shard_map/dot_general | solution.py:31
  620.0 11.8 fusion.99
  631.9 166.8 %reduce-scatter.10.cloned.1.call-done = f32[256,2048]{1,0:T(8,128)} async-done(((f32[2048,2048]{1,0:T(8,128)}), f32[256,2048]{1,0:T(8,128)}) %reduce-scatter.10.cloned.1.call-update) | async-done | bytes 2097168 | tf_op jit(solution)/shard_map/reduce_scatter | solution.py:253
  802.3 5.4 convert_reduce_fusion.4
  811.8 18.3 %convolution_bitcast_fusion.1 = f32[128,8,16,128]{3,1,2,0:T(8,128)S(1)} fusion(bf16[2048,2048]{1,0:T(8,128)(2,1)} %all-gather.6.cloned.1.call-done, f32[2048,1024]{1,0:T(8,128)} %fusion.61, f32[1024]{0:T(1024)S(1)} %copy-done.56), kind=kOutput, calls=%fused_computation.98 | convolution fusion | flops 8610906112 | bytes 25169920 | tf_op jit(solution)/shard_map/dot_general | solution.py:25
  832.2 5.8 copy.270
  838.0 50.4 %all-gather.8.cloned.1.call-done = bf16[2048,2048]{1,0:T(8,128)(2,1)} async-done(((bf16[256,2048]{1,0:T(8,128)(2,1)}), bf16[2048,2048]{1,0:T(8,128)(2,1)}) %all-gather.8.cloned.1.call-update) | async-done | bytes 8388624 | tf_op jit(solution)/shard_map/all_gather | solution.py:261
  888.3 6.7 convolution_convert_fusion
  895.0 113.7 %while.29 = (s32[]{:T(128)}, f32[2048,128]{1,0:T(8,128)S(1)}, f32[2048,128]{1,0:T(8,128)}, bf16[4,512,256]{2,1,0:T(8,128)(2,1)}, s32[4]{0:T(128)S(1)}, /*index=5...) while((s32[]{:T(128)}, f32[2048,128]{1,0:T(8,128)S(1)}, ...), condition=%wide.region_16.17_spmd.clone, body=%wide.region_14.16_spmd.clone.sunk | while | flops 2720529920 | bytes 127711568 | solution.py:135
  900.5 4.4 fusion.182
  912.9 7.2 fusion.185
  928.5 4.4 fusion.182
  936.9 4.0 fusion.184
  940.9 7.5 fusion.185
  956.9 4.4 fusion.182
  965.2 4.0 fusion.184
  969.2 7.5 fusion.185
  985.2 4.4 fusion.182
  993.6 4.0 fusion.184
  997.6 7.5 fusion.185
  1008.7 6.7 fusion.79
  1015.6 15.7 convolution_bitcast_fusion.2
  1031.3 5.7 copy.260
  1037.1 4.7 copy.271
  1045.4 12.2 pad_maximum_fusion
  1057.5 14.3 gather_fusion.1
  1071.8 12.2 select_bitcast_fusion
  1084.7 16.6 fusion.90
  1103.6 12.3 copy.226
  1116.0 12.1 copy.229
  1130.3 5.4 convolution_bitcast_fusion.3
  1135.8 5.1 convolution_bitcast_fusion.4
  1143.3 5.2 gather_fusion
  1148.5 5.1 select_bitcast_fusion.1
  1153.8 9.7 fusion.81
  1163.5 8.5 fusion.100
  1172.0 18.6 %add_add_fusion = f32[2048,2048]{1,0:T(8,128)} fusion(f32[2048,2048]{1,0:T(8,128)} %fusion.100, f32[2048,2048]{1,0:T(8,128)} %fusion.81, bf16[2048,128]{1,0:T(8,128)(2,1)S(1)} %copy-done.35, f32[2048,128]{1,0:T(8,128)S(1)} %copy-done.12), kind=kOutput, calls=%fused_computation.73 | convolution fusion | flops 1082392576 | bytes 51904512 | tf_op jit(solution)/shard_map/dot_general | solution.py:31
  1226.8 9.6 reduce-scatter.16.cloned.1.call-done
  1241.0 5.1 fusion.102
  1246.2 6.9 multiply_subtract_fusion
  1253.1 153.9 %reduce-scatter.8.cloned.1.call-done = f32[256,2048]{1,0:T(8,128)} async-done(((f32[2048,2048]{1,0:T(8,128)}), f32[256,2048]{1,0:T(8,128)}) %reduce-scatter.8.cloned.1.call-update) | async-done | bytes 2097168 | tf_op jit(solution)/shard_map/reduce_scatter | solution.py:238
  1407.1 4.1 add_add_fusion.1
  1411.2 12.0 add_multiply_fusion.1
  1423.3 8.3 add_multiply_fusion
  1431.9 10.3 all-reduce.1
  1444.2 7.1 all-reduce.8.cloned.1.call-done
  1460.1 47.1 %reduce-scatter.14.cloned.1.call-done = f32[2,4,2,128,128]{4,3,2,0,1:T(8,128)} async-done(((f32[2,16,2,128,128]{4,3,2,0,1:T(8,128)}), f32[2,4,2,128,128]{4,3,2,0,1:T(8,128)}) %reduce-scatter.14.cloned.1.call-update) | async-done | bytes 1048592 | tf_op jit(solution)/shard_map/reduce_scatter | solution.py:307
  1516.6 4.0 fusion.63
  1520.7 157.1 %reduce-scatter.12.cloned.1.call-done = f32[256,2048]{1,0:T(8,128)} async-done(((f32[2048,2048]{1,0:T(8,128)}), f32[256,2048]{1,0:T(8,128)}) %reduce-scatter.12.cloned.1.call-update) | async-done | bytes 2097168 | tf_op jit(solution)/shard_map/reduce_scatter | solution.py:275
  1680.9 38.5 %all-reduce = (f32[6,2048]{1,0:T(8,128)S(1)}, f32[128]{0:T(128)S(1)}) all-reduce(f32[6,2048]{1,0:T(8,128)S(1)} %stack.73, f32[128]{0:T(128)S(1)} %copy-done.62), channel_id=1, replica_groups=mesh['batch'=4,'head'=8] {'batch','head'}, use_global_device_ids=true, to_apply=%region_26.27 | all-reduce | flops 12416 | bytes 99328 | tf_op jit(solution)/shard_map/psum | solution.py:301
  1721.9 4.7 multiply_add_fusion
  (351 shorter events, 200.7 us)
Async XLA Ops:
  7.2 1501.5 %copy-start = (f32[2,4,2,128,128]{4,3,2,1,0:T(8,128)S(1)}, f32[2,4,2,128,128]{4,3,2,1,0:T(8,128)}, u32[]{:S(2)}) copy-start(f32[2,4,2,128,128]{4,3,2,1,0:T(8,128)} %param.54) | copy-start | bytes 3145732
  7.2 87.2 %all-gather.4.cloned.1.call-start = ((), (), s32[]{:S(2)}) async-start(), calls=%async_computation.7 | async-start | bytes 9437184 | tf_op jit(solution)/shard_map/all_gather | solution.py:219
  8.0 505.2 %all-reduce.6.cloned.1.call-start = ((), (), s32[]{:S(2)}) async-start(), calls=%async_computation.8 | async-start | bytes 33554432 | tf_op jit(solution)/shard_map/psum | solution.py:228
  10.5 92.0 %copy-start.41 = (f32[1,2048]{1,0:T(1,128)}, f32[1,2048]{1,0:T(1,128)S(1)}, u32[]{:S(2)}) copy-start(f32[1,2048]{1,0:T(1,128)S(1)} %get-tuple-element.467) | copy-start | bytes 24580
  102.5 7.2 copy-start.46
  113.0 8.0 copy-start.34
  113.0 8.0 copy-start.67
  124.4 47.9 %copy-start.22 = (bf16[256,2048]{1,0:T(8,128)(2,1)S(1)}, bf16[256,2048]{1,0:T(8,128)(2,1)}, u32[]{:S(2)}) copy-start(bf16[256,2048]{1,0:T(8,128)(2,1)} %param.49) | copy-start | bytes 3145732
  172.3 9.4 copy-start.28
  181.7 415.3 %all-gather.6.cloned.1.call-start = ((), (), s32[]{:S(2)}) async-start(), calls=%async_computation.10 | async-start | bytes 9437184 | tf_op jit(solution)/shard_map/all_gather | solution.py:247
  182.4 616.3 %reduce-scatter.10.cloned.1.call-start = ((), (), s32[]{:S(2)}) async-start(), calls=%async_computation.11 | async-start | bytes 18874368 | tf_op jit(solution)/shard_map/reduce_scatter | solution.py:253
  536.8 13.6 copy-start.24
  536.8 13.6 copy-start.43
  536.8 13.6 copy-start.53
  550.4 46.6 %copy-start.56 = (f32[1024]{0:T(1024)S(1)}, f32[1024]{0:T(1024)}, u32[]{:S(2)}) copy-start(f32[1024]{0:T(1024)} %param.45) | copy-start | bytes 12292
  597.0 23.0 %copy-start.25 = (bf16[2048,1024]{1,0:T(8,128)(2,1)S(1)}, bf16[2048,1024]{1,0:T(8,128)(2,1)}, u32[]{:S(2)}) copy-start(bf16[2048,1024]{1,0:T(8,128)(2,1)} %param.50) | copy-start | bytes 12582916
  631.7 170.6 %copy-start.18 = (bf16[256,2048]{1,0:T(8,128)(2,1)S(1)}, bf16[256,2048]{1,0:T(8,128)(2,1)}, u32[]{:S(2)}) copy-start(bf16[256,2048]{1,0:T(8,128)(2,1)} %param.39) | copy-start | bytes 3145732
  631.8 176.3 %copy-start.71 = (s32[16]{0:T(128)S(1)}, s32[16]{0:T(128)}, u32[]{:S(2)}) copy-start(s32[16]{0:T(128)} %param.41) | copy-start | bytes 196
  631.8 256.5 %all-gather.8.cloned.1.call-start = ((), (), s32[]{:S(2)}) async-start(), calls=%async_computation.12 | async-start | bytes 9437184 | tf_op jit(solution)/shard_map/all_gather | solution.py:261
  807.8 340.7 %reduce-scatter.18.cloned.1.call-start = ((), (), s32[]{:S(2)}) async-start(), calls=%async_computation.16 | async-start | bytes 1179648 | tf_op jit(solution)/shard_map/reduce_scatter | solution.py:285
  832.1 56.2 %copy-start.23 = (bf16[256,2048]{1,0:T(8,128)(2,1)S(1)}, bf16[256,2048]{1,0:T(8,128)(2,1)}, u32[]{:S(2)}) copy-start(bf16[256,2048]{1,0:T(8,128)(2,1)} %param.49) | copy-start | bytes 3145732
  838.0 57.1 %copy-start.29 = (s32[2048]{0:T(1024)S(1)}, s32[2048]{0:T(1024)}, u32[]{:S(2)}) copy-start(s32[2048]{0:T(1024)} %copy-done.28) | copy-start | bytes 24580
  912.9 7.2 copy-start.2
  940.9 7.5 copy-start.2
  969.2 7.5 copy-start.2
  997.6 7.5 copy-start.2
  1015.5 132.9 %reduce-scatter.20.cloned.1.call-start = ((), (), s32[]{:S(2)}) async-start(), calls=%async_computation.17 | async-start | bytes 1179648 | tf_op jit(solution)/shard_map/reduce_scatter | solution.py:286
  1031.3 10.5 slice-start
  1045.3 191.1 %reduce-scatter.16.cloned.1.call-start = ((), (), s32[]{:S(2)}) async-start(), calls=%async_computation.15 | async-start | bytes 20971520 | tf_op jit(solution)/shard_map/reduce_scatter | solution.py:308
  1057.5 14.3 copy-start.61
  1084.0 323.1 %reduce-scatter.8.cloned.1.call-start = ((), (), s32[]{:S(2)}) async-start(), calls=%async_computation.9 | async-start | bytes 18874368 | tf_op jit(solution)/shard_map/reduce_scatter | solution.py:238
  1101.3 350.0 %all-reduce.8.cloned.1.call-start = ((), (), s32[]{:S(2)}) async-start(), calls=%async_computation.18 | async-start | bytes 524288 | tf_op jit(solution)/shard_map/psum | solution.py:288
  1148.5 358.8 %reduce-scatter.14.cloned.1.call-start = ((), (), s32[]{:S(2)}) async-start(), calls=%async_computation.14 | async-start | bytes 5242880 | tf_op jit(solution)/shard_map/reduce_scatter | solution.py:307
  1153.7 524.1 %reduce-scatter.12.cloned.1.call-start = ((), (), s32[]{:S(2)}) async-start(), calls=%async_computation.13 | async-start | bytes 18874368 | tf_op jit(solution)/shard_map/reduce_scatter | solution.py:275
  1153.7 9.7 copy-start.13
  1153.7 9.7 copy-start.20
  1163.5 8.5 copy-start.35
  1210.8 11.7 copy-start.32
  1210.8 11.7 copy-start.55
  1246.2 160.9 %copy-start.49 = (f32[1,2048]{1,0:T(1,128)S(1)}, f32[1,2048]{1,0:T(1,128)}, u32[]{:S(2)}) copy-start(f32[1,2048]{1,0:T(1,128)} %get-tuple-element.462) | copy-start | bytes 24580
  1411.2 12.0 copy-start.26
  1423.2 8.4 copy-start.14
  1423.2 8.6 copy-start.60
  1423.2 19.7 %copy-start.64 = (f32[256]{0:T(256)S(1)}, f32[256]{0:T(256)}, u32[]{:S(2)}) copy-start(f32[256]{0:T(256)} %param.43) | copy-start | bytes 3076
  1423.2 19.7 %copy-start.65 = (f32[256]{0:T(256)S(1)}, f32[256]{0:T(256)}, u32[]{:S(2)}) copy-start(f32[256]{0:T(256)} %param.65) | copy-start | bytes 3076
  1423.3 20.3 %copy-start.58 = (f32[1024]{0:T(1024)S(1)}, f32[1024]{0:T(1024)}, u32[]{:S(2)}) copy-start(f32[1024]{0:T(1024)} %param.67) | copy-start | bytes 12292
  1423.3 29.8 %copy-start.39 = (f32[2,2,1,128,128]{4,3,2,1,0:T(8,128)S(1)}, f32[2,2,1,128,128]{4,3,2,1,0:T(8,128)}, u32[]{:S(2)}) copy-start(f32[2,2,1,128,128]{4,3,2,1,0:T(8,128)} %param.62) | copy-start | bytes 786436
  1431.6 78.3 %copy-start.30 = (bf16[1,4,2,128,128]{4,3,2,1,0:T(8,128)(2,1)S(1)}, bf16[1,4,2,128,128]{4,3,2,1,0:T(8,128)(2,1)}, u32[]{:S(2)}) copy-start(bf16[1,4,2,128,128]{4,3,2,1,0:T(8,128)(2,1)} %get-tuple-element.471) | copy-start | bytes 786436
  1442.1 9.1 copy-start.66
  1442.2 74.5 %copy-start.59 = (f32[1024]{0:T(1024)}, f32[1024]{0:T(1024)S(1)}, u32[]{:S(2)}) copy-start(f32[1024]{0:T(1024)S(1)} %get-tuple-element.435) | copy-start | bytes 12292
  1453.1 67.6 %copy-start.27 = (f32[2,2,1,128,128]{4,3,1,0,2:T(8,128)}, f32[2,2,1,128,128]{4,3,1,0,2:T(8,128)S(1)}, u32[]{:S(2)}) copy-start(f32[2,2,1,128,128]{4,3,1,0,2:T(8,128)S(1)} %constant_dynamic-update-slice_fusion.2) | copy-start | bytes 786436
  1460.1 217.6 %copy-start.42 = (f32[1,2048]{1,0:T(1,128)S(1)}, f32[1,2048]{1,0:T(1,128)}, u32[]{:S(2)}) copy-start(f32[1,2048]{1,0:T(1,128)} %copy-done.41) | copy-start | bytes 24580
  1508.7 172.1 %copy-start.8 = (f32[2,4,2,128,128]{4,3,2,1,0:T(8,128)}, f32[2,4,2,128,128]{4,3,2,1,0:T(8,128)S(1)}, u32[]{:S(2)}) copy-start(f32[2,4,2,128,128]{4,3,2,1,0:T(8,128)S(1)} %copy.206) | copy-start | bytes 3145732
  1509.8 171.0 %copy-start.47 = (f32[2048]{0:T(1024)S(1)}, f32[2048]{0:T(1024)}, u32[]{:S(2)}) copy-start(f32[2048]{0:T(1024)} %get-tuple-element.386) | copy-start | bytes 24580
  1509.8 171.0 %copy-start.48 = (f32[2048]{0:T(1024)S(1)}, f32[2048]{0:T(1024)}, u32[]{:S(2)}) copy-start(f32[2048]{0:T(1024)} %get-tuple-element.392) | copy-start | bytes 24580
  1509.8 171.0 %copy-start.50 = (f32[2048]{0:T(1024)S(1)}, f32[2048]{0:T(1024)}, u32[]{:S(2)}) copy-start(f32[2048]{0:T(1024)} %get-tuple-element.448) | copy-start | bytes 24580
  1509.8 171.0 %copy-start.51 = (f32[2048]{0:T(1024)S(1)}, f32[2048]{0:T(1024)}, u32[]{:S(2)}) copy-start(f32[2048]{0:T(1024)} %get-tuple-element.459) | copy-start | bytes 24580
  1509.8 171.1 %copy-start.62 = (f32[128]{0:T(128)S(1)}, f32[128]{0:T(128)}, u32[]{:S(2)}) copy-start(f32[128]{0:T(128)} %convert_reduce_fusion.5) | copy-start | bytes 1540
  1509.8 209.6 %copy-start.40 = (f32[6,2048]{1,0:T(8,128)S(1)}, f32[6,2048]{1,0:T(8,128)}, u32[]{:S(2)}) copy-start(f32[6,2048]{1,0:T(8,128)} %param.42) | copy-start | bytes 147460
  1509.8 209.6 %copy-start.44 = (f32[6,2048]{1,0:T(8,128)S(1)}, f32[6,2048]{1,0:T(8,128)}, u32[]{:S(2)}) copy-start(f32[6,2048]{1,0:T(8,128)} %param.64) | copy-start | bytes 147460
  1509.9 211.5 %copy-start.68 = (f32[128]{0:T(128)S(1)}, f32[128]{0:T(128)}, u32[]{:S(2)}) copy-start(f32[128]{0:T(128)} %param.44) | copy-start | bytes 1540
  1509.9 211.5 %copy-start.69 = (f32[128]{0:T(128)S(1)}, f32[128]{0:T(128)}, u32[]{:S(2)}) copy-start(f32[128]{0:T(128)} %param.66) | copy-start | bytes 1540
  1719.4 7.2 copy-start.45
  1719.4 7.2 copy-start.70
  (35 other events, 163.8 us)
Sparse Core Ops, SparseCore 0:
  9.7 84.7 all-gather.3
  181.8 331.3 all-reduce.5
  514.8 82.1 all-gather.5
  631.9 166.7 reduce-scatter.9
  807.9 80.3 all-gather.7
  1015.6 30.6 reduce-scatter.17
  1049.2 30.7 reduce-scatter.19
  1084.1 152.2 reduce-scatter.15
  1238.8 168.2 reduce-scatter.7
  1409.8 41.4 all-reduce.7
  1454.5 52.6 reduce-scatter.13
  1509.5 168.2 reduce-scatter.11
where the time goes:
time: 1750 us; the launch traced here: 1730 us
  waiting for transfers between devices  1040 us (59%)
  matrix products  338 us (19%)
  other arithmetic  143 us (8%)
  local copies, waits for them, and re-layouts  138 us (8%)
  blocking collectives  48.8 us (3%)
    psum x1, waiting for transfers between devices, body(): attn_all = lax.psum(matmul(attended, w_out), 'head')  331 us
    reduce_scatter x1, waiting for transfers between devices, body(): lax.psum_scatter(matmul_nt(grad_pre, w_up), 'head', scatter_dimension=0,...  167 us
    reduce_scatter x1, waiting for transfers between devices, body(): lax.psum_scatter(matmul_nt(grad_q, w_query) + matmul_nt(grad_k, w_key) +...  157 us
    reduce_scatter x1, waiting for transfers between devices, body(): lax.psum_scatter(matmul(lax.slice_in_dim(hidden, 0, tok_dev * lax.axis_si...  154 us
    all_gather x1, waiting for transfers between devices, body(): lax.all_gather(tokens, 'head', axis=0, tiled=True).astype(jnp.float32)  83.9 us
    dot_general x6, matrix products, matmul_nt(): lax.dot_general(first_op, second_op, (((1,), (1,)), ((), ())), preferred_...  76.2 us
    dot_general x6, matrix products, matmul_t(): lax.dot_general(first_op, second_op, (((0,), (0,)), ((), ())), preferred_...  54.7 us
    all_gather x1, waiting for transfers between devices, body(): branch_all = lax.all_gather(grad_branch, 'head', axis=0, tiled=True)  50.4 us
  transfers between devices with their start and end apart: 12, of which 10 were waited for; matrix products, arithmetic and copies ran while one was open for 20% of the time, Pallas kernels for 0%

commit v1 on v0

v1 whole, which is shorter than its diff:
```python
from functools import partial
import math

import jax
import jax.numpy as jnp
from jax import lax
from jax.experimental import pallas as pl
from jax.experimental.pallas import tpu as pltpu
from jax.sharding import PartitionSpec as P

EPSILON = 1e-05
DECAY_RATE = 0.5
MATRIX_RATE = 0.01
VECTOR_RATE = 0.1
SAFE_ADD = 1e-08
PRECISE = lax.Precision.HIGHEST
LOG2E = math.log2(math.e)
MASKED = -1e30
TILE = 128
MESH = pl.DeviceIdType.MESH
BF16 = jnp.bfloat16
F32 = jnp.float32
VMEM_LIMIT = 56 * 1024 * 1024
ANY = pl.BlockSpec(memory_space=pl.ANY)
WHOLE = pl.BlockSpec(memory_space=pltpu.VMEM)


def matmul(first_op, second_op):
    return jnp.dot(first_op, second_op, preferred_element_type=F32)


def matmul_t(first_op, second_op):
    return lax.dot_general(
        first_op, second_op, (((0,), (0,)), ((), ())), preferred_element_type=F32
    )


def matmul_nt(first_op, second_op):
    return lax.dot_general(
        first_op, second_op, (((1,), (1,)), ((), ())), preferred_element_type=F32
    )


def norm_stats(rows_in):
    mean_row = jnp.mean(rows_in, axis=-1, keepdims=True)
    centered = rows_in - mean_row
    variance = jnp.mean(centered * centered, axis=-1, keepdims=True)
    inverse = lax.rsqrt(variance + EPSILON)
    return (centered * inverse, inverse)


def norm_back(grad_out, normed, inverse, gain):
    scaled = grad_out * gain
    mean_one = jnp.mean(scaled, axis=-1, keepdims=True)
    mean_two = jnp.mean(scaled * normed, axis=-1, keepdims=True)
    return inverse * (scaled - mean_one - normed * mean_two)


def lanes(start, size, unit):
    return pl.ds(pl.multiple_of(start, unit), size)


def greet(targets):
    barrier = pltpu.get_barrier_semaphore()
    for target in targets:
        pl.semaphore_signal(barrier, inc=1, device_id=target, device_id_type=MESH)
    pl.semaphore_wait(barrier, len(targets))


def gather_weights(w_query, w_out, bias_local, batch_size, head_count):
    rows, cols = w_query.shape
    chips = head_count // 2
    ring = batch_size == 4

    def kernel(
        q_ref, w_ref, bias_ref, q_all, w_all, bias_all, loc, zs, zr, xs, xr, fs, fr, cs, cr, bs, br
    ):
        b = lax.axis_index("batch")
        h = lax.axis_index("head")
        z = h // 2
        c = h % 2
        sibling = {"head": h + 1 - 2 * c}

        def at_chip(r):
            return {"head": lax.rem(z + r, chips) * 2 + c}

        def other(d):
            return {"head": lax.rem(h + d, head_count)}

        def peer(k):
            return {"batch": b ^ k}

        def source(r):
            return lax.rem(z - r + chips, chips) * 2 + c

        def remote(src, dst, send, recv, target):
            copy = pltpu.make_async_remote_copy(
                src_ref=src,
                dst_ref=dst,
                send_sem=send,
                recv_sem=recv,
                device_id=target,
                device_id_type=MESH,
            )
            copy.start()
            return copy

        def place_query(quarter, head, half=None):
            part = rows // batch_size
            if half is not None:
                part = part // 2
                quarter = quarter * 2 + half
            return q_all.at[lanes(quarter * part, part, part), lanes(head * cols, cols, cols)]

        def place_out(quarter, head, half=None):
            part = cols // batch_size
            if half is not None:
                part = part // 2
                quarter = quarter * 2 + half
            return w_all.at[lanes(head * cols + quarter * part, part, part), :]

        greet([other(d) for d in range(1, head_count)] + [peer(k) for k in range(1, batch_size)])
        places = (place_query, place_out)
        own = (q_all.at[:, lanes(h * cols, cols, cols)], w_all.at[lanes(h * cols, cols, cols), :])
        q_part, w_part = rows // batch_size, cols // batch_size
        mine = (
            q_ref.at[lanes(b * q_part, q_part, q_part), :],
            w_ref.at[lanes(b * w_part, w_part, w_part), :],
        )
        sent = []
        received = []

        def z_start(m):
            return [
                remote(mine[m], places[m](b, h), zs.at[m, r], zr.at[m, r], at_chip(r))
                for r in range(1, chips)
            ]

        z_copies = [z_start(0), None]
        locals_ = []
        for m, src in enumerate((q_ref, w_ref)):
            local = pltpu.make_async_copy(src, own[m], loc.at[m])
            local.start()
            locals_.append(local)
            last = remote(src, own[m], cs.at[m, batch_size, 0], cr.at[m, batch_size, 0], sibling)
            sent.append(last)
            received.append(last)
        for d in range(1, head_count):
            copy = remote(bias_ref, bias_all.at[h], bs.at[d], br.at[d], other(d))
            sent.append(copy)
            received.append(copy)
        bias_own = pltpu.make_async_copy(bias_ref, bias_all.at[h], bs.at[0])
        bias_own.start()

        direct = (1, 2) if ring else tuple(range(1, batch_size))
        for m in range(2):
            if m == 1:
                z_copies[1] = z_start(1)
            place = places[m]
            hops = {}
            for r in range(1, chips):
                z_copies[m][r - 1].wait_recv()
                spot = place(b, source(r))
                for k in direct:
                    hops[k, r] = remote(spot, spot, xs.at[m, k, r], xr.at[m, k, r], peer(k))
                    sent.append(hops[k, r])
                copy = remote(spot, spot, cs.at[m, 0, r], cr.at[m, 0, r], sibling)
                sent.append(copy)
                received.append(copy)
            halves = {}
            for r in range(1, chips):
                for k in direct:
                    hops[k, r].wait_recv()
                    if ring:
                        spot = place(b ^ k, source(r), k - 1)
                        halves[k, r] = remote(
                            spot, spot, fs.at[m, k, r], fr.at[m, k, r], peer(3 - k)
                        )
                        sent.append(halves[k, r])
                    spot = place(b ^ k, source(r))
                    copy = remote(spot, spot, cs.at[m, k, r], cr.at[m, k, r], sibling)
                    sent.append(copy)
                    received.append(copy)
            if ring:
                for r in range(1, chips):
                    for k in direct:
                        halves[k, r].wait_recv()
                    spot = place(b ^ 3, source(r))
                    copy = remote(spot, spot, cs.at[m, 3, r], cr.at[m, 3, r], sibling)
                    sent.append(copy)
                    received.append(copy)
            sent.extend(z_copies[m])
        for copy in received:
            copy.wait_recv()
        for copy in sent:
            copy.wait_send()
        for local in locals_:
            local.wait()
        bias_own.wait()

    dma = pltpu.SemaphoreType.DMA
    hop = dma((2, batch_size, chips))
    return pl.pallas_call(
        kernel,
        out_shape=(
            jax.ShapeDtypeStruct((rows, cols * head_count), w_query.dtype),
            jax.ShapeDtypeStruct((cols * head_count, w_out.shape[1]), w_out.dtype),
            jax.ShapeDtypeStruct((head_count, 1, cols), F32),
        ),
        in_specs=[ANY] * 3,
        out_specs=(ANY,) * 3,
        scratch_shapes=[
            dma((2,)),
            dma((2, chips)),
            dma((2, chips)),
            hop,
            hop,
            hop,
            hop,
            dma((2, batch_size + 1, chips)),
            dma((2, batch_size + 1, chips)),
            dma((head_count,)),
            dma((head_count,)),
        ],
        compiler_params=pltpu.CompilerParams(collective_id=0, has_side_effects=True),
        cost_estimate=pl.CostEstimate(
            flops=0, bytes_accessed=200 * 1024 * 1024, transcendentals=0
        ),
        name="gather_weights",
    )(w_query, w_out, bias_local)


def project_out(attended, weight, tokens, vectors):
    tok, width = attended.shape

    def kernel(att_ref, tok_ref, vec_ref, w_ref, resid_ref, mixer_ref, normed_ref, inverse_ref):
        resid = matmul(att_ref[...], w_ref[...]) + vec_ref[4:5, :] + tok_ref[...].astype(F32)
        normed, inverse = norm_stats(resid)
        resid_ref[...] = resid
        normed_ref[...] = normed
        inverse_ref[...] = jnp.broadcast_to(inverse, inverse_ref.shape)
        mixer_ref[...] = (normed * vec_ref[2:3, :] + vec_ref[3:4, :]).astype(BF16)

    return pl.pallas_call(
        kernel,
        out_shape=(
            jax.ShapeDtypeStruct((tok, width), F32),
            jax.ShapeDtypeStruct((tok, width), BF16),
            jax.ShapeDtypeStruct((tok, width), F32),
            jax.ShapeDtypeStruct((tok, TILE), F32),
        ),
        in_specs=[WHOLE] * 4,
        out_specs=(WHOLE,) * 4,
        compiler_params=pltpu.CompilerParams(vmem_limit_bytes=VMEM_LIMIT),
        cost_estimate=pl.CostEstimate(
            flops=2 * tok * width * width, bytes_accessed=14 * width * width, transcendentals=0
        ),
        name="project_out",
    )(attended, tokens, vectors, weight)


def attention_forward(queries, key_rows, value_turned, mask, slabs):
    tok, width = queries.shape
    seq_len, head_size = key_rows.shape
    slab = width // slabs
    heads = slab // head_size
    scale = LOG2E / math.sqrt(head_size)

    def kernel(q_ref, k_ref, v_ref, mask_ref, o_ref, log_ref):
        for j in range(heads):
            spot = slice(j * head_size, (j + 1) * head_size)
            scores = matmul_nt(k_ref[...], q_ref[:, spot]) * scale + mask_ref[...]
            highest = jnp.max(scores, axis=0, keepdims=True)
            raised = jnp.exp2(scores - highest)
            total = jnp.sum(raised, axis=0, keepdims=True)
            out = matmul(v_ref[...], raised.astype(BF16)) / total
            o_ref[:, spot] = out.T.astype(BF16)
            log_ref[0, j : j + 1, :] = highest + jnp.log2(total)

    return pl.pallas_call(
        kernel,
        grid=(slabs,),
        out_shape=(
            jax.ShapeDtypeStruct((tok, width), BF16),
            jax.ShapeDtypeStruct((slabs, heads, tok), F32),
        ),
        in_specs=[
            pl.BlockSpec((tok, slab), lambda i: (0, i)),
            pl.BlockSpec((seq_len, head_size), lambda i: (0, 0)),
            pl.BlockSpec((head_size, seq_len), lambda i: (0, 0)),
            pl.BlockSpec((seq_len, tok), lambda i: (0, 0)),
        ],
        out_specs=(
            pl.BlockSpec((tok, slab), lambda i: (0, i)),
            pl.BlockSpec((1, heads, tok), lambda i: (i, 0, 0)),
        ),
        compiler_params=pltpu.CompilerParams(vmem_limit_bytes=VMEM_LIMIT),
        cost_estimate=pl.CostEstimate(
            flops=8 * tok * seq_len * width,
            bytes_accessed=4 * tok * width,
            transcendentals=tok * seq_len * slabs * heads,
        ),
        name="attention_forward",
    )(queries, key_rows, value_turned, mask)


def attention_backward(
    queries, key_rows, key_turned, value_rows, mask, log_totals, attended, grad_attended, slabs
):
    tok, width = queries.shape
    seq_len, head_size = key_rows.shape
    slab = width // slabs
    heads = slab // head_size
    scale = LOG2E / math.sqrt(head_size)
    plain_scale = 1.0 / math.sqrt(head_size)
    block = 512 if seq_len % 512 == 0 else seq_len

    def kernel(
        q_ref, k_ref, kt_ref, v_ref, mask_ref, log_ref, o_ref, g_ref, dq_ref, dkv_ref, dk, dv
    ):
        step = pl.program_id(0)

        @pl.when(step == 0)
        def _():
            dk[...] = jnp.zeros_like(dk)
            dv[...] = jnp.zeros_like(dv)

        for j in range(heads):
            spot = slice(j * head_size, (j + 1) * head_size)
            query = q_ref[:, spot]
            grad = g_ref[:, spot]
            joint = grad.astype(F32) * o_ref[:, spot].astype(F32)
            delta = jnp.sum(joint.T, axis=0, keepdims=True)
            logs = log_ref[0, j : j + 1, :]
            total = jnp.zeros((head_size, tok), F32)
            for start in range(0, seq_len, block):
                part = slice(start, start + block)
                scores = matmul_nt(k_ref[part, :], query) * scale + mask_ref[part, :]
                probs = jnp.exp2(scores - logs)
                grad_probs = matmul_nt(v_ref[part, :], grad)
                grad_scores = (probs * (grad_probs - delta)).astype(BF16)
                dv[part, :] += matmul(probs.astype(BF16), grad)
                dk[part, :] += matmul(grad_scores, query)
                total += matmul(kt_ref[:, part], grad_scores)
            dq_ref[:, spot] = (total * plain_scale).T.astype(BF16)

        @pl.when(step == slabs - 1)
        def _():
            dkv_ref[:, :head_size] = (dk[...] * plain_scale).astype(BF16)
            dkv_ref[:, head_size:] = dv[...].astype(BF16)

    whole = lambda *shape: pl.BlockSpec(shape, lambda i: (0,) * len(shape))
    part = pl.BlockSpec((tok, slab), lambda i: (0, i))
    return pl.pallas_call(
        kernel,
        grid=(slabs,),
        out_shape=(
            jax.ShapeDtypeStruct((tok, width), BF16),
            jax.ShapeDtypeStruct((seq_len, 2 * head_size), BF16),
        ),
        in_specs=[
            part,
            whole(seq_len, head_size),
            whole(head_size, seq_len),
            whole(seq_len, head_size),
            whole(seq_len, tok),
            pl.BlockSpec((1, heads, tok), lambda i: (i, 0, 0)),
            part,
            part,
        ],
        out_specs=(part, whole(seq_len, 2 * head_size)),
        scratch_shapes=[
            pltpu.VMEM((seq_len, head_size), F32),
            pltpu.VMEM((seq_len, head_size), F32),
        ],
        compiler_params=pltpu.CompilerParams(vmem_limit_bytes=VMEM_LIMIT),
        cost_estimate=pl.CostEstimate(
            flops=20 * tok * seq_len * width,
            bytes_accessed=8 * tok * width,
            transcendentals=tok * seq_len * slabs * heads,
        ),
        name="attention_backward",
    )(queries, key_rows, key_turned, value_rows, mask, log_totals, attended, grad_attended)


def tiled_gradient(wide, narrow, owner, batch_size, pieces):
    tok, width = wide.shape
    columns = narrow.shape[1]
    per_step = width // TILE // batch_size
    piece = columns // pieces

    def kernel(owner_ref, *refs):
        del owner_ref
        wide_refs, n_ref, o_ref = refs[:per_step], refs[per_step], refs[per_step + 1]
        left = jnp.concatenate([ref[...] for ref in wide_refs], axis=1)
        result = matmul_t(left, n_ref[...])
        for i in range(pieces):
            o_ref[0, i] = result[:, i * piece : (i + 1) * piece].astype(BF16)

    def pick(j):
        return pl.BlockSpec((tok, TILE), lambda i, ids: (0, ids[i * per_step + j]))

    return pl.pallas_call(
        kernel,
        grid_spec=pltpu.PrefetchScalarGridSpec(
            num_scalar_prefetch=1,
            grid=(batch_size,),
            in_specs=[pick(j) for j in range(per_step)]
            + [pl.BlockSpec((tok, columns), lambda i, ids: (0, 0))],
            out_specs=pl.BlockSpec(
                (1, pieces, per_step * TILE, piece), lambda i, ids: (i, 0, 0, 0)
            ),
        ),
        out_shape=jax.ShapeDtypeStruct((batch_size, pieces, per_step * TILE, piece), BF16),
        compiler_params=pltpu.CompilerParams(vmem_limit_bytes=VMEM_LIMIT),
        cost_estimate=pl.CostEstimate(
            flops=2 * tok * width * columns,
            bytes_accessed=2 * (tok * width + tok * columns + width * columns),
            transcendentals=0,
        ),
        name="tiled_gradient",
    )(owner, *([wide] * per_step), narrow)


def exchange_batch(chunks, batch_size):
    b = lax.axis_index("batch")
    kept = lax.dynamic_index_in_dim(chunks, b, 0, keepdims=False)
    arrived = [
        lax.ppermute(
            lax.dynamic_index_in_dim(chunks, b ^ k, 0, keepdims=False),
            "batch",
            [(i, i ^ k) for i in range(batch_size)],
        )
        for k in range(1, batch_size)
    ]
    return [kept] + arrived


def flush(chunks, batch_size, head_count):
    chips = head_count // 2
    h = lax.axis_index("head")
    z = h // 2
    c = h % 2
    _, _, rows, cols = chunks.shape
    split = chunks.reshape(batch_size, chips, 2, rows, cols)
    keep = lax.dynamic_index_in_dim(split, c, 2, keepdims=False)
    give = lax.dynamic_index_in_dim(split, 1 - c, 2, keepdims=False)
    got = lax.ppermute(give, "head", [(i, i ^ 1) for i in range(head_count)])
    paired = (keep.astype(F32) + got.astype(F32)).astype(BF16)
    parts = exchange_batch(paired, batch_size)
    summed = sum(part.astype(F32) for part in parts).astype(BF16)
    total = lax.dynamic_index_in_dim(summed, z, 0, keepdims=False).astype(F32)
    for r in range(1, chips):
        there = lax.rem(z + r, chips)
        total += lax.ppermute(
            lax.dynamic_index_in_dim(summed, there, 0, keepdims=False),
            "head",
            [(i, (i + 2 * r) % head_count) for i in range(head_count)],
        ).astype(F32)
    return total


def scatter_rows(partial_rows, head_count):
    rows, cols = partial_rows.shape
    own = rows // head_count
    chips = head_count // 2
    stacked = partial_rows.reshape(chips, 2, own, cols)

    def kernel(x_ref, o_ref, here, pair, land, cs, cr, zs, zr):
        h = lax.axis_index("head")
        z = h // 2
        c = h % 2
        sibling = {"head": h + 1 - 2 * c}

        def at_chip(r):
            return {"head": lax.rem(z + r, chips) * 2 + c}

        greet([sibling] + [at_chip(r) for r in range(1, chips)])
        swaps = []
        for r in range(chips):
            there = lax.rem(z + chips - 1 - r, chips)
            copy = pltpu.make_async_remote_copy(
                src_ref=x_ref.at[there, 1 - c],
                dst_ref=pair.at[r],
                send_sem=cs.at[r],
                recv_sem=cr.at[r],
                device_id=sibling,
                device_id_type=MESH,
            )
            copy.start()
            swaps.append(copy)
        sends = []
        for r in range(chips - 1):
            step = chips - 1 - r
            there = lax.rem(z + step, chips)
            swaps[r].wait_recv()
            here[r] = (x_ref[there, c].astype(F32) + pair[r].astype(F32)).astype(BF16)
            copy = pltpu.make_async_remote_copy(
                src_ref=here.at[r],
                dst_ref=land.at[r],
                send_sem=zs.at[r],
                recv_sem=zr.at[r],
                device_id=at_chip(step),
                device_id_type=MESH,
            )
            copy.start()
            sends.append(copy)
        swaps[chips - 1].wait_recv()
        total = x_ref[z, c].astype(F32) + pair[chips - 1].astype(F32)
        for r in range(chips - 1):
            sends[r].wait_recv()
            total += land[r].astype(F32)
        o_ref[...] = total
        for copy in swaps + sends:
            copy.wait_send()

    dma = pltpu.SemaphoreType.DMA
    return pl.pallas_call(
        kernel,
        out_shape=jax.ShapeDtypeStruct((own, cols), F32),
        in_specs=[WHOLE],
        out_specs=WHOLE,
        scratch_shapes=[
            pltpu.VMEM((chips, own, cols), BF16),
            pltpu.VMEM((chips, own, cols), BF16),
            pltpu.VMEM((chips, own, cols), BF16),
            dma((chips,)),
            dma((chips,)),
            dma((chips,)),
            dma((chips,)),
        ],
        compiler_params=pltpu.CompilerParams(
            collective_id=1, has_side_effects=True, vmem_limit_bytes=VMEM_LIMIT
        ),
        name="scatter_rows",
    )(stacked)


def small_sums(kv_parts, vector_parts, up_parts, batch_size, head_count):
    _, chips, _, rows, cols = kv_parts.shape
    _, vrows, vcols = vector_parts.shape

    def kernel(
        kv_ref, vec_ref, up_ref, kv_out, vec_out, up_out,
        kv_pair, kv_sum, kv_land, kv_half, kv_zland, kv_own, kv_all,
        vec_land, vec_sum, vec_bland, vec_total, up_land,
        s_pair, r_pair, s_kvb, r_kvb, s_kvz, r_kvz, s_kva, r_kva,
        s_vh, r_vh, s_vb, r_vb, s_va, r_va, s_up, r_up,
    ):
        b = lax.axis_index("batch")
        h = lax.axis_index("head")
        z = h // 2
        c = h % 2
        sibling = {"head": h + 1 - 2 * c}

        def at_chip(r):
            return {"head": lax.rem(z + r, chips) * 2 + c}

        def other(d):
            return {"head": lax.rem(h + d, head_count)}

        def peer(k):
            return {"batch": b ^ k}

        def remote(src, dst, send, recv, target):
            copy = pltpu.make_async_remote_copy(
                src_ref=src, dst_ref=dst, send_sem=send, recv_sem=recv,
                device_id=target, device_id_type=MESH,
            )
            copy.start()
            return copy

        greet([other(d) for d in range(1, head_count)] + [peer(k) for k in range(1, batch_size)])
        done = []
        pair_copy = remote(kv_ref.at[1 - c], kv_pair, s_pair, r_pair, sibling)
        up_copies = [
            remote(up_ref, up_land.at[k], s_up.at[k], r_up.at[k], peer(k))
            for k in range(1, batch_size)
        ]
        vec_copies = [
            remote(
                vec_ref.at[lax.rem(h + d, head_count)], vec_land.at[d], s_vh.at[d], r_vh.at[d],
                other(d),
            )
            for d in range(1, head_count)
        ]
        pair_copy.wait_recv()
        kv_sum[...] = (kv_ref[c].astype(F32) + kv_pair[...].astype(F32)).astype(BF16)
        kv_copies = [
            remote(kv_sum.at[b ^ k], kv_land.at[k], s_kvb.at[k], r_kvb.at[k], peer(k))
            for k in range(1, batch_size)
        ]
        total = vec_ref[h]
        for copy in vec_copies:
            copy.wait_recv()
        for d in range(1, head_count):
            total += vec_land[d]
        vec_sum[...] = total
        vec_bcopies = [
            remote(vec_sum, vec_bland.at[k], s_vb.at[k], r_vb.at[k], peer(k))
            for k in range(1, batch_size)
        ]
        for copy in kv_copies:
            copy.wait_recv()
        kv_total = kv_sum[b].astype(F32)
        for k in range(1, batch_size):
            kv_total += kv_land[k].astype(F32)
        kv_half[...] = kv_total.astype(BF16)
        kv_zcopies = [
            remote(
                kv_half.at[lax.rem(z + r, chips)], kv_zland.at[r], s_kvz.at[r], r_kvz.at[r],
                at_chip(r),
            )
            for r in range(1, chips)
        ]
        for copy in vec_bcopies:
            copy.wait_recv()
        total = vec_sum[...]
        for k in range(1, batch_size):
            total += vec_bland[k]
        vec_total[h] = total
        vec_acopies = [
            remote(vec_total.at[h], vec_total.at[h], s_va.at[d], r_va.at[d], other(d))
            for d in range(1, head_count)
        ]
        up_total = up_ref[...]
        for copy in up_copies:
            copy.wait_recv()
        for k in range(1, batch_size):
            up_total += up_land[k]
        up_out[...] = up_total
        for copy in kv_zcopies:
            copy.wait_recv()
        kv_mine = kv_half[z].astype(F32)
        for r in range(1, chips):
            kv_mine += kv_zland[r].astype(F32)
        kv_all[b] = kv_mine
        kv_acopies = [
            remote(kv_all.at[b], kv_all.at[b], s_kva.at[k], r_kva.at[k], peer(k))
            for k in range(1, batch_size)
        ]
        for copy in vec_acopies + kv_acopies:
            copy.wait_recv()
        kv_out[...] = kv_all[...]
        vec_out[...] = vec_total[...]
        del kv_own
        done = [pair_copy] + up_copies + vec_copies + kv_copies + vec_bcopies
        for copy in done + kv_zcopies + vec_acopies + kv_acopies:
            copy.wait_send()

    dma = pltpu.SemaphoreType.DMA
    vm = pltpu.VMEM
    nb, nh = batch_size, head_count
    return pl.pallas_call(
        kernel,
        out_shape=(
            jax.ShapeDtypeStruct((nb, rows, cols), F32),
            jax.ShapeDtypeStruct((nh, vrows, vcols), F32),
            jax.ShapeDtypeStruct(up_parts.shape, F32),
        ),
        in_specs=[WHOLE] * 3,
        out_specs=(WHOLE,) * 3,
        scratch_shapes=[
            vm((nb, chips, rows, cols), BF16),
            vm((nb, chips, rows, cols), BF16),
            vm((nb, chips, rows, cols), BF16),
            vm((chips, rows, cols), BF16),
            vm((chips, rows, cols), BF16),
            vm((8, 128), F32),
            vm((nb, rows, cols), F32),
            vm((nh, vrows, vcols), F32),
            vm((vrows, vcols), F32),
            vm((nb, vrows, vcols), F32),
            vm((nh, vrows, vcols), F32),
            vm((nb,) + up_parts.shape, F32),
            dma, dma, dma((nb,)), dma((nb,)), dma((chips,)), dma((chips,)), dma((nb,)), dma((nb,)),
            dma((nh,)), dma((nh,)), dma((nb,)), dma((nb,)), dma((nh,)), dma((nh,)),
            dma((nb,)), dma((nb,)),
        ],
        compiler_params=pltpu.CompilerParams(
            collective_id=2, has_side_effects=True, vmem_limit_bytes=VMEM_LIMIT
        ),
        name="small_sums",
    )(kv_parts.transpose(2, 0, 1, 3, 4), vector_parts, up_parts)


def split_high(value):
    high = value.astype(BF16)
    return high, (value - high.astype(F32)).astype(BF16)


def matmul_three(first_op, second_op):
    first_high, first_low = split_high(first_op)
    second_high, second_low = split_high(second_op)
    return (
        matmul(first_high, second_high)
        + matmul(first_high, second_low)
        + matmul(first_low, second_high)
    )


def shampoo(first, second, first_weight, second_weight, owned, left, right, root_left, root_right):
    _, owned_count, columns, _, _ = left.shape
    shares = len(first)

    def kernel(ids_ref, *refs):
        del ids_ref
        one, two = refs[:shares], refs[shares : 2 * shares]
        w_one, w_two, l_ref, r_ref, p_ref, q_ref, g_out, l_out, r_out, w_out = refs[2 * shares :]

        def update(turned):
            for t in range(columns):
                spot = slice(t * TILE, (t + 1) * TILE)
                share_refs = two if turned else one
                grad = share_refs[0][:, spot].astype(F32)
                for ref in share_refs[1:]:
                    grad += ref[:, spot].astype(F32)
                if turned:
                    grad = grad.T
                    weight = w_two[spot, :].astype(F32)
                else:
                    weight = w_one[:, spot].astype(F32)
                high = grad.astype(BF16)
                g_out[0, 0, t] = grad
                l_out[0, 0, t] = DECAY_RATE * l_ref[0, 0, t] + (1.0 - DECAY_RATE) * matmul_nt(
                    high, high
                )
                r_out[0, 0, t] = DECAY_RATE * r_ref[0, 0, t] + (1.0 - DECAY_RATE) * matmul_t(
                    high, high
                )
                stepped = matmul_three(p_ref[0, 0, t], grad)
                stepped = matmul_three(stepped, q_ref[0, 0, t])
                w_out[0, 0, t] = weight - MATRIX_RATE * stepped

        @pl.when(pl.program_id(0) == 0)
        def _():
            update(False)

        @pl.when(pl.program_id(0) == 1)
        def _():
            update(True)

    last = owned_count - 1
    share_one = pl.BlockSpec(
        (TILE, columns * TILE), lambda m, p, ids: (jnp.where(m == 0, p, last), 0)
    )
    share_two = pl.BlockSpec((TILE, columns * TILE), lambda m, p, ids: (jnp.where(m == 1, p, 0), 0))
    weight_one = pl.BlockSpec(
        (TILE, columns * TILE), lambda m, p, ids: (ids[jnp.where(m == 0, p, last)], 0)
    )
    weight_two = pl.BlockSpec(
        (columns * TILE, TILE), lambda m, p, ids: (0, ids[jnp.where(m == 1, p, 0)])
    )
    stat = pl.BlockSpec((1, 1, columns, TILE, TILE), lambda m, p, ids: (m, p, 0, 0, 0))
    shape = jax.ShapeDtypeStruct(left.shape, F32)
    return pl.pallas_call(
        kernel,
        grid_spec=pltpu.PrefetchScalarGridSpec(
            num_scalar_prefetch=1,
            grid=(2, owned_count),
            in_specs=[share_one] * shares
            + [share_two] * shares
            + [weight_one, weight_two]
            + [stat] * 4,
            out_specs=[stat] * 4,
        ),
        out_shape=[shape] * 4,
        compiler_params=pltpu.CompilerParams(vmem_limit_bytes=VMEM_LIMIT),
        cost_estimate=pl.CostEstimate(
            flops=left.size * TILE * 16, bytes_accessed=left.size * 40, transcendentals=0
        ),
        name="shampoo",
    )(owned, *first, *second, first_weight, second_weight, left, right, root_left, root_right)


def shampoo_update(grad_tiles, left_old, right_old, root_left, root_right, weight_tiles):
    outer_left = jnp.einsum("...ij,...kj->...ik", grad_tiles, grad_tiles, precision=PRECISE)
    outer_right = jnp.einsum("...ji,...jk->...ik", grad_tiles, grad_tiles, precision=PRECISE)
    left_new = DECAY_RATE * left_old + (1.0 - DECAY_RATE) * outer_left
    right_new = DECAY_RATE * right_old + (1.0 - DECAY_RATE) * outer_right
    stepped = jnp.einsum("...ij,...jk->...ik", root_left, grad_tiles, precision=PRECISE)
    stepped = jnp.einsum("...ij,...jk->...ik", stepped, root_right, precision=PRECISE)
    return (grad_tiles, left_new, right_new, weight_tiles - MATRIX_RATE * stepped)


def diagonal_update(gradient, second, current):
    second_new = DECAY_RATE * second + (1.0 - DECAY_RATE) * gradient * gradient
    return (
        gradient,
        second_new,
        current - VECTOR_RATE * gradient / (jnp.sqrt(second_new) + SAFE_ADD),
    )


def gelu_pair(u):
    root = math.sqrt(2.0 / math.pi)
    square = u * u
    turn = jnp.tanh(root * u * (1.0 + 0.044715 * square))
    half = 0.5 * (1.0 + turn)
    slope = half + 0.5 * u * (1.0 - turn * turn) * root * (1.0 + 3.0 * 0.044715 * square)
    return u * half, slope


def body(
    tokens,
    cotangent,
    doc_starts,
    owner,
    vectors,
    bias_query,
    bias_value,
    bias_up,
    w_query,
    w_key,
    w_value,
    w_out,
    w_up,
    w_down,
    attn_left,
    attn_right,
    attn_root_left,
    attn_root_right,
    mixer_left,
    mixer_right,
    mixer_root_left,
    mixer_root_right,
    kv_left,
    kv_right,
    kv_root_left,
    kv_root_right,
    vector_second,
    query_second,
    value_second,
    up_second,
):
    batch_size = lax.axis_size("batch")
    head_count = lax.axis_size("head")
    batch_index = lax.axis_index("batch")
    head_index = lax.axis_index("head")
    tok_dev, width = tokens.shape
    seq_len = tok_dev * head_count
    row_start = head_index * tok_dev
    head_size = w_key.shape[1]
    slab = w_query.shape[1]
    chips = head_count // 2
    gain_one = vectors[0]
    shift_one = vectors[1]
    gain_two = vectors[2]
    bias_down = vectors[5]

    positions = jnp.arange(seq_len, dtype=jnp.int32)
    documents = jnp.sum((doc_starts[0][None, :] <= positions[:, None]).astype(jnp.int32), axis=1)
    row_ids = row_start + jnp.arange(tok_dev, dtype=jnp.int32)
    row_docs = lax.dynamic_slice_in_dim(documents, row_start, tok_dev, 0)
    allowed = (documents[:, None] == row_docs[None, :]) & (positions[:, None] <= row_ids[None, :])
    mask = jnp.where(allowed, 0.0, MASKED).astype(F32)

    rows_own = tokens.astype(F32)
    normed_one, inverse_one = norm_stats(rows_own)
    normed_in = (normed_one * gain_one + shift_one).astype(BF16)
    w_kv = jnp.concatenate([w_key, w_value], axis=1)
    kv_bias = jnp.concatenate([jnp.zeros_like(bias_value), bias_value])
    kv_own = (matmul(normed_in, w_kv) + kv_bias).astype(BF16)
    kv_all = lax.all_gather(kv_own, "head", axis=0, tiled=True)
    key_rows = kv_all[:, :head_size]
    value_rows = kv_all[:, head_size:]

    w_query_all, w_out_all, bias_all = gather_weights(
        w_query, w_out, bias_query.reshape(1, slab), batch_size, head_count
    )
    cot_all = lax.all_gather(cotangent, "head", axis=0, tiled=True)

    queries = (matmul(normed_in, w_query_all) + bias_all.reshape(1, width)).astype(BF16)
    attended, log_totals = attention_forward(queries, key_rows, value_rows.T, mask, head_count)
    attended, cot_all = lax.optimization_barrier((attended, cot_all))
    resid, mixer_in, normed_two, inverse_wide = project_out(
        attended, w_out_all, tokens, vectors
    )
    inverse_two = inverse_wide[:, :1]

    mixer_all = lax.all_gather(mixer_in, "head", axis=0, tiled=True)
    grad_hidden = matmul_nt(cot_all, w_down).astype(BF16)
    pre_act = matmul(mixer_all, w_up) + bias_up
    hidden_f, slope = gelu_pair(pre_act)
    hidden = hidden_f.astype(BF16)
    grad_pre = (grad_hidden.astype(F32) * slope).astype(BF16)
    grad_mixer_in = lax.psum_scatter(
        matmul_nt(grad_pre, w_up).astype(BF16), "head", scatter_dimension=0, tiled=True
    ).astype(F32)
    grad_down = tiled_gradient(cot_all, hidden, owner, batch_size, 1)[:, 0]
    down_shares = exchange_batch(grad_down, batch_size)
    grad_up = tiled_gradient(mixer_all, grad_pre, owner, batch_size, 1)[:, 0]
    up_shares = exchange_batch(grad_up, batch_size)
    mix_one = lax.psum_scatter(
        matmul(hidden, w_down).astype(BF16), "head", scatter_dimension=0, tiled=True
    )
    grad_up_bias = jnp.sum(grad_pre.astype(F32), axis=0)

    cot_one = cotangent.astype(F32)
    grad_resid = cot_one + norm_back(grad_mixer_in, normed_two, inverse_two, gain_two)
    grad_branch = grad_resid.astype(BF16)
    grad_attended = matmul_nt(grad_branch, w_out_all).astype(BF16)
    grad_out = tiled_gradient(grad_branch, attended, owner, batch_size, head_count)
    out_total = flush(grad_out, batch_size, head_count).astype(BF16)
    grad_q, grad_kv_part = attention_backward(
        queries,
        key_rows,
        key_rows.T,
        value_rows,
        mask,
        log_totals,
        attended,
        grad_attended,
        head_count,
    )
    grad_q, down_shares, up_shares, mix_one = lax.optimization_barrier(
        (grad_q, down_shares, up_shares, mix_one)
    )
    output = resid + mix_one.astype(F32) + bias_down
    grad_query = tiled_gradient(normed_in, grad_q, owner, batch_size, head_count)
    query_total = flush(grad_query, batch_size, head_count).astype(BF16)
    grad_kv = scatter_rows(grad_kv_part, head_count)
    grad_kv_low = grad_kv.astype(BF16)
    grad_normed_in = matmul_nt(grad_q, w_query_all) + matmul_nt(grad_kv_low, w_kv)
    grad_tokens = grad_resid + norm_back(grad_normed_in, normed_one, inverse_one, gain_one)

    kv_part = matmul_t(normed_in, grad_kv_low).astype(BF16)
    kv_rows = width // head_count // batch_size
    kv_parts = kv_part.reshape(chips, 2, batch_size, kv_rows, 2 * head_size).transpose(
        2, 0, 1, 3, 4
    )
    value_bias_row = jnp.concatenate(
        [
            jnp.sum(grad_kv_low[:, head_size:].astype(F32), axis=0),
            jnp.zeros((width - head_size,), F32),
        ]
    )
    vector_part = jnp.stack(
        [
            jnp.sum(grad_normed_in * normed_one, axis=0),
            jnp.sum(grad_normed_in, axis=0),
            jnp.sum(grad_mixer_in * normed_two, axis=0),
            jnp.sum(grad_mixer_in, axis=0),
            jnp.sum(grad_branch.astype(F32), axis=0),
            jnp.sum(cot_one, axis=0),
            jnp.sum(grad_q.astype(F32), axis=0),
            value_bias_row,
        ]
    )
    kv_total, vector_wide, up_bias_total = small_sums(
        kv_parts,
        vector_part.reshape(8, head_count, width // head_count).transpose(1, 0, 2),
        grad_up_bias.reshape(8, -1),
        batch_size,
        head_count,
    )
    kv_total = kv_total.reshape(batch_size * kv_rows, 2 * head_size)
    up_bias_total = up_bias_total.reshape(-1)
    vector_all = vector_wide.transpose(1, 0, 2).reshape(8, width)
    vector_total = vector_all[:6]
    query_bias_total = lax.dynamic_slice_in_dim(vector_all[6], head_index * slab, slab, 0)
    value_bias_total = vector_all[7, :head_size]

    owned_count = attn_left.shape[1]
    owned = lax.dynamic_slice_in_dim(owner, batch_index * owned_count, owned_count, 0)
    mixer_out = shampoo(
        up_shares,
        down_shares,
        w_up,
        w_down,
        owned,
        mixer_left,
        mixer_right,
        mixer_root_left,
        mixer_root_right,
    )
    attn_out = shampoo(
        [query_total],
        [out_total],
        w_query,
        w_out,
        owned,
        attn_left,
        attn_right,
        attn_root_left,
        attn_root_right,
    )
    kv_count = width // head_count

    def kv_tiles(matrix):
        return matrix.reshape(kv_count // TILE, TILE, head_size // TILE, TILE).transpose(0, 2, 1, 3)

    kv_slab = lax.dynamic_slice_in_dim(w_kv, head_index * kv_count, kv_count, 0).astype(F32)
    kv_out = shampoo_update(
        jnp.stack([kv_tiles(kv_total[:, :head_size]), kv_tiles(kv_total[:, head_size:])]),
        kv_left,
        kv_right,
        kv_root_left,
        kv_root_right,
        jnp.stack([kv_tiles(kv_slab[:, :head_size]), kv_tiles(kv_slab[:, head_size:])]),
    )
    vec_out = diagonal_update(vector_total, vector_second, vectors)
    query_out = diagonal_update(query_bias_total, query_second, bias_query)
    value_out = diagonal_update(value_bias_total, value_second, bias_value)
    up_out = diagonal_update(up_bias_total, up_second, bias_up)
    return (
        output,
        grad_tokens,
        vec_out[0],
        vec_out[1][2:],
        vec_out[1][:2],
        vec_out[2],
        query_out[0],
        query_out[1],
        query_out[2],
        value_out[0],
        value_out[1],
        value_out[2],
        up_out[0],
        up_out[1],
        up_out[2],
        attn_out[0],
        attn_out[1],
        attn_out[2],
        attn_out[3],
        mixer_out[0],
        mixer_out[1],
        mixer_out[2],
        mixer_out[3],
        kv_out[0],
        kv_out[1],
        kv_out[2],
        kv_out[3],
    )


def solution(mesh):
    rows = P(("batch", "head"), None)
    whole = P()
    head = P("head")
    tiles = P(None, "batch", "head", None, None)
    kv_tiles = P(None, "head", None, None, None)
    in_specs = (
        rows,
        rows,
        P("batch", None),
        whole,
        whole,
        head,
        whole,
        head,
        P(None, "head"),
        whole,
        whole,
        P("head", None),
        P(None, "head"),
        P("head", None),
        *([tiles] * 8),
        *([kv_tiles] * 4),
        whole,
        head,
        whole,
        head,
    )
    out_specs = (
        rows,
        rows,
        *([whole] * 4),
        *([head] * 3),
        *([whole] * 3),
        *([head] * 3),
        *([tiles] * 8),
        *([kv_tiles] * 4),
    )
    return jax.shard_map(body, mesh=mesh, in_specs=in_specs, out_specs=out_specs, check_vma=False)
```

time: 1750 us -> 754 us (0.43)
  waiting for transfers between devices: 1040 us -> 255 us
  Pallas kernels: 0 us -> 282 us
  matrix products: 338 us -> 88.9 us
  other arithmetic: 143 us -> 33 us
  local copies, waits for them, and re-layouts: 138 us -> 39.4 us
  blocking collectives: 48.8 us -> 0 us
  starting transfers between devices: 0.71 us -> 28.8 us
    reduce_scatter x7 -> x2, waiting for transfers between devices: 535 us -> 67.5 us  [the longest x1 41.2 us: body(): lax.psum_scatter(matmul(hidden, w_down).astype(BF16), 'head', scatter_dim...]
    psum x2 -> x0, waiting for transfers between devices: 338 us -> none  [the longest x1 331 us: body(): attn_all = lax.psum(matmul(attended, w_out), 'head')]
    pallas_call x0 -> x12, Pallas kernels: none -> 282 us  [the longest x1 105 us: gather_weights(): pl.pallas_call(kernel, out_shape=(jax.ShapeDtypeStruct((rows, cols * head...]
    dot_general x34 -> x4, matrix products: 155 us -> 38.9 us  [matmul(): return jnp.dot(first_op, second_op, preferred_element_type=F32)]
    ppermute x0 -> x20, waiting for transfers between devices: none -> 78.4 us  [the longest x12 67.9 us: exchange_batch(): lax.ppermute(lax.dynamic_index_in_dim(chunks, b ^ k, 0, keepdims=False),...]
    dot_general x6 -> x1, matrix products: 54.7 us -> 0.49 us  [matmul_t(): lax.dot_general(first_op, second_op, (((0,), (0,)), ((), ())), preferred_...]
    psum x2 -> x0, blocking collectives: 48.8 us -> none  [the longest x1 38.5 us: body(): lax.psum((vector_part, grad_value_bias), ('batch', 'head'))]
    all_gather x1, waiting for transfers between devices: 35.6 us -> 0.01 us  [body(): cot_all = lax.all_gather(cotangent, 'head', axis=0, tiled=True)]
  transfers between devices with their start and end apart: 12 -> 25, of which waited for: 10 -> 9; matrix products, arithmetic and copies ran while one was open for 20% -> 13% of each run, Pallas kernels for 0% -> 33%
where the time goes in v1:
time: 754 us; the launch traced here: 742 us
  Pallas kernels  282 us (37%)
  waiting for transfers between devices  255 us (34%)
  matrix products  88.9 us (12%)
  local copies, waits for them, and re-layouts  39.4 us (5%)
  other arithmetic  33 us (4%)
  starting transfers between devices  28.8 us (4%)
  between operations  15 us (2%)
    all_gather x1, waiting for transfers between devices, body(): mixer_all = lax.all_gather(mixer_in, 'head', axis=0, tiled=True)  108 us
    pallas_call x1, Pallas kernels, gather_weights(): pl.pallas_call(kernel, out_shape=(jax.ShapeDtypeStruct((rows, cols * head...  105 us
    ppermute x12, waiting for transfers between devices, exchange_batch(): lax.ppermute(lax.dynamic_index_in_dim(chunks, b ^ k, 0, keepdims=False),...  67.9 us
    dot_general x5, matrix products, matmul_nt(): lax.dot_general(first_op, second_op, (((1,), (1,)), ((), ())), preferred_...  45.4 us
    pallas_call x4, Pallas kernels, tiled_gradient(): pl.pallas_call(kernel, grid_spec=pltpu.PrefetchScalarGridSpec(num_scalar_...  44.2 us
    reduce_scatter x1, waiting for transfers between devices, body(): lax.psum_scatter(matmul(hidden, w_down).astype(BF16), 'head', scatter_dim...  41.2 us
    dot_general x4, matrix products, matmul(): return jnp.dot(first_op, second_op, preferred_element_type=F32)  38.9 us
    pallas_call x2, Pallas kernels, shampoo(): pl.pallas_call(kernel, grid_spec=pltpu.PrefetchScalarGridSpec(num_scalar_...  33.3 us
  transfers between devices with their start and end apart: 25, of which 9 were waited for; matrix products, arithmetic and copies ran while one was open for 13% of the time, Pallas kernels for 33%

profile of v1, /device:TPU:0, one launch (start us, length us, event | category | flops | bytes accessed | tf_op | source)
XLA Modules:
  0.0 742.0 jit_solution(8863037499059610091)
XLA Ops:
  7.3 1.7 fusion.69
  8.9 1.4 convert_reduce_fusion.3
  10.4 1.6 fusion.19
  17.1 104.9 %gather_weights.1 = (bf16[2048,2048]{1,0:T(8,128)(2,1)}, bf16[2048,2048]{1,0:T(8,128)(2,1)}, f32[8,1,256]{2,1,0:T(1,128)}) custom-call(bf16[2048,256]{1,0:T(8,128)(2,1)} %refs_2_.1, bf16[256,2048]{1,0:T(8,128)(2,1)} %refs_3_.1, f32[1,256]{1,0:T(1,128)} %bitcast.218), custom_call_target="tpu_custom_call" | custom-call | bytes 209715200 | tf_op jit(solution)/shard_map/gather_weights/pallas_call | solution.py:203
  121.9 1.5 fusion.31.mask_ref
  123.5 6.9 fusion.5.q_ref
  130.3 2.5 fusion.66
  133.9 24.0 %attention_forward.1 = (bf16[256,2048]{1,0:T(8,128)(2,1)}, f32[8,2,256]{2,1,0:T(2,128)}) custom-call(bf16[256,2048]{1,0:T(8,128)(2,1)} %fusion.5.q_ref, bf16[2048,128]{1,0:T(8,128)(2,1)} %get-tuple-element.219.k_ref, bf16[128,2048]{1,0:T(8,128)(2,1)} %copy.78.v_ref, f32[2048,256]{1,0:T(8,128)} %fusion.31.mask_ref), custom_call_target="tpu_custom_call" | custom-call | flops 8589934592 | bytes 2097152 | tf_op jit(solution)/shard_map/attention_forward/pallas_call | solution.py:280
  157.9 8.8 %project_out.1 = (f32[256,2048]{1,0:T(8,128)}, bf16[256,2048]{1,0:T(8,128)(2,1)}, f32[256,2048]{1,0:T(8,128)}, f32[256,128]{1,0:T(8,128)}) custom-call(bf16[256,2048]{1,0:T(8,128)(2,1)} %get-tuple-element.64.att_ref.o_ref.refs_4_, bf16[256,2048]{1,0:T(8,128)(2,1)} %tok_ref.1, f32[6,2048]{1,0:T(8,128)} %vec_ref.1, bf16[2048,2048]{1,0:T(8,128)(2,1)} %get-tuple-element.65.w_ref), custom_call_target="tpu_custom_call" | custom-call | flops 2147483648 | bytes 58720256 | tf_op jit(solution)/shard_map/project_out/pallas_call | solution.py:244
  167.0 108.4 %all-gather.8.cloned.1.call-done.refs_0_.refs_1_.refs_2_.refs_3_ = bf16[2048,2048]{1,0:T(8,128)(2,1)} async-done(((bf16[256,2048]{1,0:T(8,128)(2,1)}), bf16[2048,2048]{1,0:T(8,128)(2,1)}) %all-gather.8.cloned.1.call-update) | async-done | bytes 8388624 | tf_op jit(solution)/shard_map/all_gather | solution.py:881
  275.3 16.9 %multiply_convert_fusion = (bf16[2048,1024]{1,0:T(8,128)(2,1)}, f32[2048,1024]{1,0:T(8,128)}) fusion(f32[1024]{0:T(1024)S(1)} %copy-done.41, bf16[2048,2048]{1,0:T(8,128)(2,1)} %all-gather.8.cloned.1.call-done.refs_0_.refs_1_.refs_2_.refs_3_, bf16[2048,1024]{1,0:T(8,128)(2,1)} %refs_8_.1), kind=kOutput, calls=%fused_computation.5 | convolution fusion | flops 8610906112 | bytes 25169920 | tf_op jit(solution)/shard_map/dot_general | solution.py:29
  292.2 17.4 %convert_reduce_fusion = (f32[1024]{0:T(1024)}, bf16[2048,1024]{1,0:T(8,128)(2,1)S(1)}) fusion(f32[2048,1024]{1,0:T(8,128)} %get-tuple-element.231, f32[1024]{0:T(1024)S(1)} %copy-done.41, bf16[2048,2048]{1,0:T(8,128)(2,1)} %all-gather.6.cloned.1.call-done.refs_0_.refs_1_.refs_2_.refs_3_, bf16[1024,2048]{1,0:T(8,128)(2,1)S(1)} %copy-done.10), kind=kOutput, calls=%fused_computation.4 | convolution fusion | flops 8638168064 | bytes 25174016 | tf_op jit(solution)/shard_map/dot_general | solution.py:39
  309.6 2.0 copy-done.12
  311.6 11.3 %convolution_convert_fusion.1 = bf16[2048,2048]{1,0:T(8,128)(2,1)} fusion(bf16[2048,1024]{1,0:T(8,128)(2,1)S(1)} %get-tuple-element.234.refs_4_, bf16[2048,1024]{1,0:T(8,128)(2,1)S(1)} %copy-done.9), kind=kOutput, calls=%fused_computation.10 | convolution fusion | flops 8594128896 | bytes 16777216 | tf_op jit(solution)/shard_map/dot_general | solution.py:39
  323.0 14.0 %convolution_convert_fusion = bf16[2048,2048]{1,0:T(8,128)(2,1)} fusion(bf16[2048,1024]{1,0:T(8,128)(2,1)} %get-tuple-element.230.refs_4_, bf16[1024,2048]{1,0:T(8,128)(2,1)} %refs_9_.1), kind=kOutput, calls=%fused_computation.9 | convolution fusion | flops 8594128896 | bytes 16777216 | tf_op jit(solution)/shard_map/dot_general | solution.py:29
  340.7 14.4 %tiled_gradient.5 = bf16[4,1,512,1024]{3,2,1,0:T(8,128)(2,1)} custom-call(s32[16]{0:T(128)} %owner_ref.7, bf16[2048,2048]{1,0:T(8,128)(2,1)} %all-gather.8.cloned.1.call-done.refs_0_.refs_1_.refs_2_.refs_3_, bf16[2048,2048]{1,0:T(8,128)(2,1)} %all-gather.8.cloned.1.call-done.refs_0_.refs_1_.refs_2_.refs_3_, ...), custom_call_target="tpu_custom_call" | custom-call | flops 8589934592 | bytes 16777216 | tf_op jit(solution)/shard_map/tiled_gradient/pallas_call | solution.py:403
  355.2 4.3 dynamic-slice_bitcast_fusion.8
  359.5 1.5 collective-permute-start.3
  361.0 1.5 collective-permute-start.4
  363.0 14.6 %tiled_gradient.4 = bf16[4,1,512,1024]{3,2,1,0:T(8,128)(2,1)} custom-call(s32[16]{0:T(128)} %owner_ref.7, bf16[2048,2048]{1,0:T(8,128)(2,1)} %all-gather.6.cloned.1.call-done.refs_0_.refs_1_.refs_2_.refs_3_, bf16[2048,2048]{1,0:T(8,128)(2,1)} %all-gather.6.cloned.1.call-done.refs_0_.refs_1_.refs_2_.refs_3_, ...), custom_call_target="tpu_custom_call" | custom-call | flops 8589934592 | bytes 16777216 | tf_op jit(solution)/shard_map/tiled_gradient/pallas_call | solution.py:403
  377.6 4.4 dynamic-slice_bitcast_fusion.12
  382.0 1.5 collective-permute-start
  383.6 1.5 collective-permute-start.1
  385.0 26.2 %reduce-scatter.3.cloned.1.call-done = bf16[256,2048]{1,0:T(8,128)(2,1)} async-done(((bf16[2048,2048]{1,0:T(8,128)(2,1)}), bf16[256,2048]{1,0:T(8,128)(2,1)}) %reduce-scatter.3.cloned.1.call-update) | async-done | bytes 1048592 | tf_op jit(solution)/shard_map/reduce_scatter | solution.py:887
  411.3 2.6 fusion.23
  413.9 2.6 convert_reduce_fusion.5
  416.5 7.8 %convolution_convert_fusion.3.g_ref = bf16[256,2048]{1,0:T(8,128)(2,1)} fusion(bf16[256,2048]{1,0:T(8,128)(2,1)S(1)} %get-tuple-element.193.refs_0_.refs_1_.refs_2_.refs_3_, bf16[2048,2048]{1,0:T(8,128)(2,1)} %get-tuple-element.65.w_ref), kind=kOutput, calls=%fused_computation.27 | convolution fusion | flops 2148007936 | bytes 10485760 | tf_op jit(solution)/shard_map/dot_general | solution.py:39
  424.3 2.6 collective-permute-start.2
  426.8 25.8 %attention_backward.1 = (bf16[256,2048]{1,0:T(8,128)(2,1)}, bf16[2048,256]{1,0:T(8,128)(2,1)}) custom-call(bf16[256,2048]{1,0:T(8,128)(2,1)} %fusion.5.q_ref, bf16[2048,128]{1,0:T(8,128)(2,1)} %get-tuple-element.219.k_ref, bf16[128,2048]{1,0:T(8,128)(2,1)} %copy.79.kt_ref, bf16[2048,128]{1,0:T(8,128)(2,1)} %get-tuple-element.216.v_ref, ...), custom_call_target="tpu_custom_call" | custom-call | flops 21474836480 | bytes 4194304 | tf_op jit(solution)/shard_map/attention_backward/pallas_call | solution.py:354
  452.6 7.5 %tiled_gradient.7 = bf16[4,8,512,256]{3,2,1,0:T(8,128)(2,1)} custom-call(s32[16]{0:T(128)} %owner_ref.7, bf16[256,2048]{1,0:T(8,128)(2,1)} %copy-done.5, bf16[256,2048]{1,0:T(8,128)(2,1)} %copy-done.5, bf16[256,2048]{1,0:T(8,128)(2,1)} %copy-done.5, bf16[256,2048]{1,0:T(8,128)(2,1)} %copy-done.5, bf16[256,2048]{1,0:T(8,128)(2,1)} %get-tuple-element.64.att_ref.o_ref.refs_4_), custom_call_target="tpu_custom_call" | custom-call | flops 2147483648 | bytes 10485760 | tf_op jit(solution)/shard_map/tiled_gradient/pallas_call | solution.py:403
  460.1 41.2 %reduce-scatter.5.cloned.1.call-done = bf16[256,2048]{1,0:T(8,128)(2,1)} async-done(((bf16[2048,2048]{1,0:T(8,128)(2,1)}), bf16[256,2048]{1,0:T(8,128)(2,1)}) %reduce-scatter.5.cloned.1.call-update) | async-done | bytes 1048592 | tf_op jit(solution)/shard_map/reduce_scatter | solution.py:894
  501.4 17.3 %scatter_rows.1 = f32[256,256]{1,0:T(8,128)} custom-call(bf16[4,2,256,256]{3,2,1,0:T(8,128)(2,1)} %bitcast.190), custom_call_target="tpu_custom_call" | custom-call | tf_op jit(solution)/shard_map/scatter_rows/pallas_call | solution.py:518
  519.6 1.7 fusion.70
  521.3 4.6 dynamic-slice_bitcast_fusion
  526.3 7.7 %tiled_gradient.6 = bf16[4,8,512,256]{3,2,1,0:T(8,128)(2,1)} custom-call(s32[16]{0:T(128)} %owner_ref.7, bf16[256,2048]{1,0:T(8,128)(2,1)} %copy-done.1, bf16[256,2048]{1,0:T(8,128)(2,1)} %copy-done.1, bf16[256,2048]{1,0:T(8,128)(2,1)} %copy-done.1, bf16[256,2048]{1,0:T(8,128)(2,1)} %copy-done.1, bf16[256,2048]{1,0:T(8,128)(2,1)} %get-tuple-element.74.refs_4_), custom_call_target="tpu_custom_call" | custom-call | flops 2147483648 | bytes 10485760 | tf_op jit(solution)/shard_map/tiled_gradient/pallas_call | solution.py:403
  534.0 4.6 dynamic-slice_bitcast_fusion.1
  539.4 7.2 fusion.18
  549.0 3.5 convert_reduce_fusion.2
  552.5 1.5 stack.45
  554.1 23.7 %small_sums.1 = (f32[4,64,256]{2,1,0:T(8,128)}, f32[8,8,256]{2,1,0:T(8,128)}, f32[8,128]{1,0:T(8,128)}) custom-call(bf16[2,4,4,64,256]{4,3,2,1,0:T(8,128)(2,1)} %bitcast.180, f32[8,8,256]{2,1,0:T(8,128)} %bitcast.197, f32[8,128]{1,0:T(8,128)} %bitcast.217), custom_call_target="tpu_custom_call" | custom-call | tf_op jit(solution)/shard_map/small_sums/pallas_call | solution.py:654
  578.8 23.1 %shampoo.3 = (f32[2,4,8,128,128]{4,3,2,1,0:T(8,128)}, f32[2,4,8,128,128]{4,3,2,1,0:T(8,128)}, f32[2,4,8,128,128]{4,3,2,1,0:T(8,128)}, f32[2,4,8,128,128]{4,3,2,1,0:T(8,128)}) custom-call(s32[4]{0:T(128)} %dynamic_slice.110.ids_ref, bf16[512,1024]{1,0:T(8,128)(2,1)} %get-tuple-element.82.refs_0_, bf16[512,1024]{1,0:T(8,128)(2,1)} %collective-permute-done.3.refs_1_, ...), custom_call_target="tpu_custom_call" | custom-call | flops 2147483648 | bytes 41943040 | tf_op jit(solution)/shard_map/shampoo/pallas_call | solution.py:756
  604.1 1.3 fusion.39
  605.5 1.4 fusion.36
  606.8 4.9 fusion
  611.8 1.2 dynamic-slice_bitcast_fusion.4
  613.0 1.4 collective-permute-start.14
  615.1 1.5 collective-permute-start.15
  617.2 3.5 fusion.1
  621.0 1.5 collective-permute-start.7
  622.5 1.5 collective-permute-start.8
  624.0 15.3 %collective-permute-done.14 = bf16[4,512,256]{2,1,0:T(8,128)(2,1)S(1)} collective-permute-done((bf16[4,512,256]{2,1,0:T(8,128)(2,1)}, bf16[4,512,256]{2,1,0:T(8,128)(2,1)S(1)}, u32[]{:S(2)}, u32[]{:S(2)}) %collective-permute-start.14) | collective-permute-done | bytes 1048608 | tf_op jit(solution)/shard_map/ppermute | solution.py:429
  639.3 2.4 collective-permute-start.9
  642.7 1.6 add_add_fusion
  644.4 19.3 %collective-permute-done.15 = bf16[4,512,256]{2,1,0:T(8,128)(2,1)S(1)} collective-permute-done((bf16[4,512,256]{2,1,0:T(8,128)(2,1)S(1)}, bf16[4,512,256]{2,1,0:T(8,128)(2,1)S(1)}, u32[]{:S(2)}, u32[]{:S(2)}) %collective-permute-start.15) | collective-permute-done | bytes 1048608 | tf_op jit(solution)/shard_map/ppermute | solution.py:429
  663.7 1.8 fusion.26
  666.7 1.6 collective-permute-start.18
  668.4 15.9 %collective-permute-done.7 = bf16[4,512,256]{2,1,0:T(8,128)(2,1)S(1)} collective-permute-done((bf16[4,512,256]{2,1,0:T(8,128)(2,1)S(1)}, bf16[4,512,256]{2,1,0:T(8,128)(2,1)S(1)}, u32[]{:S(2)}, u32[]{:S(2)}) %collective-permute-start.7) | collective-permute-done | bytes 1048608 | tf_op jit(solution)/shard_map/ppermute | solution.py:429
  684.3 3.0 collective-permute-start.19
  687.2 17.4 %collective-permute-done.8 = bf16[4,512,256]{2,1,0:T(8,128)(2,1)S(1)} collective-permute-done((bf16[4,512,256]{2,1,0:T(8,128)(2,1)S(1)}, bf16[4,512,256]{2,1,0:T(8,128)(2,1)S(1)}, u32[]{:S(2)}, u32[]{:S(2)}) %collective-permute-start.8) | collective-permute-done | bytes 1048608 | tf_op jit(solution)/shard_map/ppermute | solution.py:429
  706.3 2.0 collective-permute-start.11
  708.2 1.3 collective-permute-start.12
  712.3 4.2 collective-permute-done.10
  716.5 6.3 collective-permute-done.11
  723.7 10.2 %shampoo.2 = (f32[2,4,2,128,128]{4,3,2,1,0:T(8,128)}, f32[2,4,2,128,128]{4,3,2,1,0:T(8,128)}, f32[2,4,2,128,128]{4,3,2,1,0:T(8,128)}, f32[2,4,2,128,128]{4,3,2,1,0:T(8,128)}) custom-call(s32[4]{0:T(128)} %dynamic_slice.110.ids_ref, bf16[512,256]{1,0:T(8,128)(2,1)} %fusion.46.refs_0_, bf16[512,256]{1,0:T(8,128)(2,1)} %fusion.43.refs_1_, ...), custom_call_target="tpu_custom_call" | custom-call | flops 536870912 | bytes 10485760 | tf_op jit(solution)/shard_map/shampoo/pallas_call | solution.py:756
  (178 shorter events, 28.4 us)
Async XLA Ops:
  7.2 596.5 %copy-start = (f32[2,2,1,128,128]{4,3,2,1,0:T(8,128)S(1)}, f32[2,2,1,128,128]{4,3,2,1,0:T(8,128)}, u32[]{:S(2)}) copy-start(f32[2,2,1,128,128]{4,3,2,1,0:T(8,128)} %param.54) | copy-start | bytes 786436
  7.2 7.2 copy-start.3
  7.2 7.2 copy-start.44
  7.2 123.1 %all-gather.4.cloned.1.call-start = ((), (), s32[]{:S(2)}) async-start(), calls=%async_computation.2 | async-start | bytes 1179648 | tf_op jit(solution)/shard_map/all_gather | solution.py:864
  8.9 7.1 copy-start.25
  10.4 6.4 copy-start.29
  10.4 6.5 copy-start.47
  12.1 109.8 %copy-start.32 = (f32[256]{0:T(256)}, f32[256]{0:T(256)S(1)}, u32[]{:S(2)}) copy-start(f32[256]{0:T(256)S(1)} %add_rsqrt_fusion) | copy-start | bytes 3076
  14.4 323.9 %copy-start.13 = (bf16[2048,256]{1,0:T(8,128)(2,1)}, bf16[2048,256]{1,0:T(8,128)(2,1)S(1)}, u32[]{:S(2)}) copy-start(bf16[2048,256]{1,0:T(8,128)(2,1)S(1)} %constant_dynamic-update-slice_fusion) | copy-start | bytes 3145732
  14.9 115.4 %copy-start.1 = (bf16[256,2048]{1,0:T(8,128)(2,1)}, bf16[256,2048]{1,0:T(8,128)(2,1)S(1)}, u32[]{:S(2)}) copy-start(bf16[256,2048]{1,0:T(8,128)(2,1)S(1)} %fusion.13.refs_0_.refs_1_.refs_2_.refs_3_) | copy-start | bytes 3145732
  16.1 141.8 %all-gather.6.cloned.1.call-start = ((), (), s32[]{:S(2)}) async-start(), calls=%async_computation.3 | async-start | bytes 9437184 | tf_op jit(solution)/shard_map/all_gather | solution.py:871
  16.8 258.5 %all-gather.8.cloned.1.call-start = ((), (), s32[]{:S(2)}) async-start(), calls=%async_computation.4 | async-start | bytes 9437184 | tf_op jit(solution)/shard_map/all_gather | solution.py:881
  157.9 117.5 %copy-start.41 = (f32[1024]{0:T(1024)S(1)}, f32[1024]{0:T(1024)}, u32[]{:S(2)}) copy-start(f32[1024]{0:T(1024)} %param.37) | copy-start | bytes 12292
  166.7 244.6 %reduce-scatter.3.cloned.1.call-start = ((), (), s32[]{:S(2)}) async-start(), calls=%async_computation.5 | async-start | bytes 9437184 | tf_op jit(solution)/shard_map/reduce_scatter | solution.py:887
  275.3 16.9 %copy-start.10 = (bf16[1024,2048]{1,0:T(8,128)(2,1)S(1)}, bf16[1024,2048]{1,0:T(8,128)(2,1)}, u32[]{:S(2)}) copy-start(bf16[1024,2048]{1,0:T(8,128)(2,1)} %refs_9_.1) | copy-start | bytes 12582916
  292.2 19.4 %copy-start.9 = (bf16[2048,1024]{1,0:T(8,128)(2,1)S(1)}, bf16[2048,1024]{1,0:T(8,128)(2,1)}, u32[]{:S(2)}) copy-start(bf16[2048,1024]{1,0:T(8,128)(2,1)} %refs_8_.1) | copy-start | bytes 12582916
  323.0 178.4 %reduce-scatter.5.cloned.1.call-start = ((), (), s32[]{:S(2)}) async-start(), calls=%async_computation.6 | async-start | bytes 9437184 | tf_op jit(solution)/shard_map/reduce_scatter | solution.py:894
  359.5 64.8 %collective-permute-start.3 = (bf16[512,1024]{1,0:T(8,128)(2,1)}, bf16[512,1024]{1,0:T(8,128)(2,1)}, u32[]{:S(2)}, u32[]{:S(2)}) collective-permute-start(bf16[512,1024]{1,0:T(8,128)(2,1)} %get-tuple-element.202), channel_id=1, source_target_pairs={{0,8},{8,0},{16,24},{24,16},{1,9},{9,1},{17,25},{25,17},{2,10},{10... | collective-permute-start | bytes 3145736 | tf_op jit(solution)/shard_map/ppermute | solution.py:429
  361.0 99.1 %collective-permute-start.4 = (bf16[512,1024]{1,0:T(8,128)(2,1)}, bf16[512,1024]{1,0:T(8,128)(2,1)}, u32[]{:S(2)}, u32[]{:S(2)}) collective-permute-start(bf16[512,1024]{1,0:T(8,128)(2,1)} %get-tuple-element.201), channel_id=1, source_target_pairs={{0,16},{8,24},{16,0},{24,8},{1,17},{9,25},{17,1},{25,9},{2,18},{10... | collective-permute-start | bytes 3145736 | tf_op jit(solution)/shard_map/ppermute | solution.py:429
  362.5 97.6 %collective-permute-start.5 = (bf16[512,1024]{1,0:T(8,128)(2,1)}, bf16[512,1024]{1,0:T(8,128)(2,1)}, u32[]{:S(2)}, u32[]{:S(2)}) collective-permute-start(bf16[512,1024]{1,0:T(8,128)(2,1)} %get-tuple-element.200), channel_id=1, source_target_pairs={{0,24},{8,16},{16,8},{24,0},{1,25},{9,17},{17,9},{25,1},{2,26},{10... | collective-permute-start | bytes 3145736 | tf_op jit(solution)/shard_map/ppermute | solution.py:429
  377.6 33.7 %copy-start.6 = (f32[256,2048]{1,0:T(8,128)S(1)}, f32[256,2048]{1,0:T(8,128)}, u32[]{:S(2)}) copy-start(f32[256,2048]{1,0:T(8,128)} %get-tuple-element.71) | copy-start | bytes 6291460
  377.6 36.3 %copy-start.7 = (bf16[256,2048]{1,0:T(8,128)(2,1)S(1)}, bf16[256,2048]{1,0:T(8,128)(2,1)}, u32[]{:S(2)}) copy-start(bf16[256,2048]{1,0:T(8,128)(2,1)} %param.31) | copy-start | bytes 3145732
  382.0 78.1 %collective-permute-start = (bf16[512,1024]{1,0:T(8,128)(2,1)}, bf16[512,1024]{1,0:T(8,128)(2,1)}, u32[]{:S(2)}, u32[]{:S(2)}) collective-permute-start(bf16[512,1024]{1,0:T(8,128)(2,1)} %get-tuple-element.206), channel_id=1, source_target_pairs={{0,8},{8,0},{16,24},{24,16},{1,9},{9,1},{17,25},{25,17},{2,10},{10... | collective-permute-start | bytes 3145736 | tf_op jit(solution)/shard_map/ppermute | solution.py:429
  383.6 76.5 %collective-permute-start.1 = (bf16[512,1024]{1,0:T(8,128)(2,1)}, bf16[512,1024]{1,0:T(8,128)(2,1)}, u32[]{:S(2)}, u32[]{:S(2)}) collective-permute-start(bf16[512,1024]{1,0:T(8,128)(2,1)} %get-tuple-element.205), channel_id=1, source_target_pairs={{0,16},{8,24},{16,0},{24,8},{1,17},{9,25},{17,1},{25,9},{2,18},{10... | collective-permute-start | bytes 3145736 | tf_op jit(solution)/shard_map/ppermute | solution.py:429
  416.5 7.8 %copy-start.5 = (bf16[256,2048]{1,0:T(8,128)(2,1)}, bf16[256,2048]{1,0:T(8,128)(2,1)S(1)}, u32[]{:S(2)}) copy-start(bf16[256,2048]{1,0:T(8,128)(2,1)S(1)} %get-tuple-element.193.refs_0_.refs_1_.refs_2_.refs_3_) | copy-start | bytes 3145732
  416.5 7.8 %copy-start.16 = (bf16[512,1024]{1,0:T(8,128)(2,1)S(1)}, bf16[512,1024]{1,0:T(8,128)(2,1)}, u32[]{:S(2)}) copy-start(bf16[512,1024]{1,0:T(8,128)(2,1)} %get-tuple-element.204) | copy-start | bytes 3145732
  424.3 35.9 %collective-permute-start.2 = (bf16[512,1024]{1,0:T(8,128)(2,1)S(1)}, bf16[512,1024]{1,0:T(8,128)(2,1)}, u32[]{:S(2)}, u32[]{:S(2)}) collective-permute-start(bf16[512,1024]{1,0:T(8,128)(2,1)S(1)} %copy-done.16), channel_id=1, source_target_pairs={{0,24},{8,16},{16,8},{24,0},{1,25},{9,17},{17,9},{25,1},{2,26},{10... | collective-permute-start | bytes 3145736 | tf_op jit(solution)/shard_map/ppermute | solution.py:429
  525.9 81.0 %collective-permute-start.13 = (bf16[4,4,512,256]{3,2,1,0:T(8,128)(2,1)}, bf16[4,4,512,256]{3,2,1,0:T(8,128)(2,1)}, u32[]{:S(2)}, u32[]{:S(2)}) collective-permute-start(bf16[4,4,512,256]{3,2,1,0:T(8,128)(2,1)} %dynamic-slice_bitcast_fusion), channel_id=1, source_target_pairs={{0,1},{1,0},{2,3},{3,2},{4,5},{5,4},{6,7},{7,6},{8,9},{9,8},{10,11... | collective-permute-start | bytes 12582920 | tf_op jit(solution)/shard_map/ppermute | solution.py:448
  534.0 5.4 copy-start.4
  534.0 5.4 copy-start.11
  534.0 5.4 copy-start.26
  534.0 5.4 copy-start.30
  539.3 7.3 copy-start.2
  539.3 77.8 %collective-permute-start.6 = (bf16[4,4,512,256]{3,2,1,0:T(8,128)(2,1)}, bf16[4,4,512,256]{3,2,1,0:T(8,128)(2,1)}, u32[]{:S(2)}, u32[]{:S(2)}) collective-permute-start(bf16[4,4,512,256]{3,2,1,0:T(8,128)(2,1)} %dynamic-slice_bitcast_fusion.1), channel_id=1, source_target_pairs={{0,1},{1,0},{2,3},{3,2},{4,5},{5,4},{6,7},{7,6},{8,9},{9,8},{10,11... | collective-permute-start | bytes 12582920 | tf_op jit(solution)/shard_map/ppermute | solution.py:448
  578.7 23.2 %copy-start.40 = (f32[256]{0:T(256)S(1)}, f32[256]{0:T(256)}, u32[]{:S(2)}) copy-start(f32[256]{0:T(256)} %param.35) | copy-start | bytes 3076
  578.7 23.2 %copy-start.46 = (f32[256]{0:T(256)S(1)}, f32[256]{0:T(256)}, u32[]{:S(2)}) copy-start(f32[256]{0:T(256)} %param.57) | copy-start | bytes 3076
  578.7 23.9 %copy-start.19 = (f32[8,8,256]{2,1,0:T(8,128)S(1)}, f32[8,8,256]{2,1,0:T(8,128)}, u32[]{:S(2)}) copy-start(f32[8,8,256]{2,1,0:T(8,128)} %get-tuple-element.76) | copy-start | bytes 196612
  578.7 23.9 %copy-start.45 = (f32[128]{0:T(128)S(1)}, f32[128]{0:T(128)}, u32[]{:S(2)}) copy-start(f32[128]{0:T(128)} %param.36) | copy-start | bytes 1540
  578.7 23.8 %copy-start.48 = (f32[128]{0:T(128)S(1)}, f32[128]{0:T(128)}, u32[]{:S(2)}) copy-start(f32[128]{0:T(128)} %param.58) | copy-start | bytes 1540
  578.7 24.4 %copy-start.31 = (f32[8,128]{1,0:T(8,128)S(1)}, f32[8,128]{1,0:T(8,128)}, u32[]{:S(2)}) copy-start(f32[8,128]{1,0:T(8,128)} %get-tuple-element.77) | copy-start | bytes 12292
  578.7 24.4 %copy-start.42 = (f32[1024]{0:T(1024)S(1)}, f32[1024]{0:T(1024)}, u32[]{:S(2)}) copy-start(f32[1024]{0:T(1024)} %param.37) | copy-start | bytes 12292
  578.7 24.4 %copy-start.43 = (f32[1024]{0:T(1024)S(1)}, f32[1024]{0:T(1024)}, u32[]{:S(2)}) copy-start(f32[1024]{0:T(1024)} %param.59) | copy-start | bytes 12292
  578.7 25.0 %copy-start.22 = (f32[4,64,256]{2,1,0:T(8,128)S(1)}, f32[4,64,256]{2,1,0:T(8,128)}, u32[]{:S(2)}) copy-start(f32[4,64,256]{2,1,0:T(8,128)} %get-tuple-element.94) | copy-start | bytes 786436
  578.8 25.4 %copy-start.20 = (f32[2,2,1,128,128]{4,3,2,1,0:T(8,128)S(1)}, f32[2,2,1,128,128]{4,3,2,1,0:T(8,128)}, u32[]{:S(2)}) copy-start(f32[2,2,1,128,128]{4,3,2,1,0:T(8,128)} %param.53) | copy-start | bytes 786436
  578.8 26.7 %copy-start.21 = (f32[2,2,1,128,128]{4,3,2,1,0:T(8,128)S(1)}, f32[2,2,1,128,128]{4,3,2,1,0:T(8,128)}, u32[]{:S(2)}) copy-start(f32[2,2,1,128,128]{4,3,2,1,0:T(8,128)} %param.52) | copy-start | bytes 786436
  604.1 13.0 %slice-start = ((s8[8388608]{0:T(1024)(128)(4,1)}), s8[4194304]{0:T(1024)(128)(4,1)S(1)}, s32[]{:S(2)}) async-start(s8[8388608]{0:T(1024)(128)(4,1)} %bitcast.177), calls=%async_computation.7 | async-start | bytes 8388608
  606.8 10.3 %slice-start.1 = ((s8[8388608]{0:T(1024)(128)(4,1)}), s8[4194304]{0:T(1024)(128)(4,1)S(1)}, s32[]{:S(2)}) async-start(s8[8388608]{0:T(1024)(128)(4,1)} %bitcast.177), calls=%async_computation.8 | async-start | bytes 8388608
  613.0 26.3 %collective-permute-start.14 = (bf16[4,512,256]{2,1,0:T(8,128)(2,1)}, bf16[4,512,256]{2,1,0:T(8,128)(2,1)S(1)}, u32[]{:S(2)}, u32[]{:S(2)}) collective-permute-start(bf16[4,512,256]{2,1,0:T(8,128)(2,1)} %get-tuple-element.194), channel_id=1, source_target_pairs={{0,8},{8,0},{16,24},{24,16},{1,9},{9,1},{17,25},{25,17},{2,10},{10... | collective-permute-start | bytes 3145736 | tf_op jit(solution)/shard_map/ppermute | solution.py:429
  615.1 48.6 %collective-permute-start.15 = (bf16[4,512,256]{2,1,0:T(8,128)(2,1)S(1)}, bf16[4,512,256]{2,1,0:T(8,128)(2,1)S(1)}, u32[]{:S(2)}, u32[]{:S(2)}) collective-permute-start(bf16[4,512,256]{2,1,0:T(8,128)(2,1)S(1)} %get-tuple-element.196), channel_id=1, source_target_pairs={{0,16},{8,24},{16,0},{24,8},{1,17},{9,25},{17,1},{25,9},{2,18},{10... | collective-permute-start | bytes 3145736 | tf_op jit(solution)/shard_map/ppermute | solution.py:429
  616.6 47.1 %collective-permute-start.16 = (bf16[4,512,256]{2,1,0:T(8,128)(2,1)S(1)}, bf16[4,512,256]{2,1,0:T(8,128)(2,1)}, u32[]{:S(2)}, u32[]{:S(2)}) collective-permute-start(bf16[4,512,256]{2,1,0:T(8,128)(2,1)S(1)} %get-tuple-element.195), channel_id=1, source_target_pairs={{0,24},{8,16},{16,8},{24,0},{1,25},{9,17},{17,9},{25,1},{2,26},{10... | collective-permute-start | bytes 3145736 | tf_op jit(solution)/shard_map/ppermute | solution.py:429
  620.7 20.9 %copy-start.17 = (f32[256,128]{1,0:T(8,128)S(1)}, f32[256,128]{1,0:T(8,128)}, u32[]{:S(2)}) copy-start(f32[256,128]{1,0:T(8,128)} %get-tuple-element.221) | copy-start | bytes 393220
  620.7 20.9 %copy-start.23 = (f32[2,2,1,128,128]{4,3,2,1,0:T(8,128)S(1)}, f32[2,2,1,128,128]{4,3,2,1,0:T(8,128)}, u32[]{:S(2)}) copy-start(f32[2,2,1,128,128]{4,3,2,1,0:T(8,128)} %param.55) | copy-start | bytes 786436
  620.7 22.0 %copy-start.14 = (f32[256,2048]{1,0:T(8,128)S(1)}, f32[256,2048]{1,0:T(8,128)}, u32[]{:S(2)}) copy-start(f32[256,2048]{1,0:T(8,128)} %get-tuple-element.66) | copy-start | bytes 6291460
  620.7 22.0 %copy-start.15 = (bf16[256,2048]{1,0:T(8,128)(2,1)S(1)}, bf16[256,2048]{1,0:T(8,128)(2,1)}, u32[]{:S(2)}) copy-start(bf16[256,2048]{1,0:T(8,128)(2,1)} %reduce-scatter.5.cloned.1.call-done) | copy-start | bytes 3145732
  620.7 22.0 %copy-start.28 = (f32[1,2048]{1,0:T(1,128)S(1)}, f32[1,2048]{1,0:T(1,128)}, u32[]{:S(2)}) copy-start(f32[1,2048]{1,0:T(1,128)} %get-tuple-element.226) | copy-start | bytes 24580
  621.0 63.3 %collective-permute-start.7 = (bf16[4,512,256]{2,1,0:T(8,128)(2,1)S(1)}, bf16[4,512,256]{2,1,0:T(8,128)(2,1)S(1)}, u32[]{:S(2)}, u32[]{:S(2)}) collective-permute-start(bf16[4,512,256]{2,1,0:T(8,128)(2,1)S(1)} %get-tuple-element.197), channel_id=1, source_target_pairs={{0,8},{8,0},{16,24},{24,16},{1,9},{9,1},{17,25},{25,17},{2,10},{10... | collective-permute-start | bytes 3145736 | tf_op jit(solution)/shard_map/ppermute | solution.py:429
  622.5 82.2 %collective-permute-start.8 = (bf16[4,512,256]{2,1,0:T(8,128)(2,1)S(1)}, bf16[4,512,256]{2,1,0:T(8,128)(2,1)S(1)}, u32[]{:S(2)}, u32[]{:S(2)}) collective-permute-start(bf16[4,512,256]{2,1,0:T(8,128)(2,1)S(1)} %get-tuple-element.199), channel_id=1, source_target_pairs={{0,16},{8,24},{16,0},{24,8},{1,17},{9,25},{17,1},{25,9},{2,18},{10... | collective-permute-start | bytes 3145736 | tf_op jit(solution)/shard_map/ppermute | solution.py:429
  639.3 65.4 %collective-permute-start.9 = (bf16[4,512,256]{2,1,0:T(8,128)(2,1)S(1)}, bf16[4,512,256]{2,1,0:T(8,128)(2,1)S(1)}, u32[]{:S(2)}, u32[]{:S(2)}) collective-permute-start(bf16[4,512,256]{2,1,0:T(8,128)(2,1)S(1)} %get-tuple-element.198), channel_id=1, source_target_pairs={{0,24},{8,16},{16,8},{24,0},{1,25},{9,17},{17,9},{25,1},{2,26},{10... | collective-permute-start | bytes 3145736 | tf_op jit(solution)/shard_map/ppermute | solution.py:429
  665.5 42.7 %collective-permute-start.17 = (bf16[512,256]{1,0:T(8,128)(2,1)S(1)}, bf16[512,256]{1,0:T(8,128)(2,1)S(1)}, u32[]{:S(2)}, u32[]{:S(2)}) collective-permute-start(bf16[512,256]{1,0:T(8,128)(2,1)S(1)} %get-tuple-element.208), channel_id=1, source_target_pairs={{0,2},{1,3},{2,4},{3,5},{4,6},{5,7},{6,0},{7,1},{8,10},{9,11},{10,... | collective-permute-start | bytes 786440 | tf_op jit(solution)/shard_map/ppermute | solution.py:455
  666.7 44.8 %collective-permute-start.18 = (bf16[512,256]{1,0:T(8,128)(2,1)S(1)}, bf16[512,256]{1,0:T(8,128)(2,1)S(1)}, u32[]{:S(2)}, u32[]{:S(2)}) collective-permute-start(bf16[512,256]{1,0:T(8,128)(2,1)S(1)} %get-tuple-element.210), channel_id=1, source_target_pairs={{0,4},{1,5},{2,6},{3,7},{4,0},{5,1},{6,2},{7,3},{8,12},{9,13},{10,... | collective-permute-start | bytes 786440 | tf_op jit(solution)/shard_map/ppermute | solution.py:455
  684.3 27.2 %collective-permute-start.19 = (bf16[512,256]{1,0:T(8,128)(2,1)S(1)}, bf16[512,256]{1,0:T(8,128)(2,1)S(1)}, u32[]{:S(2)}, u32[]{:S(2)}) collective-permute-start(bf16[512,256]{1,0:T(8,128)(2,1)S(1)} %get-tuple-element.209), channel_id=1, source_target_pairs={{0,6},{1,7},{2,0},{3,1},{4,2},{5,3},{6,4},{7,5},{8,14},{9,15},{10,... | collective-permute-start | bytes 786440 | tf_op jit(solution)/shard_map/ppermute | solution.py:455
  705.4 11.1 %collective-permute-start.10 = (bf16[512,256]{1,0:T(8,128)(2,1)S(1)}, bf16[512,256]{1,0:T(8,128)(2,1)S(1)}, u32[]{:S(2)}, u32[]{:S(2)}) collective-permute-start(bf16[512,256]{1,0:T(8,128)(2,1)S(1)} %get-tuple-element.211), channel_id=1, source_target_pairs={{0,2},{1,3},{2,4},{3,5},{4,6},{5,7},{6,0},{7,1},{8,10},{9,11},{10,... | collective-permute-start | bytes 786440 | tf_op jit(solution)/shard_map/ppermute | solution.py:455
  706.3 16.5 %collective-permute-start.11 = (bf16[512,256]{1,0:T(8,128)(2,1)S(1)}, bf16[512,256]{1,0:T(8,128)(2,1)S(1)}, u32[]{:S(2)}, u32[]{:S(2)}) collective-permute-start(bf16[512,256]{1,0:T(8,128)(2,1)S(1)} %get-tuple-element.213), channel_id=1, source_target_pairs={{0,4},{1,5},{2,6},{3,7},{4,0},{5,1},{6,2},{7,3},{8,12},{9,13},{10,... | collective-permute-start | bytes 786440 | tf_op jit(solution)/shard_map/ppermute | solution.py:455
  708.2 14.6 %collective-permute-start.12 = (bf16[512,256]{1,0:T(8,128)(2,1)S(1)}, bf16[512,256]{1,0:T(8,128)(2,1)S(1)}, u32[]{:S(2)}, u32[]{:S(2)}) collective-permute-start(bf16[512,256]{1,0:T(8,128)(2,1)S(1)} %get-tuple-element.212), channel_id=1, source_target_pairs={{0,6},{1,7},{2,0},{3,1},{4,2},{5,3},{6,4},{7,5},{8,14},{9,15},{10,... | collective-permute-start | bytes 786440 | tf_op jit(solution)/shard_map/ppermute | solution.py:455
  (12 other events, 31.1 us)
Sparse Core Ops, SparseCore 0:
  16.2 34.0 all-gather.3
  51.8 102.2 all-gather.5
  166.8 108.4 all-gather.7
  323.1 88.1 reduce-scatter.2
  413.4 87.9 reduce-scatter.4

commit v2 on v1

--- a/solution.py
+++ b/solution.py
@@ -20,7 +20,7 @@
 MESH = pl.DeviceIdType.MESH
 BF16 = jnp.bfloat16
 F32 = jnp.float32
-VMEM_LIMIT = 56 * 1024 * 1024
+VMEM_LIMIT = 60 * 1024 * 1024
 ANY = pl.BlockSpec(memory_space=pl.ANY)
 WHOLE = pl.BlockSpec(memory_space=pltpu.VMEM)
 
@@ -207,7 +207,7 @@
             jax.ShapeDtypeStruct((cols * head_count, w_out.shape[1]), w_out.dtype),
             jax.ShapeDtypeStruct((head_count, 1, cols), F32),
         ),
-        in_specs=[ANY] * 3,
+        in_specs=[WHOLE] * 3,
         out_specs=(ANY,) * 3,
         scratch_shapes=[
             dma((2,)),
@@ -257,6 +257,360 @@
         ),
         name="project_out",
     )(attended, tokens, vectors, weight)
+
+
+def mixer_pass(mixer_in, cot_all, w_up, w_down, bias_up, owner, batch_size, head_count, cuts):
+    tok, width = mixer_in.shape
+    hid = w_up.shape[1]
+    n = head_count // 2
+    sub = tok // cuts
+    block = (n, 2, cuts, sub)
+    tiles = width // TILE
+    owned = tiles // batch_size
+    total_events = n * cuts
+
+    def kernel(
+        owner_ref, x_ref, cot_ref, up_ref, down_ref, bias_ref,
+        all_ref, hid_ref, pre_ref, mix_ref, grad_up_ref, grad_down_ref, out_ref, sum_ref,
+        x_buf, cot_buf, hid_buf, pre_buf, mine, give, pair_in, chain_in, right_in,
+        up_acc, down_acc, stage,
+        own_sem, x_sem, cot_sem, hid_sem, pre_sem, mix_sem,
+        right_send, left_send, side_send, side_recv, line_recv,
+        pair_send, pair_recv, chain_send, chain_recv, last_recv,
+    ):
+        h = lax.axis_index("head")
+        z = h // 2
+        c = h % 2
+        has_left = z > 0
+        has_right = z < n - 1
+
+        def at(chip):
+            return {"head": chip * 2 + c}
+
+        sibling = {"head": h + 1 - 2 * c}
+
+        def remote(src, dst, send, recv, target):
+            return pltpu.make_async_remote_copy(
+                src_ref=src, dst_ref=dst, send_sem=send, recv_sem=recv,
+                device_id=target, device_id_type=MESH,
+            )
+
+        def row_copy(chip, g, way):
+            spot = all_ref.at[chip, c, g]
+            if way == 0:
+                return remote(spot, spot, right_send.at[chip, g], line_recv.at[chip, g], at(z + 1))
+            if way == 1:
+                return remote(spot, spot, left_send.at[chip, g], line_recv.at[chip, g], at(z - 1))
+            return remote(spot, spot, side_send.at[chip, g], side_recv.at[chip, g], sibling)
+
+        def pair_copy(chip, g):
+            return remote(
+                give.at[chip, g], pair_in.at[chip, g], pair_send.at[chip, g],
+                pair_recv.at[chip, g], sibling,
+            )
+
+        def chain_copy(chip, g, target):
+            return remote(
+                mine.at[chip, g], chain_in.at[chip, g], chain_send.at[chip, g],
+                chain_recv.at[chip, g], at(target),
+            )
+
+        def last_copy(chip, g):
+            return remote(
+                mine.at[chip, g], right_in.at[g], chain_send.at[chip, g], last_recv.at[g],
+                at(z - 1),
+            )
+
+        barrier = pltpu.get_barrier_semaphore()
+        pl.semaphore_signal(barrier, inc=1, device_id=sibling, device_id_type=MESH)
+
+        @pl.when(has_left)
+        def _():
+            pl.semaphore_signal(barrier, inc=1, device_id=at(z - 1), device_id_type=MESH)
+
+        @pl.when(has_right)
+        def _():
+            pl.semaphore_signal(barrier, inc=1, device_id=at(z + 1), device_id_type=MESH)
+
+        own = pltpu.make_async_copy(x_ref, all_ref.at[z, c], own_sem)
+        own.start()
+        sum_ref[...] = jnp.zeros_like(sum_ref)
+        up_acc[...] = jnp.zeros_like(up_acc)
+        down_acc[...] = jnp.zeros_like(down_acc)
+        pl.semaphore_wait(
+            barrier, 1 + has_left.astype(jnp.int32) + has_right.astype(jnp.int32)
+        )
+        own.wait()
+
+        def pass_on(chip, g):
+            @pl.when((chip <= z) & has_right)
+            def _():
+                row_copy(chip, g, 0).start()
+
+            @pl.when((chip >= z) & has_left)
+            def _():
+                row_copy(chip, g, 1).start()
+
+            row_copy(chip, g, 2).start()
+
+        for g in range(cuts):
+            pass_on(z, g)
+
+        def compute(chip, g):
+            cot_load = pltpu.make_async_copy(cot_ref.at[chip, :, g], cot_buf, cot_sem)
+            cot_load.start()
+            row_copy(chip, g, 2).wait_recv()
+            x_load = pltpu.make_async_copy(all_ref.at[chip, :, g], x_buf, x_sem)
+            x_load.start()
+            cot_load.wait()
+            grad_hidden = matmul_nt(cot_buf[...].reshape(2 * sub, width), down_ref[...])
+            x_load.wait()
+            pre_act = matmul(x_buf[...].reshape(2 * sub, width), up_ref[...]) + bias_ref[...]
+            hidden, slope = gelu_pair(pre_act)
+            hid_buf[...] = hidden.astype(BF16).reshape(2, sub, hid)
+            hid_store = pltpu.make_async_copy(hid_buf, hid_ref.at[chip, :, g], hid_sem)
+            hid_store.start()
+            grad_pre = (grad_hidden * slope).astype(BF16)
+            pre_buf[...] = grad_pre.reshape(2, sub, hid)
+            pre_store = pltpu.make_async_copy(pre_buf, pre_ref.at[chip, :, g], pre_sem)
+            pre_store.start()
+            sum_ref[...] += jnp.sum(
+                grad_pre.astype(F32).reshape(2 * sub // 8, 8, hid), axis=0
+            )
+            share = matmul_nt(grad_pre, up_ref[...]).astype(BF16).reshape(2, sub, width)
+
+            @pl.when(c == 0)
+            def _():
+                mine[chip, g] = share[0]
+                give[chip, g] = share[1]
+
+            @pl.when(c == 1)
+            def _():
+                mine[chip, g] = share[1]
+                give[chip, g] = share[0]
+
+            pair_copy(chip, g).start()
+            hid_store.wait()
+            pre_store.wait()
+
+        def nearest(i):
+            edge = jnp.minimum(z, n - 1 - z)
+            near = (i + 1) // 2
+            inner = jnp.where(i % 2 == 1, z - near, z + near)
+            far = i - edge
+            outer = jnp.where(z < n - 1 - z, z + far, z - far)
+            return jnp.where(i <= 2 * edge, inner, outer)
+
+        def compute_rest(index):
+            chip = nearest(index // cuts)
+            g = index % cuts
+            loads = [
+                pltpu.make_async_copy(cot_ref.at[chip, :, g], cot_buf, cot_sem),
+                pltpu.make_async_copy(hid_ref.at[chip, :, g], hid_buf, hid_sem),
+                pltpu.make_async_copy(all_ref.at[chip, :, g], x_buf, x_sem),
+                pltpu.make_async_copy(pre_ref.at[chip, :, g], pre_buf, pre_sem),
+            ]
+            for load in loads:
+                load.start()
+            loads[1].wait()
+            hidden = hid_buf[...].reshape(2 * sub, hid)
+            stage[...] = matmul(hidden, down_ref[...]).astype(BF16).reshape(2, sub, width)
+            mix_store = pltpu.make_async_copy(stage, mix_ref.at[chip, :, g], mix_sem)
+            mix_store.start()
+            loads[0].wait()
+            down_acc[...] += matmul_t(cot_buf[...].reshape(2 * sub, width), hidden).reshape(
+                tiles, TILE, hid
+            )
+            loads[2].wait()
+            loads[3].wait()
+            up_acc[...] += matmul_t(
+                x_buf[...].reshape(2 * sub, width), pre_buf[...].reshape(2 * sub, hid)
+            ).reshape(tiles, TILE, hid)
+            mix_store.wait()
+
+        def add_up(chip, g, more):
+            pair_copy(chip, g).wait_recv()
+            total = mine[chip, g].astype(F32) + pair_in[chip, g].astype(F32)
+
+            @pl.when(more)
+            def _():
+                chain_copy(chip, g, z).wait_recv()
+                mine[chip, g] = (total + chain_in[chip, g].astype(F32)).astype(BF16)
+
+            @pl.when(jnp.logical_not(more))
+            def _():
+                mine[chip, g] = total.astype(BF16)
+
+        def step(t, carry):
+            d = t // cuts
+            g = t % cuts
+
+            @pl.when((d > 0) & (z >= d))
+            def _():
+                row_copy(z - d, g, 0).wait_recv()
+                pass_on(z - d, g)
+
+            @pl.when((d > 0) & (z + d < n))
+            def _():
+                row_copy(z + d, g, 1).wait_recv()
+                pass_on(z + d, g)
+
+            def one_side(side, inner):
+                chip = z + d * (2 * side - 1)
+
+                @pl.when((chip >= 0) & (chip < n) & (d < n) & ((d > 0) | (side == 0)))
+                def _():
+                    compute(chip, g)
+
+                return inner
+
+            lax.fori_loop(0, 2, one_side, 0)
+
+            from_left = jnp.maximum(t - z, 0)
+            chip_right = from_left // cuts
+            g_right = from_left % cuts
+
+            @pl.when((t >= z) & (chip_right > z) & (chip_right < n))
+            def _():
+                add_up(chip_right, g_right, has_left)
+                chain_copy(chip_right, g_right, z + 1).start()
+
+            from_right = jnp.maximum(t - (n - 1 - z), 0)
+            chip_left = n - 1 - from_right // cuts
+            g_left = from_right % cuts
+
+            @pl.when((t >= n - 1 - z) & (chip_left < z) & (chip_left >= 0))
+            def _():
+                add_up(chip_left, g_left, has_right)
+
+                @pl.when(chip_left == z - 1)
+                def _():
+                    last_copy(chip_left, g_left).start()
+
+                @pl.when(chip_left < z - 1)
+                def _():
+                    chain_copy(chip_left, g_left, z - 1).start()
+
+            events = (z >= d).astype(jnp.int32) + (z + d < n).astype(jnp.int32)
+            events = jnp.where((d == 0) | (d >= n), 1, events)
+            ready = (events < 2) & (carry < total_events)
+
+            @pl.when(ready)
+            def _():
+                compute_rest(carry)
+
+            return carry + ready.astype(jnp.int32)
+
+        done = lax.fori_loop(0, n * cuts + n - 1, step, 0)
+
+        def left_over(index, carry):
+            @pl.when(index >= done)
+            def _():
+                compute_rest(index)
+
+            return carry
+
+        lax.fori_loop(0, total_events, left_over, 0)
+
+        def put_tile(p, carry):
+            grad_up_ref[p] = up_acc[owner_ref[p]].astype(BF16)
+            grad_down_ref[p] = down_acc[owner_ref[p]].astype(BF16)
+            return carry
+
+        lax.fori_loop(0, tiles, put_tile, 0)
+
+        for g in range(cuts):
+            pair_copy(z, g).wait_recv()
+            out_ref[g] = mine[z, g].astype(F32) + pair_in[z, g].astype(F32)
+
+            @pl.when(has_left)
+            def _():
+                chain_copy(z, g, z).wait_recv()
+                out_ref[g] += chain_in[z, g].astype(F32)
+
+            @pl.when(has_right)
+            def _():
+                last_copy(z, g).wait_recv()
+                out_ref[g] += right_in[g].astype(F32)
+
+        def finish(chip, carry):
+            for g in range(cuts):
+
+                @pl.when((chip <= z) & has_right)
+                def _():
+                    row_copy(chip, g, 0).wait_send()
+
+                @pl.when((chip >= z) & has_left)
+                def _():
+                    row_copy(chip, g, 1).wait_send()
+
+                row_copy(chip, g, 2).wait_send()
+                pair_copy(chip, g).wait_send()
+
+                @pl.when(chip != z)
+                def _():
+                    chain_copy(chip, g, z).wait_send()
+
+            return carry
+
+        lax.fori_loop(0, n, finish, 0)
+
+    dma = pltpu.SemaphoreType.DMA
+    vm = pltpu.VMEM
+    each = dma((n, cuts))
+    shares = vm((n, cuts, sub, width), BF16)
+    outs = pl.pallas_call(
+        kernel,
+        out_shape=(
+            jax.ShapeDtypeStruct(block + (width,), BF16),
+            jax.ShapeDtypeStruct(block + (hid,), BF16),
+            jax.ShapeDtypeStruct(block + (hid,), BF16),
+            jax.ShapeDtypeStruct(block + (width,), BF16),
+            jax.ShapeDtypeStruct((tiles, TILE, hid), BF16),
+            jax.ShapeDtypeStruct((tiles, TILE, hid), BF16),
+            jax.ShapeDtypeStruct((cuts, sub, width), F32),
+            jax.ShapeDtypeStruct((8, hid), F32),
+        ),
+        in_specs=[pl.BlockSpec(memory_space=pltpu.SMEM), WHOLE, ANY, WHOLE, WHOLE, WHOLE],
+        out_specs=(ANY, ANY, ANY, ANY, WHOLE, WHOLE, WHOLE, WHOLE),
+        scratch_shapes=[
+            vm((2, sub, width), BF16),
+            vm((2, sub, width), BF16),
+            vm((2, sub, hid), BF16),
+            vm((2, sub, hid), BF16),
+            shares, shares, shares, shares,
+            vm((cuts, sub, width), BF16),
+            vm((tiles, TILE, hid), F32),
+            vm((tiles, TILE, hid), F32),
+            vm((2, sub, width), BF16),
+            dma, dma, dma, dma, dma, dma,
+            each, each, each, each, each,
+            each, each, each, each,
+            dma((cuts,)),
+        ],
+        compiler_params=pltpu.CompilerParams(
+            collective_id=3, has_side_effects=True, vmem_limit_bytes=VMEM_LIMIT
+        ),
+        cost_estimate=pl.CostEstimate(
+            flops=12 * n * 2 * tok * width * hid, bytes_accessed=300 * 1024 * 1024, transcendentals=0
+        ),
+        name="mixer_pass",
+    )(
+        owner,
+        mixer_in.reshape(cuts, sub, width),
+        cot_all.reshape(block + (width,)),
+        w_up,
+        w_down,
+        bias_up.reshape(1, hid),
+    )
+    _, _, _, mix_part, grad_up, grad_down, grad_in, bias_sum = outs
+    return (
+        mix_part.reshape(2 * n * tok, width),
+        grad_up.reshape(batch_size, owned * TILE, hid),
+        grad_down.reshape(batch_size, owned * TILE, hid),
+        grad_in.reshape(tok, width),
+        jnp.sum(bias_sum, axis=0),
+    )
 
 
 def attention_forward(queries, key_rows, value_turned, mask, slabs):
@@ -878,23 +1232,12 @@
     )
     inverse_two = inverse_wide[:, :1]
 
-    mixer_all = lax.all_gather(mixer_in, "head", axis=0, tiled=True)
-    grad_hidden = matmul_nt(cot_all, w_down).astype(BF16)
-    pre_act = matmul(mixer_all, w_up) + bias_up
-    hidden_f, slope = gelu_pair(pre_act)
-    hidden = hidden_f.astype(BF16)
-    grad_pre = (grad_hidden.astype(F32) * slope).astype(BF16)
-    grad_mixer_in = lax.psum_scatter(
-        matmul_nt(grad_pre, w_up).astype(BF16), "head", scatter_dimension=0, tiled=True
-    ).astype(F32)
-    grad_down = tiled_gradient(cot_all, hidden, owner, batch_size, 1)[:, 0]
-    down_shares = exchange_batch(grad_down, batch_size)
-    grad_up = tiled_gradient(mixer_all, grad_pre, owner, batch_size, 1)[:, 0]
-    up_shares = exchange_batch(grad_up, batch_size)
-    mix_one = lax.psum_scatter(
-        matmul(hidden, w_down).astype(BF16), "head", scatter_dimension=0, tiled=True
-    )
-    grad_up_bias = jnp.sum(grad_pre.astype(F32), axis=0)
+    mix_part, grad_up, grad_down, grad_mixer_in, grad_up_bias = mixer_pass(
+        mixer_in, cot_all, w_up, w_down, bias_up, owner, batch_size, head_count, 2
+    )
+    down_shares = [lax.psum_scatter(grad_down, "batch", scatter_dimension=0, tiled=False)]
+    up_shares = [lax.psum_scatter(grad_up, "batch", scatter_dimension=0, tiled=False)]
+    mix_one = lax.psum_scatter(mix_part, "head", scatter_dimension=0, tiled=True)
 
     cot_one = cotangent.astype(F32)
     grad_resid = cot_one + norm_back(grad_mixer_in, normed_two, inverse_two, gain_two)
@@ -913,12 +1256,9 @@
         grad_attended,
         head_count,
     )
-    grad_q, down_shares, up_shares, mix_one = lax.optimization_barrier(
-        (grad_q, down_shares, up_shares, mix_one)
-    )
-    output = resid + mix_one.astype(F32) + bias_down
     grad_query = tiled_gradient(normed_in, grad_q, owner, batch_size, head_count)
     query_total = flush(grad_query, batch_size, head_count).astype(BF16)
+    _, down_shares, up_shares = lax.optimization_barrier((grad_query, down_shares, up_shares))
     grad_kv = scatter_rows(grad_kv_part, head_count)
     grad_kv_low = grad_kv.astype(BF16)
     grad_normed_in = matmul_nt(grad_q, w_query_all) + matmul_nt(grad_kv_low, w_kv)
@@ -999,6 +1339,8 @@
         kv_root_right,
         jnp.stack([kv_tiles(kv_slab[:, :head_size]), kv_tiles(kv_slab[:, head_size:])]),
     )
+    _, mix_one = lax.optimization_barrier((kv_total, mix_one))
+    output = resid + mix_one.astype(F32) + bias_down
     vec_out = diagonal_update(vector_total, vector_second, vectors)
     query_out = diagonal_update(query_bias_total, query_second, bias_query)
     value_out = diagonal_update(value_bias_total, value_second, bias_value)

time: 754 us -> 657 us (0.87)
  waiting for transfers between devices: 255 us -> 90.7 us
  Pallas kernels: 282 us -> 432 us
  matrix products: 88.9 us -> 28.5 us
  starting transfers between devices: 28.8 us -> 17.4 us
  local copies, waits for them, and re-layouts: 39.4 us -> 29 us
    pallas_call x0 -> x1, Pallas kernels: none -> 176 us  [mixer_pass(): pl.pallas_call(kernel, out_shape=(jax.ShapeDtypeStruct(block + (width,),...]
    all_gather x1 -> x0, waiting for transfers between devices: 108 us -> none  [body(): mixer_all = lax.all_gather(mixer_in, 'head', axis=0, tiled=True)]
    reduce_scatter x2 -> x1, waiting for transfers between devices: 67.5 us -> 0.02 us  [body(): lax.psum_scatter(mix_part, 'head', scatter_dimension=0, tiled=True)]
    dot_general x4 -> x2, matrix products: 38.9 us -> 7.97 us  [matmul(): return jnp.dot(first_op, second_op, preferred_element_type=F32)]
    dot_general x5 -> x3, matrix products: 45.4 us -> 14.9 us  [matmul_nt(): lax.dot_general(first_op, second_op, (((1,), (1,)), ((), ())), preferred_...]
    pallas_call x4 -> x2, Pallas kernels: 44.2 us -> 15.4 us  [tiled_gradient(): pl.pallas_call(kernel, grid_spec=pltpu.PrefetchScalarGridSpec(num_scalar_...]
    ppermute x12 -> x6, starting transfers between devices: 17.9 us -> 6.28 us  [exchange_batch(): lax.ppermute(lax.dynamic_index_in_dim(chunks, b ^ k, 0, keepdims=False),...]
    ppermute x6, waiting for transfers between devices: 10.5 us -> 19 us  [flush(): lax.ppermute(lax.dynamic_index_in_dim(summed, there, 0, keepdims=False),...]
  transfers between devices with their start and end apart: 25 -> 19, of which waited for: 9 -> 6; matrix products, arithmetic and copies ran while one was open for 13% -> 12% of each run, Pallas kernels for 33% -> 38%
where the time goes in v2:
time: 657 us; the launch traced here: 647 us
  Pallas kernels  432 us (66%)
  waiting for transfers between devices  90.7 us (14%)
  other arithmetic  34 us (5%)
  local copies, waits for them, and re-layouts  29 us (4%)
  matrix products  28.5 us (4%)
  starting transfers between devices  17.4 us (3%)
  between operations  15 us (2%)
    pallas_call x1, Pallas kernels, mixer_pass(): pl.pallas_call(kernel, out_shape=(jax.ShapeDtypeStruct(block + (width,),...  176 us
    pallas_call x1, Pallas kernels, gather_weights(): pl.pallas_call(kernel, out_shape=(jax.ShapeDtypeStruct((rows, cols * head...  106 us
    ppermute x6, waiting for transfers between devices, exchange_batch(): lax.ppermute(lax.dynamic_index_in_dim(chunks, b ^ k, 0, keepdims=False),...  69.9 us
    pallas_call x2, Pallas kernels, shampoo(): pl.pallas_call(kernel, grid_spec=pltpu.PrefetchScalarGridSpec(num_scalar_...  31.7 us
    pallas_call x1, Pallas kernels, attention_backward(): pl.pallas_call(kernel, grid=(slabs,), out_shape=(jax.ShapeDtypeStruct((to...  25.9 us
    pallas_call x1, Pallas kernels, small_sums(): pl.pallas_call(kernel, out_shape=(jax.ShapeDtypeStruct((nb, rows, cols),...  25.6 us
    pallas_call x1, Pallas kernels, attention_forward(): pl.pallas_call(kernel, grid=(slabs,), out_shape=(jax.ShapeDtypeStruct((to...  24 us
    ppermute x6, waiting for transfers between devices, flush(): lax.ppermute(lax.dynamic_index_in_dim(summed, there, 0, keepdims=False),...  19 us
  transfers between devices with their start and end apart: 19, of which 6 were waited for; matrix products, arithmetic and copies ran while one was open for 12% of the time, Pallas kernels for 38%

profile of v2, /device:TPU:0, one launch (start us, length us, event | category | flops | bytes accessed | tf_op | source)
XLA Modules:
  0.0 646.7 jit_solution(7425045580368039277)
XLA Ops:
  7.3 1.7 fusion.62
  8.9 1.5 convert_reduce_fusion.1
  10.5 1.6 fusion.16
  13.4 1.1 fusion.34
  14.6 0.7 all-gather.5.cloned.1.call-update
  15.5 106.1 %gather_weights.1 = (bf16[2048,2048]{1,0:T(8,128)(2,1)}, bf16[2048,2048]{1,0:T(8,128)(2,1)}, f32[8,1,256]{2,1,0:T(1,128)}) custom-call(bf16[2048,256]{1,0:T(8,128)(2,1)} %refs_2_.2, bf16[256,2048]{1,0:T(8,128)(2,1)} %refs_3_.2, f32[1,256]{1,0:T(1,128)} %bitcast.220), custom_call_target="tpu_custom_call" | custom-call | bytes 209715200 | tf_op jit(solution)/shard_map/gather_weights/pallas_call | solution.py:203
  121.7 1.5 fusion.25.mask_ref
  123.2 6.9 %fusion.2.q_ref = bf16[256,2048]{1,0:T(8,128)(2,1)} fusion(bf16[256,2048]{1,0:T(8,128)(2,1)S(1)} %fusion.10.refs_0_.refs_1_.refs_2_.refs_3_, bf16[2048,2048]{1,0:T(8,128)(2,1)} %get-tuple-element.59, f32[2048]{0:T(1024)S(1)} %bitcast.225), kind=kOutput, calls=%fused_computation.12 | convolution fusion | flops 2148532224 | bytes 10493952 | tf_op jit(solution)/shard_map/dot_general | solution.py:29
  130.1 2.5 fusion.59
  132.6 1.0 copy.92.v_ref
  133.6 24.0 %attention_forward.1 = (bf16[256,2048]{1,0:T(8,128)(2,1)}, f32[8,2,256]{2,1,0:T(2,128)}) custom-call(bf16[256,2048]{1,0:T(8,128)(2,1)} %fusion.2.q_ref, bf16[2048,128]{1,0:T(8,128)(2,1)} %get-tuple-element.234.k_ref, bf16[128,2048]{1,0:T(8,128)(2,1)} %copy.92.v_ref, f32[2048,256]{1,0:T(8,128)} %fusion.25.mask_ref), custom_call_target="tpu_custom_call" | custom-call | flops 8589934592 | bytes 2097152 | tf_op jit(solution)/shard_map/attention_forward/pallas_call | solution.py:634
  157.5 8.8 %project_out.1 = (f32[256,2048]{1,0:T(8,128)}, bf16[256,2048]{1,0:T(8,128)(2,1)}, f32[256,2048]{1,0:T(8,128)}, f32[256,128]{1,0:T(8,128)}) custom-call(bf16[256,2048]{1,0:T(8,128)(2,1)} %get-tuple-element.62.att_ref.o_ref.refs_4_, bf16[256,2048]{1,0:T(8,128)(2,1)} %tok_ref.1, f32[6,2048]{1,0:T(8,128)} %vec_ref.1, bf16[2048,2048]{1,0:T(8,128)(2,1)} %get-tuple-element.63.w_ref), custom_call_target="tpu_custom_call" | custom-call | flops 2147483648 | bytes 58720256 | tf_op jit(solution)/shard_map/project_out/pallas_call | solution.py:244
  166.3 176.1 %mixer_pass.1 = (bf16[4,2,2,128,2048]{4,3,2,1,0:T(8,128)(2,1)}, bf16[4,2,2,128,1024]{4,3,2,1,0:T(8,128)(2,1)}, bf16[4,2,2,128,1024]{4,3,2,1,0:T(8,128)(2,1)}, bf...) custom-call(s32[16]{0:T(128)} %owner_ref.5, ...), custom_call_target="tpu_custom_call" | custom-call | flops 51539607552 | bytes 314572800 | tf_op jit(solution)/shard_map/mixer_pass/pallas_call | solution.py:562
  343.7 0.6 dynamic_slice.77.ids_ref
  344.4 0.9 dynamic-slice_convert_fusion
  345.3 1.0 copy.93.kt_ref
  346.7 1.2 copy-done.7
  347.9 1.0 fusion.23
  349.1 2.8 convert_reduce_fusion.3
  352.0 7.3 %convolution_convert_fusion.1.g_ref = bf16[256,2048]{1,0:T(8,128)(2,1)} fusion(bf16[256,2048]{1,0:T(8,128)(2,1)S(1)} %get-tuple-element.216.refs_0_.refs_1_.refs_2_.refs_3_, bf16[2048,2048]{1,0:T(8,128)(2,1)} %get-tuple-element.63.w_ref), kind=kOutput, calls=%fused_computation.14 | convolution fusion | flops 2148007936 | bytes 10485760 | tf_op jit(solution)/shard_map/dot_general | solution.py:39
  359.2 25.9 %attention_backward.1 = (bf16[256,2048]{1,0:T(8,128)(2,1)}, bf16[2048,256]{1,0:T(8,128)(2,1)}) custom-call(bf16[256,2048]{1,0:T(8,128)(2,1)} %fusion.2.q_ref, bf16[2048,128]{1,0:T(8,128)(2,1)} %get-tuple-element.234.k_ref, bf16[128,2048]{1,0:T(8,128)(2,1)} %copy.93.kt_ref, bf16[2048,128]{1,0:T(8,128)(2,1)} %get-tuple-element.231.v_ref, ...), custom_call_target="tpu_custom_call" | custom-call | flops 21474836480 | bytes 4194304 | tf_op jit(solution)/shard_map/attention_backward/pallas_call | solution.py:708
  385.2 7.7 %tiled_gradient.2 = bf16[4,8,512,256]{3,2,1,0:T(8,128)(2,1)} custom-call(s32[16]{0:T(128)} %owner_ref.5, bf16[256,2048]{1,0:T(8,128)(2,1)} %copy-done.1, bf16[256,2048]{1,0:T(8,128)(2,1)} %copy-done.1, bf16[256,2048]{1,0:T(8,128)(2,1)} %copy-done.1, bf16[256,2048]{1,0:T(8,128)(2,1)} %copy-done.1, bf16[256,2048]{1,0:T(8,128)(2,1)} %get-tuple-element.72.refs_4_), custom_call_target="tpu_custom_call" | custom-call | flops 2147483648 | bytes 10485760 | tf_op jit(solution)/shard_map/tiled_gradient/pallas_call | solution.py:757
  392.8 4.6 dynamic-slice_bitcast_fusion.1
  397.4 0.7 fusion.60
  398.1 18.5 %scatter_rows.1 = f32[256,256]{1,0:T(8,128)} custom-call(bf16[4,2,256,256]{3,2,1,0:T(8,128)(2,1)} %bitcast.192), custom_call_target="tpu_custom_call" | custom-call | tf_op jit(solution)/shard_map/scatter_rows/pallas_call | solution.py:872
  416.6 1.0 convert_element_type.149
  417.6 7.7 %tiled_gradient.3 = bf16[4,8,512,256]{3,2,1,0:T(8,128)(2,1)} custom-call(s32[16]{0:T(128)} %owner_ref.5, bf16[256,2048]{1,0:T(8,128)(2,1)} %copy-done.5, bf16[256,2048]{1,0:T(8,128)(2,1)} %copy-done.5, bf16[256,2048]{1,0:T(8,128)(2,1)} %copy-done.5, bf16[256,2048]{1,0:T(8,128)(2,1)} %copy-done.5, bf16[256,2048]{1,0:T(8,128)(2,1)} %get-tuple-element.62.att_ref.o_ref.refs_4_), custom_call_target="tpu_custom_call" | custom-call | flops 2147483648 | bytes 10485760 | tf_op jit(solution)/shard_map/tiled_gradient/pallas_call | solution.py:757
  425.4 4.7 dynamic-slice_bitcast_fusion
  430.1 0.8 convert_reduce_fusion.2
  431.4 1.0 copy.112
  433.7 5.9 fusion.63
  439.6 1.8 fusion.12
  441.4 1.6 stack.45
  443.0 25.6 %small_sums.1 = (f32[4,64,256]{2,1,0:T(8,128)}, f32[8,8,256]{2,1,0:T(8,128)}, f32[8,128]{1,0:T(8,128)}) custom-call(bf16[2,4,4,64,256]{4,3,2,1,0:T(8,128)(2,1)} %bitcast.180, f32[8,8,256]{2,1,0:T(8,128)} %bitcast.199, f32[8,128]{1,0:T(8,128)} %bitcast.215), custom_call_target="tpu_custom_call" | custom-call | tf_op jit(solution)/shard_map/small_sums/pallas_call | solution.py:1008
  468.7 0.9 slice.79
  469.6 1.0 fusion.61
  471.0 2.0 fusion.27
  473.1 0.7 divide_subtract_fusion.2
  474.9 1.4 fusion.30
  476.3 1.3 fusion.33
  477.6 5.0 fusion.1
  482.6 1.7 dynamic-slice_bitcast_fusion.7
  484.4 1.5 collective-permute-start.3
  485.9 0.7 divide_subtract_fusion
  487.1 1.4 collective-permute-start.1
  488.6 3.6 fusion
  492.4 1.6 collective-permute-start.10
  494.6 17.0 %collective-permute-done.3 = bf16[4,512,256]{2,1,0:T(8,128)(2,1)S(1)} collective-permute-done((bf16[4,512,256]{2,1,0:T(8,128)(2,1)}, bf16[4,512,256]{2,1,0:T(8,128)(2,1)S(1)}, u32[]{:S(2)}, u32[]{:S(2)}) %collective-permute-start.3) | collective-permute-done | bytes 1048608 | tf_op jit(solution)/shard_map/ppermute | solution.py:783
  512.2 2.1 fusion.15
  514.3 19.9 %collective-permute-done.2 = bf16[4,512,256]{2,1,0:T(8,128)(2,1)} collective-permute-done((bf16[4,512,256]{2,1,0:T(8,128)(2,1)}, bf16[4,512,256]{2,1,0:T(8,128)(2,1)}, u32[]{:S(2)}, u32[]{:S(2)}) %collective-permute-start.2) | collective-permute-done | bytes 1048608 | tf_op jit(solution)/shard_map/ppermute | solution.py:783
  534.2 2.4 fusion.22
  536.7 3.6 collective-permute-start.6
  540.8 15.7 %collective-permute-done.10 = bf16[4,512,256]{2,1,0:T(8,128)(2,1)S(1)} collective-permute-done((bf16[4,512,256]{2,1,0:T(8,128)(2,1)S(1)}, bf16[4,512,256]{2,1,0:T(8,128)(2,1)S(1)}, u32[]{:S(2)}, u32[]{:S(2)}) %collective-permute-start.10) | collective-permute-done | bytes 1048608 | tf_op jit(solution)/shard_map/ppermute | solution.py:783
  556.6 2.6 collective-permute-start.4
  559.2 17.2 %collective-permute-done.9 = bf16[4,512,256]{2,1,0:T(8,128)(2,1)S(1)} collective-permute-done((bf16[4,512,256]{2,1,0:T(8,128)(2,1)S(1)}, bf16[4,512,256]{2,1,0:T(8,128)(2,1)S(1)}, u32[]{:S(2)}, u32[]{:S(2)}) %collective-permute-start.9) | collective-permute-done | bytes 1048608 | tf_op jit(solution)/shard_map/ppermute | solution.py:783
  577.1 3.4 collective-permute-start.13
  581.2 0.7 fusion.47
  583.1 0.8 fusion.40.refs_0_
  584.0 3.3 collective-permute-done.13
  587.3 15.7 %collective-permute-done.12 = bf16[512,256]{1,0:T(8,128)(2,1)S(1)} collective-permute-done((bf16[512,256]{1,0:T(8,128)(2,1)S(1)}, bf16[512,256]{1,0:T(8,128)(2,1)S(1)}, u32[]{:S(2)}, u32[]{:S(2)}) %collective-permute-start.12) | collective-permute-done | bytes 262176 | tf_op jit(solution)/shard_map/ppermute | solution.py:809
  603.0 0.8 fusion.37.refs_1_
  603.8 10.2 %shampoo.2 = (f32[2,4,2,128,128]{4,3,2,1,0:T(8,128)}, f32[2,4,2,128,128]{4,3,2,1,0:T(8,128)}, f32[2,4,2,128,128]{4,3,2,1,0:T(8,128)}, f32[2,4,2,128,128]{4,3,2,1,0:T(8,128)}) custom-call(s32[4]{0:T(128)} %dynamic_slice.77.ids_ref, bf16[512,256]{1,0:T(8,128)(2,1)} %fusion.40.refs_0_, bf16[512,256]{1,0:T(8,128)(2,1)} %fusion.37.refs_1_, ...), custom_call_target="tpu_custom_call" | custom-call | flops 536870912 | bytes 10485760 | tf_op jit(solution)/shard_map/shampoo/pallas_call | solution.py:1110
  614.1 21.5 %shampoo.3 = (f32[2,4,8,128,128]{4,3,2,1,0:T(8,128)}, f32[2,4,8,128,128]{4,3,2,1,0:T(8,128)}, f32[2,4,8,128,128]{4,3,2,1,0:T(8,128)}, f32[2,4,8,128,128]{4,3,2,1,0:T(8,128)}) custom-call(s32[4]{0:T(128)} %dynamic_slice.77.ids_ref, bf16[512,1024]{1,0:T(8,128)(2,1)} %bitcast.191, bf16[512,1024]{1,0:T(8,128)(2,1)} %bitcast.190, bf16[2048,1024]{1,0:T(8,128)(2,1)} %refs_2_.3, ...), custom_call_target="tpu_custom_call" | custom-call | flops 2147483648 | bytes 41943040 | tf_op jit(solution)/shard_map/shampoo/pallas_call | solution.py:1110
  635.6 2.9 add_add_fusion
  (155 shorter events, 13.1 us)
Async XLA Ops:
  7.2 463.4 %copy-start = (f32[2,2,1,128,128]{4,3,2,1,0:T(8,128)S(1)}, f32[2,2,1,128,128]{4,3,2,1,0:T(8,128)}, u32[]{:S(2)}) copy-start(f32[2,2,1,128,128]{4,3,2,1,0:T(8,128)} %param.54) | copy-start | bytes 786436
  7.2 4.9 copy-start.12
  7.2 5.0 copy-start.13
  7.2 122.8 %all-gather.3.cloned.1.call-start = ((), (), s32[]{:S(2)}) async-start(), calls=%async_computation.3 | async-start | bytes 1179648 | tf_op jit(solution)/shard_map/all_gather | solution.py:1218
  8.9 3.5 copy-start.38
  8.9 3.5 copy-start.3
  10.5 2.5 copy-start.28
  13.4 109.8 %copy-start.1 = (bf16[256,2048]{1,0:T(8,128)(2,1)}, bf16[256,2048]{1,0:T(8,128)(2,1)S(1)}, u32[]{:S(2)}) copy-start(bf16[256,2048]{1,0:T(8,128)(2,1)S(1)} %fusion.10.refs_0_.refs_1_.refs_2_.refs_3_) | copy-start | bytes 3145732
  13.4 1.9 copy-start.43
  14.5 143.0 %all-gather.5.cloned.1.call-start = ((), (), s32[]{:S(2)}) async-start(), calls=%async_computation.4 | async-start | bytes 9437184 | tf_op jit(solution)/shard_map/all_gather | solution.py:1225
  15.3 598.7 %reduce-scatter.10.cloned.1.call-start = ((), (), s32[]{:S(2)}) async-start(), calls=%async_computation.6 | async-start | bytes 5242880
  121.6 1.6 copy-start.45
  342.4 271.6 %reduce-scatter.12.cloned.1.call-start = ((), (), s32[]{:S(2)}) async-start(), calls=%async_computation.7 | async-start | bytes 5242880
  343.0 292.6 %reduce-scatter.8.cloned.1.call-start = ((), (), s32[]{:S(2)}) async-start(), calls=%async_computation.5 | async-start | bytes 9437184 | tf_op jit(solution)/shard_map/reduce_scatter | solution.py:1240
  343.1 3.2 copy-start.23
  343.1 3.3 copy-start.6
  346.3 1.6 copy-start.7
  347.9 1.2 copy-start.9
  352.0 7.3 %copy-start.5 = (bf16[256,2048]{1,0:T(8,128)(2,1)}, bf16[256,2048]{1,0:T(8,128)(2,1)S(1)}, u32[]{:S(2)}) copy-start(bf16[256,2048]{1,0:T(8,128)(2,1)S(1)} %get-tuple-element.216.refs_0_.refs_1_.refs_2_.refs_3_) | copy-start | bytes 3145732
  397.4 80.2 %collective-permute-start = (bf16[4,4,512,256]{3,2,1,0:T(8,128)(2,1)}, bf16[4,4,512,256]{3,2,1,0:T(8,128)(2,1)}, u32[]{:S(2)}, u32[]{:S(2)}) collective-permute-start(bf16[4,4,512,256]{3,2,1,0:T(8,128)(2,1)} %dynamic-slice_bitcast_fusion.1), channel_id=1, source_target_pairs={{0,1},{1,0},{2,3},{3,2},{4,5},{5,4},{6,7},{7,6},{8,9},{9,8},{10,11... | collective-permute-start | bytes 12582920 | tf_op jit(solution)/shard_map/ppermute | solution.py:802
  425.3 4.8 copy-start.10
  425.4 5.5 copy-start.2
  430.1 58.4 %collective-permute-start.7 = (bf16[4,4,512,256]{3,2,1,0:T(8,128)(2,1)}, bf16[4,4,512,256]{3,2,1,0:T(8,128)(2,1)}, u32[]{:S(2)}, u32[]{:S(2)}) collective-permute-start(bf16[4,4,512,256]{3,2,1,0:T(8,128)(2,1)} %dynamic-slice_bitcast_fusion), channel_id=1, source_target_pairs={{0,1},{1,0},{2,3},{3,2},{4,5},{5,4},{6,7},{7,6},{8,9},{9,8},{10,11... | collective-permute-start | bytes 12582920 | tf_op jit(solution)/shard_map/ppermute | solution.py:802
  430.9 2.2 copy-start.26
  433.7 5.9 copy-start.4
  433.7 5.9 copy-start.18
  433.7 5.9 copy-start.29
  433.7 5.9 copy-start.32
  441.4 29.6 %copy-start.14 = (f32[256,128]{1,0:T(8,128)S(1)}, f32[256,128]{1,0:T(8,128)}, u32[]{:S(2)}) copy-start(f32[256,128]{1,0:T(8,128)} %get-tuple-element.235) | copy-start | bytes 393220
  442.9 28.1 %copy-start.15 = (f32[256,128]{1,0:T(8,128)S(1)}, f32[256,128]{1,0:T(8,128)}, u32[]{:S(2)}) copy-start(f32[256,128]{1,0:T(8,128)} %get-tuple-element.236) | copy-start | bytes 393220
  442.9 30.1 %copy-start.41 = (f32[256]{0:T(256)S(1)}, f32[256]{0:T(256)}, u32[]{:S(2)}) copy-start(f32[256]{0:T(256)} %get-tuple-element.201) | copy-start | bytes 3076
  442.9 30.1 %copy-start.42 = (f32[256]{0:T(256)S(1)}, f32[256]{0:T(256)}, u32[]{:S(2)}) copy-start(f32[256]{0:T(256)} %get-tuple-element.203) | copy-start | bytes 3076
  443.0 30.1 %copy-start.34 = (f32[256]{0:T(256)S(1)}, f32[256]{0:T(256)}, u32[]{:S(2)}) copy-start(f32[256]{0:T(256)} %param.35) | copy-start | bytes 3076
  443.0 30.1 %copy-start.40 = (f32[256]{0:T(256)S(1)}, f32[256]{0:T(256)}, u32[]{:S(2)}) copy-start(f32[256]{0:T(256)} %param.57) | copy-start | bytes 3076
  443.0 30.8 %copy-start.39 = (f32[128]{0:T(128)S(1)}, f32[128]{0:T(128)}, u32[]{:S(2)}) copy-start(f32[128]{0:T(128)} %param.36) | copy-start | bytes 1540
  443.0 30.8 %copy-start.44 = (f32[128]{0:T(128)S(1)}, f32[128]{0:T(128)}, u32[]{:S(2)}) copy-start(f32[128]{0:T(128)} %param.58) | copy-start | bytes 1540
  443.0 31.3 %copy-start.35 = (f32[1024]{0:T(1024)S(1)}, f32[1024]{0:T(1024)}, u32[]{:S(2)}) copy-start(f32[1024]{0:T(1024)} %param.37) | copy-start | bytes 12292
  443.0 31.3 %copy-start.36 = (f32[1024]{0:T(1024)S(1)}, f32[1024]{0:T(1024)}, u32[]{:S(2)}) copy-start(f32[1024]{0:T(1024)} %param.59) | copy-start | bytes 12292
  443.0 31.9 %copy-start.21 = (f32[2,2,1,128,128]{4,3,2,1,0:T(8,128)S(1)}, f32[2,2,1,128,128]{4,3,2,1,0:T(8,128)}, u32[]{:S(2)}) copy-start(f32[2,2,1,128,128]{4,3,2,1,0:T(8,128)} %param.52) | copy-start | bytes 786436
  468.7 5.1 copy-start.19
  468.7 5.6 copy-start.27
  468.7 7.6 %copy-start.22 = (f32[2,2,1,128,128]{4,3,2,1,0:T(8,128)S(1)}, f32[2,2,1,128,128]{4,3,2,1,0:T(8,128)}, u32[]{:S(2)}) copy-start(f32[2,2,1,128,128]{4,3,2,1,0:T(8,128)} %param.53) | copy-start | bytes 786436
  476.3 12.2 %slice-start = ((s8[8388608]{0:T(1024)(128)(4,1)}), s8[4194304]{0:T(1024)(128)(4,1)S(1)}, s32[]{:S(2)}) async-start(s8[8388608]{0:T(1024)(128)(4,1)} %bitcast.172), calls=%async_computation.8 | async-start | bytes 8388608
  477.6 10.9 %slice-start.1 = ((s8[8388608]{0:T(1024)(128)(4,1)}), s8[4194304]{0:T(1024)(128)(4,1)S(1)}, s32[]{:S(2)}) async-start(s8[8388608]{0:T(1024)(128)(4,1)} %bitcast.172), calls=%async_computation.9 | async-start | bytes 8388608
  482.6 3.3 copy-start.16
  482.6 3.3 copy-start.24
  484.4 27.3 %collective-permute-start.3 = (bf16[4,512,256]{2,1,0:T(8,128)(2,1)}, bf16[4,512,256]{2,1,0:T(8,128)(2,1)S(1)}, u32[]{:S(2)}, u32[]{:S(2)}) collective-permute-start(bf16[4,512,256]{2,1,0:T(8,128)(2,1)} %get-tuple-element.222), channel_id=1, source_target_pairs={{0,24},{8,16},{16,8},{24,0},{1,25},{9,17},{17,9},{25,1},{2,26},{10... | collective-permute-start | bytes 3145736 | tf_op jit(solution)/shard_map/ppermute | solution.py:783
  486.6 47.7 %collective-permute-start.2 = (bf16[4,512,256]{2,1,0:T(8,128)(2,1)}, bf16[4,512,256]{2,1,0:T(8,128)(2,1)}, u32[]{:S(2)}, u32[]{:S(2)}) collective-permute-start(bf16[4,512,256]{2,1,0:T(8,128)(2,1)} %get-tuple-element.223), channel_id=1, source_target_pairs={{0,16},{8,24},{16,0},{24,8},{1,17},{9,25},{17,1},{25,9},{2,18},{10... | collective-permute-start | bytes 3145736 | tf_op jit(solution)/shard_map/ppermute | solution.py:783
  487.1 47.1 %collective-permute-start.1 = (bf16[4,512,256]{2,1,0:T(8,128)(2,1)}, bf16[4,512,256]{2,1,0:T(8,128)(2,1)}, u32[]{:S(2)}, u32[]{:S(2)}) collective-permute-start(bf16[4,512,256]{2,1,0:T(8,128)(2,1)} %get-tuple-element.221), channel_id=1, source_target_pairs={{0,8},{8,0},{16,24},{24,16},{1,9},{9,1},{17,25},{25,17},{2,10},{10... | collective-permute-start | bytes 3145736 | tf_op jit(solution)/shard_map/ppermute | solution.py:783
  492.1 20.1 %copy-start.8 = (f32[256,2048]{1,0:T(8,128)S(1)}, f32[256,2048]{1,0:T(8,128)}, u32[]{:S(2)}) copy-start(f32[256,2048]{1,0:T(8,128)} %get-tuple-element.217) | copy-start | bytes 6291460
  492.2 20.1 %copy-start.30 = (f32[256]{0:T(256)S(1)}, f32[256]{0:T(256)}, u32[]{:S(2)}) copy-start(f32[256]{0:T(256)} %copy-done.28) | copy-start | bytes 3076
  492.2 20.1 %copy-start.33 = (f32[256]{0:T(256)S(1)}, f32[256]{0:T(256)}, u32[]{:S(2)}) copy-start(f32[256]{0:T(256)} %copy-done.31) | copy-start | bytes 3076
  492.4 64.2 %collective-permute-start.10 = (bf16[4,512,256]{2,1,0:T(8,128)(2,1)S(1)}, bf16[4,512,256]{2,1,0:T(8,128)(2,1)S(1)}, u32[]{:S(2)}, u32[]{:S(2)}) collective-permute-start(bf16[4,512,256]{2,1,0:T(8,128)(2,1)S(1)} %get-tuple-element.219), channel_id=1, source_target_pairs={{0,24},{8,16},{16,8},{24,0},{1,25},{9,17},{17,9},{25,1},{2,26},{10... | collective-permute-start | bytes 3145736 | tf_op jit(solution)/shard_map/ppermute | solution.py:783
  494.0 82.5 %collective-permute-start.9 = (bf16[4,512,256]{2,1,0:T(8,128)(2,1)S(1)}, bf16[4,512,256]{2,1,0:T(8,128)(2,1)S(1)}, u32[]{:S(2)}, u32[]{:S(2)}) collective-permute-start(bf16[4,512,256]{2,1,0:T(8,128)(2,1)S(1)} %get-tuple-element.220), channel_id=1, source_target_pairs={{0,16},{8,24},{16,0},{24,8},{1,17},{9,25},{17,1},{25,9},{2,18},{10... | collective-permute-start | bytes 3145736 | tf_op jit(solution)/shard_map/ppermute | solution.py:783
  511.6 64.9 %collective-permute-start.8 = (bf16[4,512,256]{2,1,0:T(8,128)(2,1)S(1)}, bf16[4,512,256]{2,1,0:T(8,128)(2,1)S(1)}, u32[]{:S(2)}, u32[]{:S(2)}) collective-permute-start(bf16[4,512,256]{2,1,0:T(8,128)(2,1)S(1)} %get-tuple-element.218), channel_id=1, source_target_pairs={{0,8},{8,0},{16,24},{24,16},{1,9},{9,1},{17,25},{25,17},{2,10},{10... | collective-permute-start | bytes 3145736 | tf_op jit(solution)/shard_map/ppermute | solution.py:783
  536.7 43.8 %collective-permute-start.6 = (bf16[512,256]{1,0:T(8,128)(2,1)S(1)}, bf16[512,256]{1,0:T(8,128)(2,1)S(1)}, u32[]{:S(2)}, u32[]{:S(2)}) collective-permute-start(bf16[512,256]{1,0:T(8,128)(2,1)S(1)} %get-tuple-element.228), channel_id=1, source_target_pairs={{0,6},{1,7},{2,0},{3,1},{4,2},{5,3},{6,4},{7,5},{8,14},{9,15},{10,... | collective-permute-start | bytes 786440 | tf_op jit(solution)/shard_map/ppermute | solution.py:809
  540.3 42.8 %collective-permute-start.5 = (bf16[512,256]{1,0:T(8,128)(2,1)S(1)}, bf16[512,256]{1,0:T(8,128)(2,1)S(1)}, u32[]{:S(2)}, u32[]{:S(2)}) collective-permute-start(bf16[512,256]{1,0:T(8,128)(2,1)S(1)} %get-tuple-element.229), channel_id=1, source_target_pairs={{0,4},{1,5},{2,6},{3,7},{4,0},{5,1},{6,2},{7,3},{8,12},{9,13},{10,... | collective-permute-start | bytes 786440 | tf_op jit(solution)/shard_map/ppermute | solution.py:809
  556.6 26.5 %collective-permute-start.4 = (bf16[512,256]{1,0:T(8,128)(2,1)S(1)}, bf16[512,256]{1,0:T(8,128)(2,1)S(1)}, u32[]{:S(2)}, u32[]{:S(2)}) collective-permute-start(bf16[512,256]{1,0:T(8,128)(2,1)S(1)} %get-tuple-element.227), channel_id=1, source_target_pairs={{0,2},{1,3},{2,4},{3,5},{4,6},{5,7},{6,0},{7,1},{8,10},{9,11},{10,... | collective-permute-start | bytes 786440 | tf_op jit(solution)/shard_map/ppermute | solution.py:809
  577.1 10.2 %collective-permute-start.13 = (bf16[512,256]{1,0:T(8,128)(2,1)S(1)}, bf16[512,256]{1,0:T(8,128)(2,1)S(1)}, u32[]{:S(2)}, u32[]{:S(2)}) collective-permute-start(bf16[512,256]{1,0:T(8,128)(2,1)S(1)} %get-tuple-element.225), channel_id=1, source_target_pairs={{0,6},{1,7},{2,0},{3,1},{4,2},{5,3},{6,4},{7,5},{8,14},{9,15},{10,... | collective-permute-start | bytes 786440 | tf_op jit(solution)/shard_map/ppermute | solution.py:809
  580.5 22.4 %collective-permute-start.12 = (bf16[512,256]{1,0:T(8,128)(2,1)S(1)}, bf16[512,256]{1,0:T(8,128)(2,1)S(1)}, u32[]{:S(2)}, u32[]{:S(2)}) collective-permute-start(bf16[512,256]{1,0:T(8,128)(2,1)S(1)} %get-tuple-element.226), channel_id=1, source_target_pairs={{0,4},{1,5},{2,6},{3,7},{4,0},{5,1},{6,2},{7,3},{8,12},{9,13},{10,... | collective-permute-start | bytes 786440 | tf_op jit(solution)/shard_map/ppermute | solution.py:809
  580.5 22.4 %collective-permute-start.11 = (bf16[512,256]{1,0:T(8,128)(2,1)S(1)}, bf16[512,256]{1,0:T(8,128)(2,1)S(1)}, u32[]{:S(2)}, u32[]{:S(2)}) collective-permute-start(bf16[512,256]{1,0:T(8,128)(2,1)S(1)} %get-tuple-element.224), channel_id=1, source_target_pairs={{0,2},{1,3},{2,4},{3,5},{4,6},{5,7},{6,0},{7,1},{8,10},{9,11},{10,... | collective-permute-start | bytes 786440 | tf_op jit(solution)/shard_map/ppermute | solution.py:809
  614.1 21.6 %copy-start.11 = (f32[256,2048]{1,0:T(8,128)S(1)}, f32[256,2048]{1,0:T(8,128)}, u32[]{:S(2)}) copy-start(f32[256,2048]{1,0:T(8,128)} %get-tuple-element.64) | copy-start | bytes 6291460
  614.1 21.6 %copy-start.25 = (f32[1,2048]{1,0:T(1,128)S(1)}, f32[1,2048]{1,0:T(1,128)}, u32[]{:S(2)}) copy-start(f32[1,2048]{1,0:T(1,128)} %get-tuple-element.241) | copy-start | bytes 24580
  635.6 2.9 copy-start.20
  (3 other events, 2.4 us)
Sparse Core Ops, SparseCore 0:
  14.7 35.4 all-gather.2
  51.8 103.6 all-gather.4
  342.6 49.6 reduce-scatter.9
  395.3 52.6 reduce-scatter.11
  450.2 92.3 reduce-scatter.7

commit v3 on v2

v3 whole, which is shorter than its diff:
```python
from functools import partial
import math

import jax
import jax.numpy as jnp
from jax import lax
from jax.experimental import pallas as pl
from jax.experimental.pallas import tpu as pltpu
from jax.sharding import PartitionSpec as P

EPSILON = 1e-05
DECAY_RATE = 0.5
MATRIX_RATE = 0.01
VECTOR_RATE = 0.1
SAFE_ADD = 1e-08
PRECISE = lax.Precision.HIGHEST
LOG2E = math.log2(math.e)
MASKED = -1e30
TILE = 128
MESH = pl.DeviceIdType.MESH
BF16 = jnp.bfloat16
F32 = jnp.float32
VMEM_LIMIT = 60 * 1024 * 1024
ANY = pl.BlockSpec(memory_space=pl.ANY)
WHOLE = pl.BlockSpec(memory_space=pltpu.VMEM)


def matmul(first_op, second_op):
    return jnp.dot(first_op, second_op, preferred_element_type=F32)


def matmul_t(first_op, second_op):
    return lax.dot_general(
        first_op, second_op, (((0,), (0,)), ((), ())), preferred_element_type=F32
    )


def matmul_nt(first_op, second_op):
    return lax.dot_general(
        first_op, second_op, (((1,), (1,)), ((), ())), preferred_element_type=F32
    )


def norm_stats(rows_in):
    mean_row = jnp.mean(rows_in, axis=-1, keepdims=True)
    centered = rows_in - mean_row
    variance = jnp.mean(centered * centered, axis=-1, keepdims=True)
    inverse = lax.rsqrt(variance + EPSILON)
    return (centered * inverse, inverse)


def norm_back(grad_out, normed, inverse, gain):
    scaled = grad_out * gain
    mean_one = jnp.mean(scaled, axis=-1, keepdims=True)
    mean_two = jnp.mean(scaled * normed, axis=-1, keepdims=True)
    return inverse * (scaled - mean_one - normed * mean_two)


def lanes(start, size, unit):
    return pl.ds(pl.multiple_of(start, unit), size)


def greet(targets):
    barrier = pltpu.get_barrier_semaphore()
    for target in targets:
        pl.semaphore_signal(barrier, inc=1, device_id=target, device_id_type=MESH)
    pl.semaphore_wait(barrier, len(targets))


def gather_tools(batch_size, head_count):
    chips = head_count // 2
    b = lax.axis_index("batch")
    h = lax.axis_index("head")
    z = h // 2
    c = h % 2

    def at_chip(r):
        return {"head": lax.rem(z + r, chips) * 2 + c}

    def other(d):
        return {"head": lax.rem(h + d, head_count)}

    def peer(k):
        return {"batch": b ^ k}

    def source(r):
        return lax.rem(z - r + chips, chips) * 2 + c

    def remote(src, dst, send, recv, target):
        copy = pltpu.make_async_remote_copy(
            src_ref=src,
            dst_ref=dst,
            send_sem=send,
            recv_sem=recv,
            device_id=target,
            device_id_type=MESH,
        )
        copy.start()
        return copy

    return b, h, {"head": h + 1 - 2 * c}, at_chip, other, peer, source, remote


def plane_exchange(place, tools, sems, batch_size, chips):
    b, _, sibling, _, _, peer, source, remote = tools
    xs, xr, fs, fr, cs, cr = sems
    ring = batch_size == 4
    direct = (1, 2) if ring else tuple(range(1, batch_size))
    hops = {}

    def start(r):
        spot = place(b, source(r))
        for k in direct:
            hops[k, r] = remote(spot, spot, xs.at[k, r], xr.at[k, r], peer(k))

    def finish():
        halves = {}
        sent = list(hops.values())
        received = []
        for r in range(1, chips):
            for k in direct:
                hops[k, r].wait_recv()
                if ring:
                    spot = place(b ^ k, source(r), k - 1)
                    halves[k, r] = remote(spot, spot, fs.at[k, r], fr.at[k, r], peer(3 - k))
                spot = place(b ^ k, source(r))
                received.append(remote(spot, spot, cs.at[k, r], cr.at[k, r], sibling))
        if ring:
            for r in range(1, chips):
                for k in direct:
                    halves[k, r].wait_recv()
                spot = place(b ^ 3, source(r))
                received.append(remote(spot, spot, cs.at[3, r], cr.at[3, r], sibling))
        return received, sent + received + list(halves.values())

    return start, finish


def place_rows(w_all, rows, batch_size):
    def place(quarter, head, half=None):
        part = rows // batch_size
        if half is not None:
            part = part // 2
            quarter = quarter * 2 + half
        return w_all.at[lanes(head * rows + quarter * part, part, part), :]

    return place


def gather_weights(w_query, w_out, bias_local, batch_size, head_count):
    rows, cols = w_query.shape
    chips = head_count // 2

    def kernel(
        q_ref, w_ref, bias_ref, q_all, w_all, bias_all, loc, zs, zr, ys, yr, xs, xr, fs, fr, cs, cr,
        bs, br,
    ):
        tools = gather_tools(batch_size, head_count)
        b, h, sibling, at_chip, other, peer, source, remote = tools

        def place_query(quarter, head, half=None):
            part = rows // batch_size
            if half is not None:
                part = part // 2
                quarter = quarter * 2 + half
            return q_all.at[lanes(quarter * part, part, part), lanes(head * cols, cols, cols)]

        place_out = place_rows(w_all, cols, batch_size)
        greet([other(d) for d in range(1, head_count)] + [peer(k) for k in range(1, batch_size)])
        own = (q_all.at[:, lanes(h * cols, cols, cols)], w_all.at[lanes(h * cols, cols, cols), :])
        q_part, w_part = rows // batch_size, cols // batch_size
        mine = (
            q_ref.at[lanes(b * q_part, q_part, q_part), :],
            w_ref.at[lanes(b * w_part, w_part, w_part), :],
        )
        sent = []
        received = []

        def z_start(m, place):
            copies = [
                remote(mine[m], place(b, h), zs.at[m, r], zr.at[m, r], at_chip(r))
                for r in range(1, chips)
            ]
            sent.extend(copies)
            return copies

        z_query = z_start(0, place_query)
        locals_ = []
        for m, src in enumerate((q_ref, w_ref)):
            local = pltpu.make_async_copy(src, own[m], loc.at[m])
            local.start()
            locals_.append(local)
            last = remote(src, own[m], ys.at[m, 0], yr.at[m, 0], sibling)
            sent.append(last)
            received.append(last)
        for d in range(1, head_count):
            copy = remote(bias_ref, bias_all.at[h], bs.at[d], br.at[d], other(d))
            sent.append(copy)
            received.append(copy)
        bias_own = pltpu.make_async_copy(bias_ref, bias_all.at[h], bs.at[0])
        bias_own.start()

        start, finish = plane_exchange(
            place_query, tools, (xs, xr, fs, fr, cs, cr), batch_size, chips
        )

        def across(m, place, r):
            spot = place(b, source(r))
            copy = remote(spot, spot, ys.at[m, r], yr.at[m, r], sibling)
            sent.append(copy)
            received.append(copy)

        for r in range(1, chips):
            z_query[r - 1].wait_recv()
            start(r)
            across(0, place_query, r)
        z_out = z_start(1, place_out)
        more_received, more_sent = finish()
        received.extend(more_received)
        sent.extend(more_sent)
        for r in range(1, chips):
            z_out[r - 1].wait_recv()
            across(1, place_out, r)
        for copy in received:
            copy.wait_recv()
        for copy in sent:
            copy.wait_send()
        for local in locals_:
            local.wait()
        bias_own.wait()

    dma = pltpu.SemaphoreType.DMA
    hop = dma((batch_size, chips))
    two = dma((2, chips))
    return pl.pallas_call(
        kernel,
        out_shape=(
            jax.ShapeDtypeStruct((rows, cols * head_count), w_query.dtype),
            jax.ShapeDtypeStruct((cols * head_count, w_out.shape[1]), w_out.dtype),
            jax.ShapeDtypeStruct((head_count, 1, cols), F32),
        ),
        in_specs=[WHOLE] * 3,
        out_specs=(ANY,) * 3,
        scratch_shapes=[
            dma((2,)), two, two, two, two, hop, hop, hop, hop, hop, hop,
            dma((head_count,)), dma((head_count,)),
        ],
        compiler_params=pltpu.CompilerParams(collective_id=0, has_side_effects=True),
        cost_estimate=pl.CostEstimate(
            flops=0, bytes_accessed=120 * 1024 * 1024, transcendentals=0
        ),
        name="gather_weights",
    )(w_query, w_out, bias_local)


def gather_rest(w_all, batch_size, head_count):
    chips = head_count // 2
    rows = w_all.shape[0] // head_count

    def kernel(in_ref, w_ref, xs, xr, fs, fr, cs, cr):
        del in_ref
        tools = gather_tools(batch_size, head_count)
        _, _, sibling, _, _, peer, _, _ = tools
        greet([sibling] + [peer(k) for k in range(1, batch_size)])
        start, finish = plane_exchange(
            place_rows(w_ref, rows, batch_size), tools, (xs, xr, fs, fr, cs, cr), batch_size, chips
        )
        for r in range(1, chips):
            start(r)
        received, sent = finish()
        for copy in received:
            copy.wait_recv()
        for copy in sent:
            copy.wait_send()

    hop = pltpu.SemaphoreType.DMA((batch_size, chips))
    return pl.pallas_call(
        kernel,
        out_shape=jax.ShapeDtypeStruct(w_all.shape, w_all.dtype),
        in_specs=[ANY],
        out_specs=ANY,
        scratch_shapes=[hop] * 6,
        input_output_aliases={0: 0},
        compiler_params=pltpu.CompilerParams(collective_id=5, has_side_effects=True),
        cost_estimate=pl.CostEstimate(
            flops=0, bytes_accessed=100 * 1024 * 1024, transcendentals=0
        ),
        name="gather_rest",
    )(w_all)


def project_out(attended, weight, tokens, vectors):
    tok, width = attended.shape

    def kernel(att_ref, tok_ref, vec_ref, w_ref, resid_ref, mixer_ref, normed_ref, inverse_ref):
        resid = matmul(att_ref[...], w_ref[...]) + vec_ref[4:5, :] + tok_ref[...].astype(F32)
        normed, inverse = norm_stats(resid)
        resid_ref[...] = resid
        normed_ref[...] = normed
        inverse_ref[...] = jnp.broadcast_to(inverse, inverse_ref.shape)
        mixer_ref[...] = (normed * vec_ref[2:3, :] + vec_ref[3:4, :]).astype(BF16)

    return pl.pallas_call(
        kernel,
        out_shape=(
            jax.ShapeDtypeStruct((tok, width), F32),
            jax.ShapeDtypeStruct((tok, width), BF16),
            jax.ShapeDtypeStruct((tok, width), F32),
            jax.ShapeDtypeStruct((tok, TILE), F32),
        ),
        in_specs=[WHOLE] * 4,
        out_specs=(WHOLE,) * 4,
        compiler_params=pltpu.CompilerParams(vmem_limit_bytes=VMEM_LIMIT),
        cost_estimate=pl.CostEstimate(
            flops=2 * tok * width * width, bytes_accessed=14 * width * width, transcendentals=0
        ),
        name="project_out",
    )(attended, tokens, vectors, weight)


def mixer_pass(mixer_in, cot_all, w_up, w_down, bias_up, owner, batch_size, head_count, cuts):
    tok, width = mixer_in.shape
    hid = w_up.shape[1]
    n = head_count // 2
    sub = tok // cuts
    block = (n, 2, cuts, sub)
    tiles = width // TILE
    owned = tiles // batch_size
    total_events = n * cuts

    def kernel(
        owner_ref, x_ref, cot_ref, up_ref, down_ref, bias_ref,
        all_ref, hid_ref, pre_ref, mix_ref, grad_up_ref, down_ref_all, out_ref, sum_ref,
        x_buf, cot_buf, hid_buf, pre_buf, mine, give, pair_in, chain_in, right_in,
        up_acc, down_acc, stage, grad_down_ref,
        own_sem, x_sem, cot_sem, hid_sem, pre_sem, mix_sem,
        right_send, left_send, side_send, side_recv, line_recv,
        pair_send, pair_recv, chain_send, chain_recv, last_recv, down_send, down_recv, down_sem,
    ):
        h = lax.axis_index("head")
        z = h // 2
        c = h % 2
        has_left = z > 0
        has_right = z < n - 1

        def at(chip):
            return {"head": chip * 2 + c}

        sibling = {"head": h + 1 - 2 * c}

        def remote(src, dst, send, recv, target):
            return pltpu.make_async_remote_copy(
                src_ref=src, dst_ref=dst, send_sem=send, recv_sem=recv,
                device_id=target, device_id_type=MESH,
            )

        def row_copy(chip, g, way):
            spot = all_ref.at[chip, c, g]
            if way == 0:
                return remote(spot, spot, right_send.at[chip, g], line_recv.at[chip, g], at(z + 1))
            if way == 1:
                return remote(spot, spot, left_send.at[chip, g], line_recv.at[chip, g], at(z - 1))
            return remote(spot, spot, side_send.at[chip, g], side_recv.at[chip, g], sibling)

        def pair_copy(chip, g):
            return remote(
                give.at[chip, g], pair_in.at[chip, g], pair_send.at[chip, g],
                pair_recv.at[chip, g], sibling,
            )

        def chain_copy(chip, g, target):
            return remote(
                mine.at[chip, g], chain_in.at[chip, g], chain_send.at[chip, g],
                chain_recv.at[chip, g], at(target),
            )

        def last_copy(chip, g):
            return remote(
                mine.at[chip, g], right_in.at[g], chain_send.at[chip, g], last_recv.at[g],
                at(z - 1),
            )

        b = lax.axis_index("batch")

        def peer(k):
            return {"batch": b ^ k}

        def down_copy(k):
            return remote(
                grad_down_ref.at[pl.ds((b ^ k) * owned, owned)], down_ref_all.at[k],
                down_send.at[k], down_recv.at[k], peer(k),
            )

        def down_own():
            return pltpu.make_async_copy(
                grad_down_ref.at[pl.ds(b * owned, owned)], down_ref_all.at[0], down_sem
            )

        barrier = pltpu.get_barrier_semaphore()
        pl.semaphore_signal(barrier, inc=1, device_id=sibling, device_id_type=MESH)
        for k in range(1, batch_size):
            pl.semaphore_signal(barrier, inc=1, device_id=peer(k), device_id_type=MESH)

        @pl.when(has_left)
        def _():
            pl.semaphore_signal(barrier, inc=1, device_id=at(z - 1), device_id_type=MESH)

        @pl.when(has_right)
        def _():
            pl.semaphore_signal(barrier, inc=1, device_id=at(z + 1), device_id_type=MESH)

        own = pltpu.make_async_copy(x_ref, all_ref.at[z, c], own_sem)
        own.start()
        sum_ref[...] = jnp.zeros_like(sum_ref)
        up_acc[...] = jnp.zeros_like(up_acc)
        down_acc[...] = jnp.zeros_like(down_acc)
        pl.semaphore_wait(
            barrier, batch_size + has_left.astype(jnp.int32) + has_right.astype(jnp.int32)
        )
        own.wait()

        def pass_on(chip, g):
            @pl.when((chip <= z) & has_right)
            def _():
                row_copy(chip, g, 0).start()

            @pl.when((chip >= z) & has_left)
            def _():
                row_copy(chip, g, 1).start()

            row_copy(chip, g, 2).start()

        for g in range(cuts):
            pass_on(z, g)

        def compute(chip, g):
            cot_load = pltpu.make_async_copy(cot_ref.at[chip, :, g], cot_buf, cot_sem)
            cot_load.start()
            row_copy(chip, g, 2).wait_recv()
            x_load = pltpu.make_async_copy(all_ref.at[chip, :, g], x_buf, x_sem)
            x_load.start()
            cot_load.wait()
            grad_hidden = matmul_nt(cot_buf[...].reshape(2 * sub, width), down_ref[...])
            x_load.wait()
            pre_act = matmul(x_buf[...].reshape(2 * sub, width), up_ref[...]) + bias_ref[...]
            hidden, slope = gelu_pair(pre_act)
            hid_buf[...] = hidden.astype(BF16).reshape(2, sub, hid)
            hid_store = pltpu.make_async_copy(hid_buf, hid_ref.at[chip, :, g], hid_sem)
            hid_store.start()
            grad_pre = (grad_hidden * slope).astype(BF16)
            pre_buf[...] = grad_pre.reshape(2, sub, hid)
            pre_store = pltpu.make_async_copy(pre_buf, pre_ref.at[chip, :, g], pre_sem)
            pre_store.start()
            sum_ref[...] += jnp.sum(
                grad_pre.astype(F32).reshape(2 * sub // 8, 8, hid), axis=0
            )
            share = matmul_nt(grad_pre, up_ref[...]).astype(BF16).reshape(2, sub, width)

            @pl.when(c == 0)
            def _():
                mine[chip, g] = share[0]
                give[chip, g] = share[1]

            @pl.when(c == 1)
            def _():
                mine[chip, g] = share[1]
                give[chip, g] = share[0]

            pair_copy(chip, g).start()
            down_acc[...] += matmul_t(
                cot_buf[...].reshape(2 * sub, width), hid_buf[...].reshape(2 * sub, hid)
            ).reshape(tiles, TILE, hid)
            hid_store.wait()
            pre_store.wait()

        def nearest(i):
            edge = jnp.minimum(z, n - 1 - z)
            near = (i + 1) // 2
            inner = jnp.where(i % 2 == 1, z - near, z + near)
            far = i - edge
            outer = jnp.where(z < n - 1 - z, z + far, z - far)
            return jnp.where(i <= 2 * edge, inner, outer)

        def compute_rest(index):
            chip = nearest(index // cuts)
            g = index % cuts
            loads = [
                pltpu.make_async_copy(hid_ref.at[chip, :, g], hid_buf, hid_sem),
                pltpu.make_async_copy(all_ref.at[chip, :, g], x_buf, x_sem),
                pltpu.make_async_copy(pre_ref.at[chip, :, g], pre_buf, pre_sem),
            ]
            for load in loads:
                load.start()
            loads[0].wait()
            hidden = hid_buf[...].reshape(2 * sub, hid)
            stage[...] = matmul(hidden, down_ref[...]).astype(BF16).reshape(2, sub, width)
            mix_store = pltpu.make_async_copy(stage, mix_ref.at[chip, :, g], mix_sem)
            mix_store.start()
            loads[1].wait()
            loads[2].wait()
            up_acc[...] += matmul_t(
                x_buf[...].reshape(2 * sub, width), pre_buf[...].reshape(2 * sub, hid)
            ).reshape(tiles, TILE, hid)
            mix_store.wait()

        def add_up(chip, g, more):
            pair_copy(chip, g).wait_recv()
            total = mine[chip, g].astype(F32) + pair_in[chip, g].astype(F32)

            @pl.when(more)
            def _():
                chain_copy(chip, g, z).wait_recv()
                mine[chip, g] = (total + chain_in[chip, g].astype(F32)).astype(BF16)

            @pl.when(jnp.logical_not(more))
            def _():
                mine[chip, g] = total.astype(BF16)

        def step(t, carry):
            d = t // cuts
            g = t % cuts

            @pl.when((d > 0) & (z >= d))
            def _():
                row_copy(z - d, g, 0).wait_recv()
                pass_on(z - d, g)

            @pl.when((d > 0) & (z + d < n))
            def _():
                row_copy(z + d, g, 1).wait_recv()
                pass_on(z + d, g)

            def one_side(side, inner):
                chip = z + d * (2 * side - 1)

                @pl.when((chip >= 0) & (chip < n) & (d < n) & ((d > 0) | (side == 0)))
                def _():
                    compute(chip, g)

                return inner

            lax.fori_loop(0, 2, one_side, 0)

            @pl.when(t == (jnp.maximum(z, n - 1 - z) + 1) * cuts - 1)
            def _():
                def put_down(p, inner):
                    grad_down_ref[p] = down_acc[owner_ref[p]].astype(BF16)
                    return inner

                lax.fori_loop(0, tiles, put_down, 0)
                for k in range(1, batch_size):
                    down_copy(k).start()
                down_own().start()

            from_left = jnp.maximum(t - z, 0)
            chip_right = from_left // cuts
            g_right = from_left % cuts

            @pl.when((t >= z) & (chip_right > z) & (chip_right < n))
            def _():
                add_up(chip_right, g_right, has_left)
                chain_copy(chip_right, g_right, z + 1).start()

            from_right = jnp.maximum(t - (n - 1 - z), 0)
            chip_left = n - 1 - from_right // cuts
            g_left = from_right % cuts

            @pl.when((t >= n - 1 - z) & (chip_left < z) & (chip_left >= 0))
            def _():
                add_up(chip_left, g_left, has_right)

                @pl.when(chip_left == z - 1)
                def _():
                    last_copy(chip_left, g_left).start()

                @pl.when(chip_left < z - 1)
                def _():
                    chain_copy(chip_left, g_left, z - 1).start()

            events = (z >= d).astype(jnp.int32) + (z + d < n).astype(jnp.int32)
            events = jnp.where((d == 0) | (d >= n), 1, events)
            ready = (events < 2) & (carry < total_events)

            @pl.when(ready)
            def _():
                compute_rest(carry)

            return carry + ready.astype(jnp.int32)

        done = lax.fori_loop(0, n * cuts + n - 1, step, 0)

        def left_over(index, carry):
            @pl.when(index >= done)
            def _():
                compute_rest(index)

            return carry

        lax.fori_loop(0, total_events, left_over, 0)

        def put_tile(p, carry):
            grad_up_ref[p] = up_acc[owner_ref[p]].astype(BF16)
            return carry

        lax.fori_loop(0, tiles, put_tile, 0)

        for g in range(cuts):
            pair_copy(z, g).wait_recv()
            out_ref[g] = mine[z, g].astype(F32) + pair_in[z, g].astype(F32)

            @pl.when(has_left)
            def _():
                chain_copy(z, g, z).wait_recv()
                out_ref[g] += chain_in[z, g].astype(F32)

            @pl.when(has_right)
            def _():
                last_copy(z, g).wait_recv()
                out_ref[g] += right_in[g].astype(F32)

        def finish(chip, carry):
            for g in range(cuts):

                @pl.when((chip <= z) & has_right)
                def _():
                    row_copy(chip, g, 0).wait_send()

                @pl.when((chip >= z) & has_left)
                def _():
                    row_copy(chip, g, 1).wait_send()

                row_copy(chip, g, 2).wait_send()
                pair_copy(chip, g).wait_send()

                @pl.when(chip != z)
                def _():
                    chain_copy(chip, g, z).wait_send()

            return carry

        lax.fori_loop(0, n, finish, 0)
        for k in range(1, batch_size):
            down_copy(k).wait()
        down_own().wait()

    dma = pltpu.SemaphoreType.DMA
    vm = pltpu.VMEM
    each = dma((n, cuts))
    shares = vm((n, cuts, sub, width), BF16)
    outs = pl.pallas_call(
        kernel,
        out_shape=(
            jax.ShapeDtypeStruct(block + (width,), BF16),
            jax.ShapeDtypeStruct(block + (hid,), BF16),
            jax.ShapeDtypeStruct(block + (hid,), BF16),
            jax.ShapeDtypeStruct(block + (width,), BF16),
            jax.ShapeDtypeStruct((tiles, TILE, hid), BF16),
            jax.ShapeDtypeStruct((batch_size, owned, TILE, hid), BF16),
            jax.ShapeDtypeStruct((cuts, sub, width), F32),
            jax.ShapeDtypeStruct((8, hid), F32),
        ),
        in_specs=[pl.BlockSpec(memory_space=pltpu.SMEM), WHOLE, ANY, WHOLE, WHOLE, WHOLE],
        out_specs=(ANY, ANY, ANY, ANY, WHOLE, ANY, WHOLE, WHOLE),
        scratch_shapes=[
            vm((2, sub, width), BF16),
            vm((2, sub, width), BF16),
            vm((2, sub, hid), BF16),
            vm((2, sub, hid), BF16),
            shares, shares, shares, shares,
            vm((cuts, sub, width), BF16),
            vm((tiles, TILE, hid), F32),
            vm((tiles, TILE, hid), F32),
            vm((2, sub, width), BF16),
            vm((tiles, TILE, hid), BF16),
            dma, dma, dma, dma, dma, dma,
            each, each, each, each, each,
            each, each, each, each,
            dma((cuts,)),
            dma((batch_size,)), dma((batch_size,)), dma,
        ],
        compiler_params=pltpu.CompilerParams(
            collective_id=3, has_side_effects=True, vmem_limit_bytes=VMEM_LIMIT
        ),
        cost_estimate=pl.CostEstimate(
            flops=12 * n * 2 * tok * width * hid, bytes_accessed=300 * 1024 * 1024, transcendentals=0
        ),
        name="mixer_pass",
    )(
        owner,
        mixer_in.reshape(cuts, sub, width),
        cot_all.reshape(block + (width,)),
        w_up,
        w_down,
        bias_up.reshape(1, hid),
    )
    _, _, _, mix_part, grad_up, grad_down, grad_in, bias_sum = outs
    return (
        mix_part.reshape(2 * n * tok, width),
        grad_up.reshape(batch_size, owned * TILE, hid),
        grad_down.reshape(batch_size, owned * TILE, hid),
        grad_in.reshape(tok, width),
        jnp.sum(bias_sum, axis=0),
    )


def attention_forward(queries, key_rows, value_turned, mask, slabs):
    tok, width = queries.shape
    seq_len, head_size = key_rows.shape
    slab = width // slabs
    heads = slab // head_size
    scale = LOG2E / math.sqrt(head_size)

    def kernel(q_ref, k_ref, v_ref, mask_ref, o_ref, log_ref):
        for j in range(heads):
            spot = slice(j * head_size, (j + 1) * head_size)
            scores = matmul_nt(k_ref[...], q_ref[:, spot]) * scale + mask_ref[...]
            highest = jnp.max(scores, axis=0, keepdims=True)
            raised = jnp.exp2(scores - highest)
            total = jnp.sum(raised, axis=0, keepdims=True)
            out = matmul(v_ref[...], raised.astype(BF16)) / total
            o_ref[:, spot] = out.T.astype(BF16)
            log_ref[0, j : j + 1, :] = highest + jnp.log2(total)

    return pl.pallas_call(
        kernel,
        grid=(slabs,),
        out_shape=(
            jax.ShapeDtypeStruct((tok, width), BF16),
            jax.ShapeDtypeStruct((slabs, heads, tok), F32),
        ),
        in_specs=[
            pl.BlockSpec((tok, slab), lambda i: (0, i)),
            pl.BlockSpec((seq_len, head_size), lambda i: (0, 0)),
            pl.BlockSpec((head_size, seq_len), lambda i: (0, 0)),
            pl.BlockSpec((seq_len, tok), lambda i: (0, 0)),
        ],
        out_specs=(
            pl.BlockSpec((tok, slab), lambda i: (0, i)),
            pl.BlockSpec((1, heads, tok), lambda i: (i, 0, 0)),
        ),
        compiler_params=pltpu.CompilerParams(vmem_limit_bytes=VMEM_LIMIT),
        cost_estimate=pl.CostEstimate(
            flops=8 * tok * seq_len * width,
            bytes_accessed=4 * tok * width,
            transcendentals=tok * seq_len * slabs * heads,
        ),
        name="attention_forward",
    )(queries, key_rows, value_turned, mask)


def backward_pass(
    owner, grad_mixer, cotangent, tokens, normed_two, inverse_two, vectors, queries, attended,
    log_totals, key_rows, key_turned, value_rows, mask, w_query_all, w_out_all, w_kv, up_parts,
    grad_up, batch_size, head_count,
):
    tok, width = tokens.shape
    seq_len, head_size = key_rows.shape
    slab = width // head_count
    heads = slab // head_size
    n = head_count // 2
    tiles = width // TILE
    cols_out = width // batch_size
    owned = tiles // batch_size
    half_rows = slab // 2
    kv_cols = 2 * head_size
    kv_rows = width // head_count // batch_size
    ring = batch_size == 4
    scale = LOG2E / math.sqrt(head_size)
    plain_scale = 1.0 / math.sqrt(head_size)
    block = 512 if seq_len % 512 == 0 else seq_len

    def kernel(
        owner_ref, gm_ref, cot_ref, tok_ref, n2_ref, i2_ref, vec_ref, q_ref, att_ref, log_ref,
        k_ref, kt_ref, v_ref, mask_ref, wq_ref, wo_ref, wkv_ref, up_ref, gu_ref,
        tokens_out, query_out, out_out, kv_out, vec_out, up_out, gu_out,
        branch, wide_tiles, normed_owned, branch_owned, grad_in, wq_buf, wo_buf, dk, dv,
        give, mine, pair_in, land, hop, z_land,
        dkv, dkv_pair, dkv_here, dkv_land,
        kv_part, kv_pair, kv_sum, kv_land, kv_half, kv_zland,
        vec_part, vec_land, vec_sum, vec_bland, up_land,
        gm_sem, n2_sem, cot_sem, free_sem, wq_sem, wo_sem, pair_send, pair_recv, hop_send, hop_recv, land_send, land_recv,
        z_send, z_recv, dkv_s, dkv_r, dkz_s, dkz_r,
        s_pair, r_pair, s_kvb, r_kvb, s_kvz, r_kvz, s_kva, r_kva,
        s_vh, r_vh, s_vb, r_vb, s_va, r_va, s_up, r_up, gu_send, gu_recv, gu_sem,
    ):
        b = lax.axis_index("batch")
        h = lax.axis_index("head")
        z = h // 2
        c = h % 2
        sibling = {"head": h + 1 - 2 * c}

        def at_chip(r):
            return {"head": lax.rem(z + r, n) * 2 + c}

        def other(d):
            return {"head": lax.rem(h + d, head_count)}

        def peer(k):
            return {"batch": b ^ k}

        def remote(src, dst, send, recv, target):
            return pltpu.make_async_remote_copy(
                src_ref=src, dst_ref=dst, send_sem=send, recv_sem=recv,
                device_id=target, device_id_type=MESH,
            )

        greet([other(d) for d in range(1, head_count)] + [peer(k) for k in range(1, batch_size)])

        up_copies = [
            remote(up_ref, up_land.at[k], s_up.at[k], r_up.at[k], peer(k))
            for k in range(1, batch_size)
        ]
        for copy in up_copies:
            copy.start()

        gu_own = pltpu.make_async_copy(gu_ref.at[b], gu_out.at[0], gu_sem)
        gu_own.start()

        def gu_copies(p):
            part = pl.ds(p * TILE, TILE)
            return [
                remote(
                    gu_ref.at[b ^ k, part], gu_out.at[k, part], gu_send.at[k, p], gu_recv.at[k, p],
                    peer(k),
                )
                for k in range(1, batch_size)
            ]

        for copy in gu_copies(0):
            copy.start()

        def slab_at(s):
            chip = lax.rem(z + 1 + s // 2, n)
            return chip * 2 + jnp.where(s % 2 == 0, 1 - c, c)

        def weight_loads(s):
            i = slab_at(s)
            return (
                pltpu.make_async_copy(
                    wq_ref.at[:, lanes(i * slab, slab, slab)], wq_buf, wq_sem
                ),
                pltpu.make_async_copy(
                    wo_ref.at[lanes(i * slab, slab, slab), :], wo_buf, wo_sem
                ),
            )

        norm_loads = (
            pltpu.make_async_copy(gm_ref, tokens_out, gm_sem),
            pltpu.make_async_copy(n2_ref, grad_in, n2_sem),
            pltpu.make_async_copy(cot_ref, branch, cot_sem),
        )
        for load in norm_loads + weight_loads(0):
            load.start()

        def put_vector(row, value):
            for i in range(head_count):
                vec_part[i, row : row + 1, :] = value[:, i * slab : (i + 1) * slab]

        def column_sum(value):
            return jnp.sum(value, axis=0, keepdims=True)

        for load in norm_loads:
            load.wait()
        grad_mix = tokens_out[...]
        normed_two_rows = grad_in[...]
        grad_out_rows = branch[...].astype(F32)
        put_vector(5, column_sum(grad_out_rows))
        grad_resid = grad_out_rows + norm_back(
            grad_mix, normed_two_rows, i2_ref[:, :1], vec_ref[2:3, :]
        )
        put_vector(2, column_sum(grad_mix * normed_two_rows))
        put_vector(3, column_sum(grad_mix))
        tokens_out[...] = grad_resid
        grad_branch = grad_resid.astype(BF16)
        branch[...] = grad_branch

        put_vector(4, column_sum(grad_branch.astype(F32)))

        for p in range(tiles):
            wide_tiles[p] = branch[:, p * TILE : (p + 1) * TILE]

        for p in range(tiles):
            branch_owned[:, p * TILE : (p + 1) * TILE] = wide_tiles[owner_ref[p]]
        normed_one, inverse_one = norm_stats(tok_ref[...].astype(F32))
        normed_in = (normed_one * vec_ref[0:1, :] + vec_ref[1:2, :]).astype(BF16)
        for p in range(tiles):
            wide_tiles[p] = normed_in[:, p * TILE : (p + 1) * TILE]

        for p in range(tiles):
            normed_owned[:, p * TILE : (p + 1) * TILE] = wide_tiles[owner_ref[p]]
        dk[...] = jnp.zeros_like(dk)
        dv[...] = jnp.zeros_like(dv)
        grad_in[...] = jnp.zeros_like(grad_in)

        def pair_copy(q):
            return remote(
                give.at[q % 2], pair_in.at[q % 2], pair_send.at[q], pair_recv.at[q], sibling
            )

        halves = (pl.ds(0, half_rows), pl.ds(half_rows, half_rows))

        def hop_copy(q, k):
            part = halves[1 if k == 1 else 0]
            return remote(
                mine.at[q, b ^ 3, part], hop.at[q, k - 1], hop_send.at[q, k], hop_recv.at[q, k],
                peer(k),
            )

        def land_copy(q, k, which):
            if which is None:
                return remote(
                    mine.at[q, b ^ k], land.at[q, k - 1], land_send.at[q, k, 0],
                    land_recv.at[q, k, 0], peer(k),
                )
            part = halves[which]
            return remote(
                mine.at[q, b ^ k, part], land.at[q, k - 1, part], land_send.at[q, k, which],
                land_recv.at[q, k, which], peer(k),
            )

        def z_copy(q):
            return remote(
                mine.at[q, b], z_land.at[q], z_send.at[q], z_recv.at[q], at_chip(q % n + 1)
            )

        def pair_start(q, value):
            @pl.when(q >= 2)
            def _():
                pair_copy(q - 2).wait_send()
                pl.semaphore_wait(free_sem, 1)

            for k in range(batch_size):
                give[q % 2, k] = value[:, k * cols_out : (k + 1) * cols_out]
            pair_copy(q).start()

        def plane_start(q):
            pair_copy(q).wait_recv()
            mine[q] = (mine[q].astype(F32) + pair_in[q % 2].astype(F32)).astype(BF16)

            @pl.when(q < 2 * n - 2)
            def _():
                pl.semaphore_signal(free_sem, inc=1, device_id=sibling, device_id_type=MESH)

            if ring:
                hop_copy(q, 1).start()
                hop_copy(q, 2).start()
                land_copy(q, 1, 1).start()
                land_copy(q, 2, 0).start()
            else:
                for k in range(1, batch_size):
                    land_copy(q, k, None).start()

        def plane_hop(q):
            if not ring:
                return
            for k in (1, 2):
                hop_copy(q, 3 - k).wait_recv()
                which = 0 if k == 1 else 1
                part = halves[which]
                mine[q, b ^ k, part, :] = (
                    mine[q, b ^ k, part, :].astype(F32) + hop[q, 2 - k].astype(F32)
                ).astype(BF16)
                land_copy(q, k, which).start()

        def plane_end(q):
            total = mine[q, b].astype(F32)
            for k in range(1, 3 if ring else batch_size):
                for which in (0, 1) if ring else (None,):
                    land_copy(q, k, which).wait_recv()
                total += land[q, k - 1].astype(F32)
            mine[q, b] = total.astype(BF16)

            @pl.when(q % n < n - 1)
            def _():
                z_copy(q).start()

        def out_gradient(i):
            att = att_ref[:, lanes(i * slab, slab, slab)]
            return matmul(att.astype(F32).T.astype(BF16), branch_owned[...]).astype(BF16)

        def put_mine(q, value):
            for k in range(batch_size):
                mine[q, k] = value[:, k * cols_out : (k + 1) * cols_out]

        def out_pairs(j, carry):
            pair_start(j, out_gradient(slab_at(2 * j)))
            put_mine(j, out_gradient(slab_at(2 * j + 1)))

            @pl.when(j >= 1)
            def _():
                plane_start(j - 1)

            return carry

        lax.fori_loop(0, n, out_pairs, 0)
        plane_start(n - 1)

        def work(s, carry):
            j = s // 2
            i = slab_at(s)
            cols = lanes(i * slab, slab, slab)

            loads = weight_loads(s)
            loads[1].wait()
            grad_att = matmul_nt(branch[...], wo_buf[...]).astype(BF16)

            @pl.when(s + 1 < head_count)
            def _():
                weight_loads(s + 1)[1].start()

            queries_here = q_ref[:, cols]
            att_here = att_ref[:, cols]
            logs_here = log_ref[i]
            parts = []
            for e in range(heads):
                spot = slice(e * head_size, (e + 1) * head_size)
                query = queries_here[:, spot]
                grad = grad_att[:, spot]
                joint = grad.astype(F32) * att_here[:, spot].astype(F32)
                delta = jnp.sum(joint.T, axis=0, keepdims=True)
                logs = logs_here[e : e + 1, :]
                total = jnp.zeros((head_size, tok), F32)
                for start in range(0, seq_len, block):
                    part = slice(start, start + block)
                    scores = matmul_nt(k_ref[part, :], query) * scale
                    probs = jnp.exp2(scores + (mask_ref[part, :].astype(F32) - logs))
                    grad_probs = matmul_nt(v_ref[part, :], grad)
                    grad_scores = (probs * (grad_probs - delta)).astype(BF16)
                    dv[part, :] += matmul(probs.astype(BF16), grad)
                    dk[part, :] += matmul(grad_scores, query)
                    total += matmul(kt_ref[:, part], grad_scores)
                parts.append(total * plain_scale)
            turned = jnp.concatenate(parts, axis=0) if heads > 1 else parts[0]
            grad_q = turned.T.astype(BF16)
            vec_part[i, 6:7, :] = column_sum(grad_q.astype(F32))
            grad_query = matmul(turned.astype(BF16), normed_owned[...]).astype(BF16)

            @pl.when(s % 2 == 0)
            def _():
                pair_start(n + j, grad_query)

            @pl.when(s % 2 == 1)
            def _():
                put_mine(n + j, grad_query)

            loads[0].wait()
            grad_in[...] += matmul_nt(grad_q, wq_buf[...])

            @pl.when(s + 1 < head_count)
            def _():
                weight_loads(s + 1)[0].start()

            @pl.when(s < n)
            def _():
                plane_hop(s)

            @pl.when((s >= 2) & (s < n + 2))
            def _():
                plane_end(s - 2)

            @pl.when(s % 2 == 1)
            def _():
                plane_start(n + j)

                @pl.when(j >= 1)
                def _():
                    plane_hop(n + j - 1)

                @pl.when(j >= 2)
                def _():
                    plane_end(n + j - 2)

            return carry

        lax.fori_loop(0, head_count, work, 0)

        dkv[:, :, :, :head_size] = (dk[...] * plain_scale).astype(BF16).reshape(n, 2, tok, head_size)
        dkv[:, :, :, head_size:] = dv[...].astype(BF16).reshape(n, 2, tok, head_size)
        dkv_swap = remote(dkv.at[:, 1 - c], dkv_pair, dkv_s, dkv_r, sibling)
        dkv_swap.start()
        dkv_swap.wait_recv()
        for r in range(n):
            dkv_here[r] = (dkv[r, c].astype(F32) + dkv_pair[r].astype(F32)).astype(BF16)
        dkv_copies = [
            remote(
                dkv_here.at[lax.rem(z + r, n)], dkv_land.at[r], dkz_s.at[r], dkz_r.at[r],
                at_chip(r),
            )
            for r in range(1, n)
        ]
        for copy in dkv_copies:
            copy.start()
        normed_one, inverse_one = norm_stats(tok_ref[...].astype(F32))
        normed_in = (normed_one * vec_ref[0:1, :] + vec_ref[1:2, :]).astype(BF16)
        plane_hop(2 * n - 1)
        for p in range(1, owned):
            for copy in gu_copies(p):
                copy.start()
        grad_kv = dkv_here[z].astype(F32)
        for copy in dkv_copies:
            copy.wait_recv()
        for r in range(1, n):
            grad_kv += dkv_land[r].astype(F32)
        grad_kv = grad_kv.astype(BF16)

        kv_part[...] = (
            matmul_t(normed_in, grad_kv)
            .astype(BF16)
            .reshape(n, 2, batch_size, kv_rows, kv_cols)
        )
        pair_kv = remote(kv_part.at[:, 1 - c], kv_pair, s_pair, r_pair, sibling)
        pair_kv.start()

        grad_normed = grad_in[...] + matmul_nt(grad_kv, wkv_ref[...])
        pair_kv.wait_recv()
        for r in range(n):
            kv_sum[r] = (kv_part[r, c].astype(F32) + kv_pair[r].astype(F32)).astype(BF16)
        kv_copies = [
            remote(kv_sum.at[:, b ^ k], kv_land.at[k], s_kvb.at[k], r_kvb.at[k], peer(k))
            for k in range(1, batch_size)
        ]
        for copy in kv_copies:
            copy.start()
        put_vector(0, column_sum(grad_normed * normed_one))
        put_vector(1, column_sum(grad_normed))
        for i in range(head_count):
            vec_part[i, 7:8, :] = jnp.zeros((1, slab), F32)
        vec_part[0, 7:8, :head_size] = column_sum(grad_kv[:, head_size:].astype(F32))
        vec_copies = [
            remote(
                vec_part.at[lax.rem(h + d, head_count)], vec_land.at[d], s_vh.at[d], r_vh.at[d],
                other(d),
            )
            for d in range(1, head_count)
        ]
        for copy in vec_copies:
            copy.start()
        tokens_out[...] += norm_back(grad_normed, normed_one, inverse_one, vec_ref[0:1, :])
        total = vec_part[h]
        for copy in vec_copies:
            copy.wait_recv()
        for d in range(1, head_count):
            total += vec_land[d]
        vec_sum[...] = total
        vec_bcopies = [
            remote(vec_sum, vec_bland.at[k], s_vb.at[k], r_vb.at[k], peer(k))
            for k in range(1, batch_size)
        ]
        for copy in vec_bcopies:
            copy.start()
        up_total = up_ref[...]
        for copy in up_copies:
            copy.wait_recv()
        for k in range(1, batch_size):
            up_total += up_land[k]
        up_out[...] = up_total
        for copy in kv_copies:
            copy.wait_recv()
        kv_total = kv_sum[:, b].astype(F32)
        for k in range(1, batch_size):
            kv_total += kv_land[k].astype(F32)
        kv_half[...] = kv_total.astype(BF16)
        kv_zcopies = [
            remote(
                kv_half.at[lax.rem(z + r, n)], kv_zland.at[r], s_kvz.at[r], r_kvz.at[r], at_chip(r)
            )
            for r in range(1, n)
        ]
        for copy in kv_zcopies:
            copy.start()
        for copy in vec_bcopies:
            copy.wait_recv()
        total = vec_sum[...]
        for k in range(1, batch_size):
            total += vec_bland[k]
        vec_out[h] = total
        vec_acopies = [
            remote(vec_out.at[h], vec_out.at[h], s_va.at[d], r_va.at[d], other(d))
            for d in range(1, head_count)
        ]
        for copy in vec_acopies:
            copy.start()
        for copy in kv_zcopies:
            copy.wait_recv()
        kv_mine = kv_half[z].astype(F32)
        for r in range(1, n):
            kv_mine += kv_zland[r].astype(F32)
        kv_out[b] = kv_mine
        kv_acopies = [
            remote(kv_out.at[b], kv_out.at[b], s_kva.at[k], r_kva.at[k], peer(k))
            for k in range(1, batch_size)
        ]
        for copy in kv_acopies:
            copy.start()

        plane_end(2 * n - 2)
        plane_end(2 * n - 1)
        for first, target in ((0, out_out), (n, query_out)):
            total = mine[first + n - 1, b].astype(F32)
            for r in range(n - 1):
                z_copy(first + r).wait_recv()
                total += z_land[first + r].astype(F32)
            target[0] = total.astype(BF16)
        for copy in vec_acopies + kv_acopies:
            copy.wait_recv()

        for copy in up_copies + [dkv_swap, pair_kv] + dkv_copies + vec_copies + kv_copies:
            copy.wait_send()
        for copy in vec_bcopies + kv_zcopies + vec_acopies + kv_acopies:
            copy.wait_send()
        pair_copy(2 * n - 2).wait_send()
        pair_copy(2 * n - 1).wait_send()
        for p in range(owned):
            for copy in gu_copies(p):
                copy.wait()
        gu_own.wait()

        def finish(q, carry):
            @pl.when(q % n < n - 1)
            def _():
                z_copy(q).wait_send()

            if ring:
                for k in (1, 2):
                    hop_copy(q, k).wait_send()
                    for which in (0, 1):
                        land_copy(q, k, which).wait_send()
            else:
                for k in range(1, batch_size):
                    land_copy(q, k, None).wait_send()
            return carry

        lax.fori_loop(0, 2 * n, finish, 0)

    dma = pltpu.SemaphoreType.DMA
    vm = pltpu.VMEM
    nb, nh = batch_size, head_count
    lands = 2 if ring else nb - 1
    shared = (nb, slab, cols_out)
    return pl.pallas_call(
        kernel,
        out_shape=(
            jax.ShapeDtypeStruct((tok, width), F32),
            jax.ShapeDtypeStruct((1, slab, cols_out), BF16),
            jax.ShapeDtypeStruct((1, slab, cols_out), BF16),
            jax.ShapeDtypeStruct((nb, kv_rows, kv_cols), F32),
            jax.ShapeDtypeStruct((nh, 8, slab), F32),
            jax.ShapeDtypeStruct(up_parts.shape, F32),
            jax.ShapeDtypeStruct(grad_up.shape, grad_up.dtype),
        ),
        in_specs=[pl.BlockSpec(memory_space=pltpu.SMEM), ANY, ANY, WHOLE, ANY]
        + [WHOLE] * 9
        + [ANY, ANY, WHOLE, WHOLE, ANY],
        out_specs=(WHOLE,) * 6 + (ANY,),
        scratch_shapes=[
            vm((tok, width), BF16),
            vm((tiles, tok, TILE), BF16),
            vm((tok, width), BF16),
            vm((tok, width), BF16),
            vm((tok, width), F32),
            vm((width, slab), BF16),
            vm((slab, width), BF16),
            vm((seq_len, head_size), F32),
            vm((seq_len, head_size), F32),
            vm((2,) + shared, BF16),
            vm((2 * n,) + shared, BF16),
            vm((2,) + shared, BF16),
            vm((2 * n, lands, slab, cols_out), BF16),
            vm((2 * n, 2, half_rows, cols_out) if ring else (1, 1, 16, TILE), BF16),
            vm((2 * n, slab, cols_out), BF16),
            vm((n, 2, tok, kv_cols), BF16),
            vm((n, tok, kv_cols), BF16),
            vm((n, tok, kv_cols), BF16),
            vm((n, tok, kv_cols), BF16),
            vm((n, 2, nb, kv_rows, kv_cols), BF16),
            vm((n, nb, kv_rows, kv_cols), BF16),
            vm((n, nb, kv_rows, kv_cols), BF16),
            vm((nb, n, kv_rows, kv_cols), BF16),
            vm((n, kv_rows, kv_cols), BF16),
            vm((n, kv_rows, kv_cols), BF16),
            vm((nh, 8, slab), F32),
            vm((nh, 8, slab), F32),
            vm((8, slab), F32),
            vm((nb, 8, slab), F32),
            vm((nb,) + up_parts.shape, F32),
            dma, dma, dma, pltpu.SemaphoreType.REGULAR, dma, dma,
            dma((2 * n,)), dma((2 * n,)), dma((2 * n, 3)), dma((2 * n, 3)),
            dma((2 * n, nb, 2)), dma((2 * n, nb, 2)), dma((2 * n,)), dma((2 * n,)), dma, dma, dma((n,)), dma((n,)),
            dma, dma, dma((nb,)), dma((nb,)), dma((n,)), dma((n,)), dma((nb,)), dma((nb,)),
            dma((nh,)), dma((nh,)), dma((nb,)), dma((nb,)), dma((nh,)), dma((nh,)),
            dma((nb,)), dma((nb,)), dma((nb, owned)), dma((nb, owned)), dma,
        ],
        compiler_params=pltpu.CompilerParams(
            collective_id=4, has_side_effects=True, vmem_limit_bytes=VMEM_LIMIT + 2 * 1024 * 1024
        ),
        cost_estimate=pl.CostEstimate(
            flops=20 * tok * seq_len * width + 8 * tok * width * width,
            bytes_accessed=200 * 1024 * 1024,
            transcendentals=tok * seq_len * width // head_size,
        ),
        name="backward_pass",
    )(
        owner, grad_mixer, cotangent, tokens, normed_two, inverse_two, vectors, queries, attended,
        log_totals, key_rows, key_turned, value_rows, mask, w_query_all, w_out_all, w_kv, up_parts,
        grad_up,
    )


def split_high(value):
    high = value.astype(BF16)
    return high, (value - high.astype(F32)).astype(BF16)


def matmul_three(first_op, second_op):
    first_high, first_low = split_high(first_op)
    second_high, second_low = split_high(second_op)
    return (
        matmul(first_high, second_high)
        + matmul(first_high, second_low)
        + matmul(first_low, second_high)
    )


def shampoo(
    first, second, first_weight, second_weight, owned, left, right, root_left, root_right, wide_rows
):
    _, owned_count, columns, _, _ = left.shape

    def kernel(ids_ref, *refs):
        del ids_ref
        one, two, w_one, w_two, l_ref, r_ref, p_ref, q_ref, g_out, l_out, r_out, w_out = refs

        def update(turned):
            for t in range(columns):
                spot = slice(t * TILE, (t + 1) * TILE)
                shares = two if turned else one
                part = (slice(None), spot) if wide_rows else (spot, slice(None))
                grad = shares[(0,) + part].astype(F32)
                for i in range(1, shares.shape[0]):
                    grad += shares[(i,) + part].astype(F32)
                if turned == wide_rows:
                    grad = grad.T
                if turned:
                    weight = w_two[spot, :].astype(F32)
                else:
                    weight = w_one[:, spot].astype(F32)
                high = grad.astype(BF16)
                g_out[0, 0, t] = grad
                l_out[0, 0, t] = DECAY_RATE * l_ref[0, 0, t] + (1.0 - DECAY_RATE) * matmul_nt(
                    high, high
                )
                r_out[0, 0, t] = DECAY_RATE * r_ref[0, 0, t] + (1.0 - DECAY_RATE) * matmul_t(
                    high, high
                )
                stepped = matmul_three(p_ref[0, 0, t], grad)
                stepped = matmul_three(stepped, q_ref[0, 0, t])
                w_out[0, 0, t] = weight - MATRIX_RATE * stepped

        @pl.when(pl.program_id(0) == 0)
        def _():
            update(False)

        @pl.when(pl.program_id(0) == 1)
        def _():
            update(True)

    last = owned_count - 1
    def share(array, place):
        if wide_rows:
            return pl.BlockSpec(
                (array.shape[0], TILE, columns * TILE), lambda m, p, ids: (0, place(m, p), 0)
            )
        return pl.BlockSpec(
            (array.shape[0], columns * TILE, TILE), lambda m, p, ids: (0, 0, place(m, p))
        )

    share_one = share(first, lambda m, p: jnp.where(m == 0, p, last))
    share_two = share(second, lambda m, p: jnp.where(m == 1, p, 0))
    weight_one = pl.BlockSpec(
        (TILE, columns * TILE), lambda m, p, ids: (ids[jnp.where(m == 0, p, last)], 0)
    )
    weight_two = pl.BlockSpec(
        (columns * TILE, TILE), lambda m, p, ids: (0, ids[jnp.where(m == 1, p, 0)])
    )
    stat = pl.BlockSpec((1, 1, columns, TILE, TILE), lambda m, p, ids: (m, p, 0, 0, 0))
    shape = jax.ShapeDtypeStruct(left.shape, F32)
    return pl.pallas_call(
        kernel,
        grid_spec=pltpu.PrefetchScalarGridSpec(
            num_scalar_prefetch=1,
            grid=(2, owned_count),
            in_specs=[share_one, share_two, weight_one, weight_two] + [stat] * 4,
            out_specs=[stat] * 4,
        ),
        out_shape=[shape] * 4,
        compiler_params=pltpu.CompilerParams(vmem_limit_bytes=VMEM_LIMIT),
        cost_estimate=pl.CostEstimate(
            flops=left.size * TILE * 16, bytes_accessed=left.size * 40, transcendentals=0
        ),
        name="shampoo",
    )(owned, first, second, first_weight, second_weight, left, right, root_left, root_right)


def shampoo_update(grad_tiles, left_old, right_old, root_left, root_right, weight_tiles):
    outer_left = jnp.einsum("...ij,...kj->...ik", grad_tiles, grad_tiles, precision=PRECISE)
    outer_right = jnp.einsum("...ji,...jk->...ik", grad_tiles, grad_tiles, precision=PRECISE)
    left_new = DECAY_RATE * left_old + (1.0 - DECAY_RATE) * outer_left
    right_new = DECAY_RATE * right_old + (1.0 - DECAY_RATE) * outer_right
    stepped = jnp.einsum("...ij,...jk->...ik", root_left, grad_tiles, precision=PRECISE)
    stepped = jnp.einsum("...ij,...jk->...ik", stepped, root_right, precision=PRECISE)
    return (grad_tiles, left_new, right_new, weight_tiles - MATRIX_RATE * stepped)


def diagonal_update(gradient, second, current):
    second_new = DECAY_RATE * second + (1.0 - DECAY_RATE) * gradient * gradient
    return (
        gradient,
        second_new,
        current - VECTOR_RATE * gradient / (jnp.sqrt(second_new) + SAFE_ADD),
    )


def gelu_pair(u):
    root = math.sqrt(2.0 / math.pi)
    square = u * u
    turn = jnp.tanh(root * u * (1.0 + 0.044715 * square))
    half = 0.5 * (1.0 + turn)
    slope = half + 0.5 * u * (1.0 - turn * turn) * root * (1.0 + 3.0 * 0.044715 * square)
    return u * half, slope


def body(
    tokens,
    cotangent,
    doc_starts,
    owner,
    vectors,
    bias_query,
    bias_value,
    bias_up,
    w_query,
    w_key,
    w_value,
    w_out,
    w_up,
    w_down,
    attn_left,
    attn_right,
    attn_root_left,
    attn_root_right,
    mixer_left,
    mixer_right,
    mixer_root_left,
    mixer_root_right,
    kv_left,
    kv_right,
    kv_root_left,
    kv_root_right,
    vector_second,
    query_second,
    value_second,
    up_second,
):
    batch_size = lax.axis_size("batch")
    head_count = lax.axis_size("head")
    batch_index = lax.axis_index("batch")
    head_index = lax.axis_index("head")
    tok_dev, width = tokens.shape
    seq_len = tok_dev * head_count
    row_start = head_index * tok_dev
    head_size = w_key.shape[1]
    slab = w_query.shape[1]
    gain_one = vectors[0]
    shift_one = vectors[1]
    bias_down = vectors[5]

    positions = jnp.arange(seq_len, dtype=jnp.int32)
    documents = jnp.sum((doc_starts[0][None, :] <= positions[:, None]).astype(jnp.int32), axis=1)
    row_ids = row_start + jnp.arange(tok_dev, dtype=jnp.int32)
    row_docs = lax.dynamic_slice_in_dim(documents, row_start, tok_dev, 0)
    allowed = (documents[:, None] == row_docs[None, :]) & (positions[:, None] <= row_ids[None, :])
    mask = jnp.where(allowed, 0.0, MASKED).astype(F32)

    rows_own = tokens.astype(F32)
    normed_one, inverse_one = norm_stats(rows_own)
    normed_in = (normed_one * gain_one + shift_one).astype(BF16)
    w_kv = jnp.concatenate([w_key, w_value], axis=1)
    kv_bias = jnp.concatenate([jnp.zeros_like(bias_value), bias_value])
    kv_own = (matmul(normed_in, w_kv) + kv_bias).astype(BF16)
    kv_all = lax.all_gather(kv_own, "head", axis=0, tiled=True)
    key_rows = kv_all[:, :head_size]
    value_rows = kv_all[:, head_size:]

    w_query_all, w_out_part, bias_all = gather_weights(
        w_query, w_out, bias_query.reshape(1, slab), batch_size, head_count
    )
    w_out_part, cotangent_later = lax.optimization_barrier((w_out_part, cotangent))
    w_out_all = gather_rest(w_out_part, batch_size, head_count)
    cot_all = lax.all_gather(cotangent_later, "head", axis=0, tiled=True)

    queries = (matmul(normed_in, w_query_all) + bias_all.reshape(1, width)).astype(BF16)
    attended, log_totals = attention_forward(queries, key_rows, value_rows.T, mask, head_count)
    resid, mixer_in, normed_two, inverse_wide = project_out(
        attended, w_out_all, tokens, vectors
    )

    mix_part, grad_up, down_shares, grad_mixer_in, grad_up_bias = mixer_pass(
        mixer_in, cot_all, w_up, w_down, bias_up, owner, batch_size, head_count, 2
    )
    mix_one = lax.psum_scatter(mix_part, "head", scatter_dimension=0, tiled=True)

    kv_rows = width // head_count // batch_size
    grad_tokens, query_share, out_share, kv_total, vector_wide, up_bias_total, up_shares = backward_pass(
        owner,
        grad_mixer_in,
        cotangent,
        tokens,
        normed_two,
        inverse_wide,
        vectors,
        queries,
        attended,
        log_totals,
        key_rows,
        key_rows.T,
        value_rows,
        mask.astype(BF16),
        w_query_all,
        w_out_all,
        w_kv,
        grad_up_bias.reshape(8, -1),
        grad_up,
        batch_size,
        head_count,
    )
    kv_total = kv_total.reshape(batch_size * kv_rows, 2 * head_size)
    up_bias_total = up_bias_total.reshape(-1)
    vector_all = vector_wide.transpose(1, 0, 2).reshape(8, width)
    vector_total = vector_all[:6]
    query_bias_total = lax.dynamic_slice_in_dim(vector_all[6], head_index * slab, slab, 0)
    value_bias_total = vector_all[7, :head_size]

    owned_count = attn_left.shape[1]
    owned = lax.dynamic_slice_in_dim(owner, batch_index * owned_count, owned_count, 0)
    mixer_out = shampoo(
        up_shares,
        down_shares,
        w_up,
        w_down,
        owned,
        mixer_left,
        mixer_right,
        mixer_root_left,
        mixer_root_right,
        True,
    )
    attn_out = shampoo(
        query_share,
        out_share,
        w_query,
        w_out,
        owned,
        attn_left,
        attn_right,
        attn_root_left,
        attn_root_right,
        False,
    )
    kv_count = width // head_count

    def kv_tiles(matrix):
        return matrix.reshape(kv_count // TILE, TILE, head_size // TILE, TILE).transpose(0, 2, 1, 3)

    kv_slab = lax.dynamic_slice_in_dim(w_kv, head_index * kv_count, kv_count, 0).astype(F32)
    kv_out = shampoo_update(
        jnp.stack([kv_tiles(kv_total[:, :head_size]), kv_tiles(kv_total[:, head_size:])]),
        kv_left,
        kv_right,
        kv_root_left,
        kv_root_right,
        jnp.stack([kv_tiles(kv_slab[:, :head_size]), kv_tiles(kv_slab[:, head_size:])]),
    )
    _, mix_one = lax.optimization_barrier((kv_total, mix_one))
    output = resid + mix_one.astype(F32) + bias_down
    vec_out = diagonal_update(vector_total, vector_second, vectors)
    query_out = diagonal_update(query_bias_total, query_second, bias_query)
    value_out = diagonal_update(value_bias_total, value_second, bias_value)
    up_out = diagonal_update(up_bias_total, up_second, bias_up)
    return (
        output,
        grad_tokens,
        vec_out[0],
        vec_out[1][2:],
        vec_out[1][:2],
        vec_out[2],
        query_out[0],
        query_out[1],
        query_out[2],
        value_out[0],
        value_out[1],
        value_out[2],
        up_out[0],
        up_out[1],
        up_out[2],
        attn_out[0],
        attn_out[1],
        attn_out[2],
        attn_out[3],
        mixer_out[0],
        mixer_out[1],
        mixer_out[2],
        mixer_out[3],
        kv_out[0],
        kv_out[1],
        kv_out[2],
        kv_out[3],
    )


def solution(mesh):
    rows = P(("batch", "head"), None)
    whole = P()
    head = P("head")
    tiles = P(None, "batch", "head", None, None)
    kv_tiles = P(None, "head", None, None, None)
    in_specs = (
        rows,
        rows,
        P("batch", None),
        whole,
        whole,
        head,
        whole,
        head,
        P(None, "head"),
        whole,
        whole,
        P("head", None),
        P(None, "head"),
        P("head", None),
        *([tiles] * 8),
        *([kv_tiles] * 4),
        whole,
        head,
        whole,
        head,
    )
    out_specs = (
        rows,
        rows,
        *([whole] * 4),
        *([head] * 3),
        *([whole] * 3),
        *([head] * 3),
        *([tiles] * 8),
        *([kv_tiles] * 4),
    )
    return jax.shard_map(body, mesh=mesh, in_specs=in_specs, out_specs=out_specs, check_vma=False)
```

time: 657 us -> 533 us (0.81)
  waiting for transfers between devices: 90.7 us -> 11.6 us
  Pallas kernels: 432 us -> 462 us
  other arithmetic: 34 us -> 12.8 us
  starting transfers between devices: 17.4 us -> 0.12 us
  local copies, waits for them, and re-layouts: 29 us -> 11.8 us
  matrix products: 28.5 us -> 12.2 us
    pallas_call x5 -> x2, Pallas kernels: 85.4 us -> 187 us  [the longest x1 156 us: backward_pass(): pl.pallas_call(kernel, out_shape=(jax.ShapeDtypeStruct((tok, width), F32)...]
    ppermute x14 -> x0, waiting for transfers between devices: 88.9 us -> none  [the longest x6 69.9 us: exchange_batch(): lax.ppermute(lax.dynamic_index_in_dim(chunks, b ^ k, 0, keepdims=False),...]
    pallas_call x1, Pallas kernels: 106 us -> 60.6 us  [gather_weights(): pl.pallas_call(kernel, out_shape=(jax.ShapeDtypeStruct((rows, cols * head...]
    pallas_call x1, Pallas kernels: 176 us -> 148 us  [mixer_pass(): pl.pallas_call(kernel, out_shape=(jax.ShapeDtypeStruct(block + (width,),...]
    ppermute x14 -> x0, starting transfers between devices: 17.2 us -> none  [the longest x6 10.9 us: flush(): lax.ppermute(lax.dynamic_index_in_dim(summed, there, 0, keepdims=False),...]
    dot_general x4 -> x0, matrix products: 15.4 us -> none  [the longest x3 14.9 us: matmul_nt(): lax.dot_general(first_op, second_op, (((1,), (1,)), ((), ())), preferred_...]
    convert_element_type x8 -> x1, other arithmetic: 14.6 us -> 1.87 us  [body(): mask.astype(BF16)]
    all_gather x1, waiting for transfers between devices: 0.01 us -> 11.6 us  [body(): cot_all = lax.all_gather(cotangent_later, 'head', axis=0, tiled=True)]
  transfers between devices with their start and end apart: 19 -> 3, of which waited for: 6 -> 1; matrix products, arithmetic and copies ran while one was open for 12% -> 5% of each run, Pallas kernels for 38% -> 60%
where the time goes in v3:
time: 533 us; the launch traced here: 525 us
  Pallas kernels  462 us (87%)
  between operations  14.6 us (3%)
  other arithmetic  12.8 us (2%)
  matrix products  12.2 us (2%)
  local copies, waits for them, and re-layouts  11.8 us (2%)
  waiting for transfers between devices  11.6 us (2%)
    pallas_call x1, Pallas kernels, backward_pass(): pl.pallas_call(kernel, out_shape=(jax.ShapeDtypeStruct((tok, width), F32)...  156 us
    pallas_call x1, Pallas kernels, mixer_pass(): pl.pallas_call(kernel, out_shape=(jax.ShapeDtypeStruct(block + (width,),...  148 us
    pallas_call x1, Pallas kernels, gather_weights(): pl.pallas_call(kernel, out_shape=(jax.ShapeDtypeStruct((rows, cols * head...  60.6 us
    pallas_call x2, Pallas kernels, shampoo(): pl.pallas_call(kernel, grid_spec=pltpu.PrefetchScalarGridSpec(num_scalar_...  33.2 us
    pallas_call x1, Pallas kernels, gather_rest(): pl.pallas_call(kernel, out_shape=jax.ShapeDtypeStruct(w_all.shape, w_all....  31.3 us
    pallas_call x1, Pallas kernels, attention_forward(): pl.pallas_call(kernel, grid=(slabs,), out_shape=(jax.ShapeDtypeStruct((to...  24 us
    all_gather x1, waiting for transfers between devices, body(): cot_all = lax.all_gather(cotangent_later, 'head', axis=0, tiled=True)  11.6 us
  transfers between devices with their start and end apart: 3, of which 1 were waited for; matrix products, arithmetic and copies ran while one was open for 5% of the time, Pallas kernels for 60%

profile of v3, /device:TPU:0, one launch (start us, length us, event | category | flops | bytes accessed | tf_op | source)
XLA Modules:
  0.0 524.8 jit_solution(8522151536361269259)
XLA Ops:
  7.2 0.0 copy-start
  7.2 0.0 copy-start.4
  7.2 0.0 copy-start.5
  7.2 0.0 all-gather.3.cloned.1.call-start
  7.3 1.0 fusion.41
  8.3 0.0 copy-start.19
  8.3 0.0 copy-start.1
  8.3 1.5 convert_reduce_fusion
  9.9 1.6 fusion.3
  11.5 0.1 constant_dynamic-update-slice_fusion.1
  11.6 0.1 constant_dynamic-update-slice_fusion.wkv_ref
  11.8 0.0 copy-start.6
  11.8 1.2 fusion.17
  13.1 0.0 all-gather.3.cloned.1.call-update
  13.1 0.0 all-gather.5.cloned.1.call-start
  13.1 60.6 %gather_weights.1 = (bf16[2048,2048]{1,0:T(8,128)(2,1)}, bf16[2048,2048]{1,0:T(8,128)(2,1)}, f32[8,1,256]{2,1,0:T(1,128)}) custom-call(bf16[2048,256]{1,0:T(8,128)(2,1)} %refs_2_.2, bf16[256,2048]{1,0:T(8,128)(2,1)} %refs_3_.2, f32[1,256]{1,0:T(1,128)} %bitcast.104), custom_call_target="tpu_custom_call" | custom-call | bytes 125829120 | tf_op jit(solution)/shard_map/gather_weights/pallas_call | solution.py:235
  73.7 0.0 all-gather.5.cloned.1.call-update
  73.8 0.0 reduce-scatter.2.cloned.1.call-start
  73.8 0.0 copy-start.21
  73.8 31.3 %gather_rest.1.w_ref.wo_ref = bf16[2048,2048]{1,0:T(8,128)(2,1)} custom-call(bf16[2048,2048]{1,0:T(8,128)(2,1)} %get-tuple-element.63.in_ref), custom_call_target="tpu_custom_call", output_to_operand_aliasing={{}: (0, {})} | custom-call | bytes 104857600 | tf_op jit(solution)/shard_map/gather_rest/pallas_call | solution.py:277
  105.2 0.0 copy-start.23
  105.2 0.0 copy-done.21
  105.2 0.1 convert_reduce_fusion.1
  105.3 0.1 dynamic_slice.12
  105.4 1.9 fusion.18
  107.2 6.8 %fusion.q_ref = bf16[256,2048]{1,0:T(8,128)(2,1)} fusion(bf16[2048,2048]{1,0:T(8,128)(2,1)} %get-tuple-element.59.wq_ref, f32[2048]{0:T(1024)S(1)} %bitcast.110, bf16[256,2048]{1,0:T(8,128)(2,1)S(1)} %copy-done.1, f32[2048]{0:T(1024)S(1)} %bitcast.101, f32[2048]{0:T(1024)S(1)} %bitcast.103, f32[256]{0:T(256)S(1)} %add_rsqrt_fusion, ...), kind=kOutput, calls=%fused_computation.3 | convolution fusion | flops 2151677952 | bytes 10512384 | tf_op jit(solution)/shard_map/dot_general | solution.py:29
  114.0 2.4 fusion.38
  116.5 1.0 copy.67.v_ref
  117.5 24.0 %attention_forward.1 = (bf16[256,2048]{1,0:T(8,128)(2,1)}, f32[8,2,256]{2,1,0:T(2,128)}) custom-call(bf16[256,2048]{1,0:T(8,128)(2,1)} %fusion.q_ref, bf16[2048,128]{1,0:T(8,128)(2,1)} %get-tuple-element.156.k_ref, bf16[128,2048]{1,0:T(8,128)(2,1)} %copy.67.v_ref, f32[2048,256]{1,0:T(8,128)} %get-tuple-element.167.mask_ref), custom_call_target="tpu_custom_call" | custom-call | flops 8589934592 | bytes 2097152 | tf_op jit(solution)/shard_map/attention_forward/pallas_call | solution.py:724
  141.5 8.8 %project_out.1 = (f32[256,2048]{1,0:T(8,128)}, bf16[256,2048]{1,0:T(8,128)(2,1)}, f32[256,2048]{1,0:T(8,128)}, f32[256,128]{1,0:T(8,128)}) custom-call(bf16[256,2048]{1,0:T(8,128)(2,1)} %get-tuple-element.61.att_ref, bf16[256,2048]{1,0:T(8,128)(2,1)} %tok_ref.3, f32[6,2048]{1,0:T(8,128)} %vec_ref.3, bf16[2048,2048]{1,0:T(8,128)(2,1)} %gather_rest.1.w_ref.wo_ref), custom_call_target="tpu_custom_call" | custom-call | flops 2147483648 | bytes 58720256 | tf_op jit(solution)/shard_map/project_out/pallas_call | solution.py:303
  150.3 11.6 %all-gather.5.cloned.1.call-done = bf16[2048,2048]{1,0:T(8,128)(2,1)} async-done(((bf16[256,2048]{1,0:T(8,128)(2,1)}), bf16[2048,2048]{1,0:T(8,128)(2,1)}) %all-gather.5.cloned.1.call-update) | async-done | bytes 8388624 | tf_op jit(solution)/shard_map/all_gather | solution.py:1499
  161.9 148.2 %mixer_pass.1 = (bf16[4,2,2,128,2048]{4,3,2,1,0:T(8,128)(2,1)}, bf16[4,2,2,128,1024]{4,3,2,1,0:T(8,128)(2,1)}, bf16[4,2,2,128,1024]{4,3,2,1,0:T(8,128)(2,1)}, bf...) custom-call(s32[16]{0:T(128)} %owner_ref.3, ...), custom_call_target="tpu_custom_call" | custom-call | flops 51539607552 | bytes 314572800 | tf_op jit(solution)/shard_map/mixer_pass/pallas_call | solution.py:650
  310.1 0.0 copy-start.24
  310.1 0.0 reduce-scatter.2.cloned.1.call-update
  310.1 0.6 copy-done.24
  310.7 0.6 dynamic_slice.14.ids_ref
  311.4 1.0 copy.68.kt_ref
  312.4 0.6 reduce_sum.39
  313.0 155.6 %backward_pass.1 = (f32[256,2048]{1,0:T(8,128)}, bf16[1,256,512]{2,1,0:T(8,128)(2,1)}, bf16[1,256,512]{2,1,0:T(8,128)(2,1)}, f32[4,64,256]{2,1,0:T(8,128)}, f32[...) custom-call(s32[16]{0:T(128)} %owner_ref.3, f32[256,2048]{1,0:T(8,128)} %bitcast.112, ...), custom_call_target="tpu_custom_call" | custom-call | flops 30064771072 | bytes 209715200 | tf_op jit(solution)/shard_map/backward_pass/pallas_call | solution.py:1240
  468.6 1.5 divide_subtract_fusion
  470.2 0.6 slice.64
  470.8 0.6 slice.65
  471.4 0.8 slice.66
  472.2 0.0 copy-start.12
  472.3 10.3 %shampoo.2 = (f32[2,4,2,128,128]{4,3,2,1,0:T(8,128)}, f32[2,4,2,128,128]{4,3,2,1,0:T(8,128)}, f32[2,4,2,128,128]{4,3,2,1,0:T(8,128)}, f32[2,4,2,128,128]{4,3,2,1,0:T(8,128)}) custom-call(s32[4]{0:T(128)} %dynamic_slice.14.ids_ref, bf16[1,256,512]{2,1,0:T(8,128)(2,1)} %get-tuple-element.79.refs_0_, bf16[1,256,512]{2,1,0:T(8,128)(2,1)} %get-tuple-element.80.refs_1_, ...), custom_call_target="tpu_custom_call" | custom-call | flops 536870912 | bytes 10485760 | tf_op jit(solution)/shard_map/shampoo/pallas_call | solution.py:1387
  482.6 0.0 copy-done.11
  482.6 0.7 fusion.25
  483.3 0.4 fusion.20
  483.7 1.1 fusion.10
  484.9 0.0 copy-start.17
  484.9 0.0 copy-start.18
  484.9 0.0 copy-start.9
  484.9 0.0 copy-start.10
  484.9 0.0 copy-start.2
  484.9 22.8 %shampoo.3 = (f32[2,4,8,128,128]{4,3,2,1,0:T(8,128)}, f32[2,4,8,128,128]{4,3,2,1,0:T(8,128)}, f32[2,4,8,128,128]{4,3,2,1,0:T(8,128)}, f32[2,4,8,128,128]{4,3,2,1,0:T(8,128)}) custom-call(s32[4]{0:T(128)} %dynamic_slice.14.ids_ref, bf16[4,512,1024]{2,1,0:T(8,128)(2,1)} %get-tuple-element.85.refs_0_, bf16[4,512,1024]{2,1,0:T(8,128)(2,1)} %bitcast.81, ...), custom_call_target="tpu_custom_call" | custom-call | flops 2147483648 | bytes 41943040 | tf_op jit(solution)/shard_map/shampoo/pallas_call | solution.py:1387
  507.8 0.7 divide_subtract_fusion.2
  508.4 0.5 divide_subtract_fusion.3
  509.0 0.6 divide_subtract_fusion.1
  509.6 1.3 fusion.16
  510.9 1.4 fusion.13
  512.3 3.0 add_add_fusion
  515.3 1.3 copy.82
  516.6 0.6 copy.83
  517.3 0.6 copy.84
  (41 shorter events, 0.1 us)
Async XLA Ops:
  7.2 476.1 %copy-start = (f32[2,2,1,128,128]{4,3,2,1,0:T(8,128)S(1)}, f32[2,2,1,128,128]{4,3,2,1,0:T(8,128)}, u32[]{:S(2)}) copy-start(f32[2,2,1,128,128]{4,3,2,1,0:T(8,128)} %param.54) | copy-start | bytes 786436
  7.2 4.3 copy-start.4
  7.2 4.4 copy-start.5
  7.2 106.8 %all-gather.3.cloned.1.call-start = ((), (), s32[]{:S(2)}) async-start(), calls=%async_computation.1 | async-start | bytes 1179648 | tf_op jit(solution)/shard_map/all_gather | solution.py:1490
  8.3 3.5 copy-start.19
  8.3 3.5 copy-start.1
  11.8 299.5 %copy-start.6 = (bf16[2048,256]{1,0:T(8,128)(2,1)}, bf16[2048,256]{1,0:T(8,128)(2,1)S(1)}, u32[]{:S(2)}) copy-start(bf16[2048,256]{1,0:T(8,128)(2,1)S(1)} %constant_dynamic-update-slice_fusion.wkv_ref) | copy-start | bytes 3145732
  13.1 148.8 %all-gather.5.cloned.1.call-start = ((), (), s32[]{:S(2)}) async-start(), calls=%async_computation.2 | async-start | bytes 9437184 | tf_op jit(solution)/shard_map/all_gather | solution.py:1499
  73.8 438.5 %reduce-scatter.2.cloned.1.call-start = ((), (), s32[]{:S(2)}) async-start(), calls=%async_computation.3 | async-start | bytes 9437184 | tf_op jit(solution)/shard_map/reduce_scatter | solution.py:1510
  73.8 31.4 %copy-start.21 = (s32[1,4]{1,0:T(1,128)S(1)}, s32[1,4]{1,0:T(1,128)}, u32[]{:S(2)}) copy-start(s32[1,4]{1,0:T(1,128)} %param.32) | copy-start | bytes 52
  105.2 2.1 copy-start.23
  310.1 0.7 copy-start.24
  310.1 2.3 copy-start.14
  313.0 155.6 %copy-start.7 = (f32[6,2048]{1,0:T(8,128)S(1)}, f32[6,2048]{1,0:T(8,128)}, u32[]{:S(2)}) copy-start(f32[6,2048]{1,0:T(8,128)} %vec_ref.3) | copy-start | bytes 147460
  313.0 155.6 %copy-start.13 = (f32[6,2048]{1,0:T(8,128)S(1)}, f32[6,2048]{1,0:T(8,128)}, u32[]{:S(2)}) copy-start(f32[6,2048]{1,0:T(8,128)} %param.56) | copy-start | bytes 147460
  472.2 10.4 %copy-start.11 = (f32[4,64,256]{2,1,0:T(8,128)S(1)}, f32[4,64,256]{2,1,0:T(8,128)}, u32[]{:S(2)}) copy-start(f32[4,64,256]{2,1,0:T(8,128)} %get-tuple-element.73) | copy-start | bytes 786436
  472.2 11.5 %copy-start.12 = (f32[2,2,1,128,128]{4,3,2,1,0:T(8,128)S(1)}, f32[2,2,1,128,128]{4,3,2,1,0:T(8,128)}, u32[]{:S(2)}) copy-start(f32[2,2,1,128,128]{4,3,2,1,0:T(8,128)} %param.55) | copy-start | bytes 786436
  484.9 22.9 %copy-start.16 = (f32[256]{0:T(256)S(1)}, f32[256]{0:T(256)}, u32[]{:S(2)}) copy-start(f32[256]{0:T(256)} %param.35) | copy-start | bytes 3076
  484.9 22.9 %copy-start.20 = (f32[256]{0:T(256)S(1)}, f32[256]{0:T(256)}, u32[]{:S(2)}) copy-start(f32[256]{0:T(256)} %param.57) | copy-start | bytes 3076
  484.9 23.6 %copy-start.8 = (f32[8,8,256]{2,1,0:T(8,128)S(1)}, f32[8,8,256]{2,1,0:T(8,128)}, u32[]{:S(2)}) copy-start(f32[8,8,256]{2,1,0:T(8,128)} %get-tuple-element.77) | copy-start | bytes 196612
  484.9 23.6 %copy-start.22 = (f32[128]{0:T(128)S(1)}, f32[128]{0:T(128)}, u32[]{:S(2)}) copy-start(f32[128]{0:T(128)} %param.58) | copy-start | bytes 1540
  484.9 24.1 %copy-start.15 = (f32[8,128]{1,0:T(8,128)S(1)}, f32[8,128]{1,0:T(8,128)}, u32[]{:S(2)}) copy-start(f32[8,128]{1,0:T(8,128)} %get-tuple-element.78) | copy-start | bytes 12292
  484.9 24.1 %copy-start.17 = (f32[1024]{0:T(1024)S(1)}, f32[1024]{0:T(1024)}, u32[]{:S(2)}) copy-start(f32[1024]{0:T(1024)} %param.37) | copy-start | bytes 12292
  484.9 24.1 %copy-start.18 = (f32[1024]{0:T(1024)S(1)}, f32[1024]{0:T(1024)}, u32[]{:S(2)}) copy-start(f32[1024]{0:T(1024)} %param.59) | copy-start | bytes 12292
  484.9 24.7 %copy-start.9 = (f32[2,2,1,128,128]{4,3,2,1,0:T(8,128)S(1)}, f32[2,2,1,128,128]{4,3,2,1,0:T(8,128)}, u32[]{:S(2)}) copy-start(f32[2,2,1,128,128]{4,3,2,1,0:T(8,128)} %param.53) | copy-start | bytes 786436
  484.9 26.0 %copy-start.10 = (f32[2,2,1,128,128]{4,3,2,1,0:T(8,128)S(1)}, f32[2,2,1,128,128]{4,3,2,1,0:T(8,128)}, u32[]{:S(2)}) copy-start(f32[2,2,1,128,128]{4,3,2,1,0:T(8,128)} %param.52) | copy-start | bytes 786436
  484.9 27.4 %copy-start.2 = (f32[256,2048]{1,0:T(8,128)S(1)}, f32[256,2048]{1,0:T(8,128)}, u32[]{:S(2)}) copy-start(f32[256,2048]{1,0:T(8,128)} %get-tuple-element.64) | copy-start | bytes 6291460
  512.3 3.0 copy-start.3
Sparse Core Ops, SparseCore 0:
  13.2 34.2 all-gather.2
  73.9 87.9 all-gather.4
  310.2 121.0 reduce-scatter.1

commit v4 on v3

--- a/solution.py
+++ b/solution.py
@@ -74,20 +74,14 @@
     z = h // 2
     c = h % 2
 
-    def at_chip(r):
-        return {"head": lax.rem(z + r, chips) * 2 + c}
-
-    def other(d):
-        return {"head": lax.rem(h + d, head_count)}
+    def at(chip):
+        return {"head": chip * 2 + c}
 
     def peer(k):
         return {"batch": b ^ k}
 
-    def source(r):
-        return lax.rem(z - r + chips, chips) * 2 + c
-
     def remote(src, dst, send, recv, target):
-        copy = pltpu.make_async_remote_copy(
+        return pltpu.make_async_remote_copy(
             src_ref=src,
             dst_ref=dst,
             send_sem=send,
@@ -95,54 +89,68 @@
             device_id=target,
             device_id_type=MESH,
         )
-        copy.start()
-        return copy
-
-    return b, h, {"head": h + 1 - 2 * c}, at_chip, other, peer, source, remote
-
-
-def plane_exchange(place, tools, sems, batch_size, chips):
-    b, _, sibling, _, _, peer, source, remote = tools
+
+    others = [lax.rem(z + i, chips) for i in range(1, chips)]
+    return b, h, z, c, {"head": h + 1 - 2 * c}, at, peer, remote, others
+
+
+def plane_exchange(place, tools, sems, batch_size):
+    b, _, _, _, sibling, _, peer, remote, others = tools
     xs, xr, fs, fr, cs, cr = sems
     ring = batch_size == 4
     direct = (1, 2) if ring else tuple(range(1, batch_size))
-    hops = {}
-
-    def start(r):
-        spot = place(b, source(r))
+
+    def hop(k, chip):
+        spot = place(b, chip)
+        return remote(spot, spot, xs.at[k, chip], xr.at[k, chip], peer(k))
+
+    def half(k, chip):
+        spot = place(b ^ k, chip, k - 1)
+        return remote(spot, spot, fs.at[k, chip], fr.at[k, chip], peer(3 - k))
+
+    def side(k, chip):
+        spot = place(b ^ k, chip)
+        return remote(spot, spot, cs.at[k, chip], cr.at[k, chip], sibling)
+
+    def start(chip):
         for k in direct:
-            hops[k, r] = remote(spot, spot, xs.at[k, r], xr.at[k, r], peer(k))
+            hop(k, chip).start()
+        side(0, chip).start()
+
+    def turn():
+        for chip in others:
+            for k in direct:
+                hop(k, chip).wait_recv()
+                if ring:
+                    half(k, chip).start()
+                side(k, chip).start()
+
+    def close():
+        if ring:
+            for chip in others:
+                for k in direct:
+                    half(k, chip).wait_recv()
+                side(3, chip).start()
 
     def finish():
-        halves = {}
-        sent = list(hops.values())
-        received = []
-        for r in range(1, chips):
+        for chip in others:
+            for k in range(batch_size):
+                side(k, chip).wait()
             for k in direct:
-                hops[k, r].wait_recv()
+                hop(k, chip).wait_send()
                 if ring:
-                    spot = place(b ^ k, source(r), k - 1)
-                    halves[k, r] = remote(spot, spot, fs.at[k, r], fr.at[k, r], peer(3 - k))
-                spot = place(b ^ k, source(r))
-                received.append(remote(spot, spot, cs.at[k, r], cr.at[k, r], sibling))
-        if ring:
-            for r in range(1, chips):
-                for k in direct:
-                    halves[k, r].wait_recv()
-                spot = place(b ^ 3, source(r))
-                received.append(remote(spot, spot, cs.at[3, r], cr.at[3, r], sibling))
-        return received, sent + received + list(halves.values())
-
-    return start, finish
-
-
-def place_rows(w_all, rows, batch_size):
-    def place(quarter, head, half=None):
+                    half(k, chip).wait_send()
+
+    return start, turn, close, finish
+
+
+def place_rows(w_all, rows, core, batch_size):
+    def place(quarter, chip, half=None):
         part = rows // batch_size
         if half is not None:
             part = part // 2
             quarter = quarter * 2 + half
-        return w_all.at[lanes(head * rows + quarter * part, part, part), :]
+        return w_all.at[lanes((chip * 2 + core) * rows + quarter * part, part, part), :]
 
     return place
 
@@ -152,20 +160,26 @@
     chips = head_count // 2
 
     def kernel(
-        q_ref, w_ref, bias_ref, q_all, w_all, bias_all, loc, zs, zr, ys, yr, xs, xr, fs, fr, cs, cr,
-        bs, br,
+        q_ref, w_ref, bias_ref, q_all, w_all, bias_all, loc, right, left, line, ys, yr, sides_s,
+        sides_r, xs, xr, fs, fr, cs, cr, bs, br,
     ):
         tools = gather_tools(batch_size, head_count)
-        b, h, sibling, at_chip, other, peer, source, remote = tools
-
-        def place_query(quarter, head, half=None):
+        b, h, z, c, sibling, at, peer, remote, others = tools
+        has_left = z > 0
+        has_right = z < chips - 1
+
+        def other(d):
+            return {"head": lax.rem(h + d, head_count)}
+
+        def place_query(quarter, chip, half=None):
             part = rows // batch_size
             if half is not None:
                 part = part // 2
                 quarter = quarter * 2 + half
+            head = chip * 2 + c
             return q_all.at[lanes(quarter * part, part, part), lanes(head * cols, cols, cols)]
 
-        place_out = place_rows(w_all, cols, batch_size)
+        places = (place_query, place_rows(w_all, cols, c, batch_size))
         greet([other(d) for d in range(1, head_count)] + [peer(k) for k in range(1, batch_size)])
         own = (q_all.at[:, lanes(h * cols, cols, cols)], w_all.at[lanes(h * cols, cols, cols), :])
         q_part, w_part = rows // batch_size, cols // batch_size
@@ -173,61 +187,100 @@
             q_ref.at[lanes(b * q_part, q_part, q_part), :],
             w_ref.at[lanes(b * w_part, w_part, w_part), :],
         )
-        sent = []
-        received = []
-
-        def z_start(m, place):
-            copies = [
-                remote(mine[m], place(b, h), zs.at[m, r], zr.at[m, r], at_chip(r))
-                for r in range(1, chips)
-            ]
-            sent.extend(copies)
-            return copies
-
-        z_query = z_start(0, place_query)
-        locals_ = []
-        for m, src in enumerate((q_ref, w_ref)):
-            local = pltpu.make_async_copy(src, own[m], loc.at[m])
-            local.start()
-            locals_.append(local)
-            last = remote(src, own[m], ys.at[m, 0], yr.at[m, 0], sibling)
-            sent.append(last)
-            received.append(last)
-        for d in range(1, head_count):
-            copy = remote(bias_ref, bias_all.at[h], bs.at[d], br.at[d], other(d))
-            sent.append(copy)
-            received.append(copy)
+
+        def z_copy(m, chip, to_right, src=None):
+            spot = places[m](b, chip)
+            src = spot if src is None else src
+            if to_right:
+                return remote(src, spot, right.at[m, chip], line.at[m, chip], at(z + 1))
+            return remote(src, spot, left.at[m, chip], line.at[m, chip], at(z - 1))
+
+        def z_first(m):
+            @pl.when(has_right)
+            def _():
+                z_copy(m, z, True, mine[m]).start()
+
+            @pl.when(has_left)
+            def _():
+                z_copy(m, z, False, mine[m]).start()
+
+        def z_steps(m, d, then):
+            @pl.when(z >= d)
+            def _():
+                z_copy(m, z - d, True).wait_recv()
+
+                @pl.when(has_right)
+                def _():
+                    z_copy(m, z - d, True).start()
+
+                then(z - d)
+
+            @pl.when(z + d < chips)
+            def _():
+                z_copy(m, z + d, False).wait_recv()
+
+                @pl.when(has_left)
+                def _():
+                    z_copy(m, z + d, False).start()
+
+                then(z + d)
+
+        z_first(0)
+        locals_ = [
+            pltpu.make_async_copy(src, own[m], loc.at[m]) for m, src in enumerate((q_ref, w_ref))
+        ]
+        slices = [
+            remote(src, own[m], ys.at[m], yr.at[m], sibling) for m, src in enumerate((q_ref, w_ref))
+        ]
+        biases = [
+            remote(bias_ref, bias_all.at[h], bs.at[d], br.at[d], other(d))
+            for d in range(1, head_count)
+        ]
         bias_own = pltpu.make_async_copy(bias_ref, bias_all.at[h], bs.at[0])
-        bias_own.start()
-
-        start, finish = plane_exchange(
-            place_query, tools, (xs, xr, fs, fr, cs, cr), batch_size, chips
+        for copy in locals_ + slices + biases + [bias_own]:
+            copy.start()
+
+        start, turn, close, finish = plane_exchange(
+            place_query, tools, (xs, xr, fs, fr, cs, cr), batch_size
         )
 
-        def across(m, place, r):
-            spot = place(b, source(r))
-            copy = remote(spot, spot, ys.at[m, r], yr.at[m, r], sibling)
-            sent.append(copy)
-            received.append(copy)
-
-        for r in range(1, chips):
-            z_query[r - 1].wait_recv()
-            start(r)
-            across(0, place_query, r)
-        z_out = z_start(1, place_out)
-        more_received, more_sent = finish()
-        received.extend(more_received)
-        sent.extend(more_sent)
-        for r in range(1, chips):
-            z_out[r - 1].wait_recv()
-            across(1, place_out, r)
-        for copy in received:
-            copy.wait_recv()
-        for copy in sent:
-            copy.wait_send()
-        for local in locals_:
-            local.wait()
-        bias_own.wait()
+        def side(chip):
+            spot = places[1](b, chip)
+            return remote(spot, spot, sides_s.at[chip], sides_r.at[chip], sibling)
+
+        for d in range(1, chips):
+            z_steps(0, d, start)
+            if d == 1:
+                z_first(1)
+        turn()
+        for d in range(1, chips):
+            z_steps(1, d, lambda chip: side(chip).start())
+        close()
+        finish()
+        for chip in others:
+            side(chip).wait()
+        for m in range(2):
+
+            @pl.when(has_right)
+            def _():
+                z_copy(m, z, True, mine[m]).wait_send()
+
+            @pl.when(has_left)
+            def _():
+                z_copy(m, z, False, mine[m]).wait_send()
+
+            for d in range(1, chips):
+
+                @pl.when((z >= d) & has_right)
+                def _():
+                    z_copy(m, z - d, True).wait_send()
+
+                @pl.when((z + d < chips) & has_left)
+                def _():
+                    z_copy(m, z + d, False).wait_send()
+
+        for copy in locals_ + slices + biases + [bias_own]:
+            copy.wait()
 
     dma = pltpu.SemaphoreType.DMA
     hop = dma((batch_size, chips))
@@ -242,8 +295,8 @@
         in_specs=[WHOLE] * 3,
         out_specs=(ANY,) * 3,
         scratch_shapes=[
-            dma((2,)), two, two, two, two, hop, hop, hop, hop, hop, hop,
-            dma((head_count,)), dma((head_count,)),
+            dma((2,)), two, two, two, dma((2,)), dma((2,)), dma((chips,)), dma((chips,)),
+            hop, hop, hop, hop, hop, hop, dma((head_count,)), dma((head_count,)),
         ],
         compiler_params=pltpu.CompilerParams(collective_id=0, has_side_effects=True),
         cost_estimate=pl.CostEstimate(
@@ -253,40 +306,71 @@
     )(w_query, w_out, bias_local)
 
 
-def gather_rest(w_all, batch_size, head_count):
+def gather_rest(w_all, kv_own, batch_size, head_count):
     chips = head_count // 2
     rows = w_all.shape[0] // head_count
-
-    def kernel(in_ref, w_ref, xs, xr, fs, fr, cs, cr):
+    tok, kv_cols = kv_own.shape
+
+    def kernel(
+        in_ref, kv_ref, w_ref, kv_all, xs, xr, fs, fr, cs, cr, own_sem, zs, zr, ss, sr
+    ):
         del in_ref
         tools = gather_tools(batch_size, head_count)
-        _, _, sibling, _, _, peer, _, _ = tools
-        greet([sibling] + [peer(k) for k in range(1, batch_size)])
-        start, finish = plane_exchange(
-            place_rows(w_ref, rows, batch_size), tools, (xs, xr, fs, fr, cs, cr), batch_size, chips
+        _, h, z, c, sibling, at, peer, remote, others = tools
+        greet([sibling] + [at(chip) for chip in others] + [peer(k) for k in range(1, batch_size)])
+
+        def place(chip):
+            return kv_all.at[lanes((chip * 2 + c) * tok, tok, tok), :]
+
+        own = pltpu.make_async_copy(kv_ref, place(z), own_sem)
+        own.start()
+
+        def away(i):
+            return remote(kv_ref, place(z), zs.at[i], zr.at[i], at(others[i]))
+
+        def side(chip):
+            src = kv_ref if chip is z else place(chip)
+            return remote(src, place(chip), ss.at[chip], sr.at[chip], sibling)
+
+        for i in range(chips - 1):
+            away(i).start()
+        side(z).start()
+        start, turn, close, finish = plane_exchange(
+            place_rows(w_ref, rows, c, batch_size), tools, (xs, xr, fs, fr, cs, cr), batch_size
         )
-        for r in range(1, chips):
-            start(r)
-        received, sent = finish()
-        for copy in received:
-            copy.wait_recv()
-        for copy in sent:
-            copy.wait_send()
-
-    hop = pltpu.SemaphoreType.DMA((batch_size, chips))
+        for chip in others:
+            start(chip)
+        turn()
+        for i in range(chips - 1):
+            away(i).wait_recv()
+            side(others[chips - 2 - i]).start()
+        close()
+        finish()
+        side(z).wait()
+        for i in range(chips - 1):
+            side(others[i]).wait()
+            away(i).wait_send()
+        own.wait()
+
+    dma = pltpu.SemaphoreType.DMA
+    hop = dma((batch_size, chips))
+    line = dma((chips,))
     return pl.pallas_call(
         kernel,
-        out_shape=jax.ShapeDtypeStruct(w_all.shape, w_all.dtype),
-        in_specs=[ANY],
-        out_specs=ANY,
-        scratch_shapes=[hop] * 6,
+        out_shape=(
+            jax.ShapeDtypeStruct(w_all.shape, w_all.dtype),
+            jax.ShapeDtypeStruct((head_count * tok, kv_cols), kv_own.dtype),
+        ),
+        in_specs=[ANY, WHOLE],
+        out_specs=(ANY, ANY),
+        scratch_shapes=[hop] * 6 + [dma, line, line, line, line],
         input_output_aliases={0: 0},
         compiler_params=pltpu.CompilerParams(collective_id=5, has_side_effects=True),
         cost_estimate=pl.CostEstimate(
             flops=0, bytes_accessed=100 * 1024 * 1024, transcendentals=0
         ),
         name="gather_rest",
-    )(w_all)
+    )(w_all, kv_own)
 
 
 def project_out(attended, weight, tokens, vectors):
@@ -327,16 +411,20 @@
     tiles = width // TILE
     owned = tiles // batch_size
     total_events = n * cuts
+    pieces = 2
+    piece = sub // pieces
 
     def kernel(
         owner_ref, x_ref, cot_ref, up_ref, down_ref, bias_ref,
-        all_ref, hid_ref, pre_ref, mix_ref, grad_up_ref, down_ref_all, out_ref, sum_ref,
+        all_ref, hid_ref, pre_ref, mix_a_ref, mix_b_ref, grad_up_ref, down_ref_all, out_ref,
+        sum_ref,
         x_buf, cot_buf, hid_buf, pre_buf, mine, give, pair_in, chain_in, right_in,
         up_acc, down_acc, stage, grad_down_ref,
         own_sem, x_sem, cot_sem, hid_sem, pre_sem, mix_sem,
         right_send, left_send, side_send, side_recv, line_recv,
         pair_send, pair_recv, chain_send, chain_recv, last_recv, down_send, down_recv, down_sem,
     ):
+        mix_refs = (mix_a_ref, mix_b_ref)
         h = lax.axis_index("head")
         z = h // 2
         c = h % 2
@@ -368,16 +456,18 @@
                 pair_recv.at[chip, g], sibling,
             )
 
-        def chain_copy(chip, g, target):
+        def chain_copy(chip, g, e, target):
+            part = pl.ds(e * piece, piece)
             return remote(
-                mine.at[chip, g], chain_in.at[chip, g], chain_send.at[chip, g],
-                chain_recv.at[chip, g], at(target),
+                mine.at[chip, g, part], chain_in.at[chip, g, part], chain_send.at[chip, g, e],
+                chain_recv.at[chip, g, e], at(target),
             )
 
-        def last_copy(chip, g):
+        def last_copy(chip, g, e):
+            part = pl.ds(e * piece, piece)
             return remote(
-                mine.at[chip, g], right_in.at[g], chain_send.at[chip, g], last_recv.at[g],
-                at(z - 1),
+                mine.at[chip, g, part], right_in.at[g, part], chain_send.at[chip, g, e],
+                last_recv.at[g, e], at(z - 1),
             )
 
         b = lax.axis_index("batch")
@@ -494,27 +584,33 @@
             loads[0].wait()
             hidden = hid_buf[...].reshape(2 * sub, hid)
             stage[...] = matmul(hidden, down_ref[...]).astype(BF16).reshape(2, sub, width)
-            mix_store = pltpu.make_async_copy(stage, mix_ref.at[chip, :, g], mix_sem)
-            mix_store.start()
+            for cut in range(cuts):
+
+                @pl.when(g == cut)
+                def _():
+                    pltpu.make_async_copy(stage, mix_refs[cut].at[chip], mix_sem).start()
+
             loads[1].wait()
             loads[2].wait()
             up_acc[...] += matmul_t(
                 x_buf[...].reshape(2 * sub, width), pre_buf[...].reshape(2 * sub, hid)
             ).reshape(tiles, TILE, hid)
-            mix_store.wait()
-
-        def add_up(chip, g, more):
-            pair_copy(chip, g).wait_recv()
-            total = mine[chip, g].astype(F32) + pair_in[chip, g].astype(F32)
+            pltpu.make_async_copy(stage, mix_refs[0].at[chip], mix_sem).wait()
+
+        def add_up(chip, g, e, more):
+            part = pl.ds(e * piece, piece)
+            total = mine[chip, g, part, :].astype(F32) + pair_in[chip, g, part, :].astype(F32)
 
             @pl.when(more)
             def _():
-                chain_copy(chip, g, z).wait_recv()
-                mine[chip, g] = (total + chain_in[chip, g].astype(F32)).astype(BF16)
+                chain_copy(chip, g, e, z).wait_recv()
+                mine[chip, g, part, :] = (
+                    total + chain_in[chip, g, part, :].astype(F32)
+                ).astype(BF16)
 
             @pl.when(jnp.logical_not(more))
             def _():
-                mine[chip, g] = total.astype(BF16)
+                mine[chip, g, part, :] = total.astype(BF16)
 
         def step(t, carry):
             d = t // cuts
@@ -558,8 +654,10 @@
 
             @pl.when((t >= z) & (chip_right > z) & (chip_right < n))
             def _():
-                add_up(chip_right, g_right, has_left)
-                chain_copy(chip_right, g_right, z + 1).start()
+                pair_copy(chip_right, g_right).wait_recv()
+                for e in range(pieces):
+                    add_up(chip_right, g_right, e, has_left)
+                    chain_copy(chip_right, g_right, e, z + 1).start()
 
             from_right = jnp.maximum(t - (n - 1 - z), 0)
             chip_left = n - 1 - from_right // cuts
@@ -567,15 +665,17 @@
 
             @pl.when((t >= n - 1 - z) & (chip_left < z) & (chip_left >= 0))
             def _():
-                add_up(chip_left, g_left, has_right)
-
-                @pl.when(chip_left == z - 1)
-                def _():
-                    last_copy(chip_left, g_left).start()
-
-                @pl.when(chip_left < z - 1)
-                def _():
-                    chain_copy(chip_left, g_left, z - 1).start()
+                pair_copy(chip_left, g_left).wait_recv()
+                for e in range(pieces):
+                    add_up(chip_left, g_left, e, has_right)
+
+                    @pl.when(chip_left == z - 1)
+                    def _():
+                        last_copy(chip_left, g_left, e).start()
+
+                    @pl.when(chip_left < z - 1)
+                    def _():
+                        chain_copy(chip_left, g_left, e, z - 1).start()
 
             events = (z >= d).astype(jnp.int32) + (z + d < n).astype(jnp.int32)
             events = jnp.where((d == 0) | (d >= n), 1, events)
@@ -610,12 +710,14 @@
 
             @pl.when(has_left)
             def _():
-                chain_copy(z, g, z).wait_recv()
+                for e in range(pieces):
+                    chain_copy(z, g, e, z).wait_recv()
                 out_ref[g] += chain_in[z, g].astype(F32)
 
             @pl.when(has_right)
             def _():
-                last_copy(z, g).wait_recv()
+                for e in range(pieces):
+                    last_copy(z, g, e).wait_recv()
                 out_ref[g] += right_in[g].astype(F32)
 
         def finish(chip, carry):
@@ -634,7 +736,8 @@
 
                 @pl.when(chip != z)
                 def _():
-                    chain_copy(chip, g, z).wait_send()
+                    for e in range(pieces):
+                        chain_copy(chip, g, e, z).wait_send()
 
             return carry
 
@@ -653,14 +756,15 @@
             jax.ShapeDtypeStruct(block + (width,), BF16),
             jax.ShapeDtypeStruct(block + (hid,), BF16),
             jax.ShapeDtypeStruct(block + (hid,), BF16),
-            jax.ShapeDtypeStruct(block + (width,), BF16),
+            jax.ShapeDtypeStruct((n, 2, sub, width), BF16),
+            jax.ShapeDtypeStruct((n, 2, sub, width), BF16),
             jax.ShapeDtypeStruct((tiles, TILE, hid), BF16),
             jax.ShapeDtypeStruct((batch_size, owned, TILE, hid), BF16),
             jax.ShapeDtypeStruct((cuts, sub, width), F32),
             jax.ShapeDtypeStruct((8, hid), F32),
         ),
         in_specs=[pl.BlockSpec(memory_space=pltpu.SMEM), WHOLE, ANY, WHOLE, WHOLE, WHOLE],
-        out_specs=(ANY, ANY, ANY, ANY, WHOLE, ANY, WHOLE, WHOLE),
+        out_specs=(ANY, ANY, ANY, ANY, ANY, WHOLE, ANY, WHOLE, WHOLE),
         scratch_shapes=[
             vm((2, sub, width), BF16),
             vm((2, sub, width), BF16),
@@ -674,8 +778,8 @@
             vm((tiles, TILE, hid), BF16),
             dma, dma, dma, dma, dma, dma,
             each, each, each, each, each,
-            each, each, each, each,
-            dma((cuts,)),
+            each, each, dma((n, cuts, pieces)), dma((n, cuts, pieces)),
+            dma((cuts, pieces)),
             dma((batch_size,)), dma((batch_size,)), dma,
         ],
         compiler_params=pltpu.CompilerParams(
@@ -693,9 +797,10 @@
         w_down,
         bias_up.reshape(1, hid),
     )
-    _, _, _, mix_part, grad_up, grad_down, grad_in, bias_sum = outs
+    _, _, _, mix_a, mix_b, grad_up, grad_down, grad_in, bias_sum = outs
     return (
-        mix_part.reshape(2 * n * tok, width),
+        mix_a.reshape(2 * n * sub, width),
+        mix_b.reshape(2 * n * sub, width),
         grad_up.reshape(batch_size, owned * TILE, hid),
         grad_down.reshape(batch_size, owned * TILE, hid),
         grad_in.reshape(tok, width),
@@ -751,7 +856,7 @@
 def backward_pass(
     owner, grad_mixer, cotangent, tokens, normed_two, inverse_two, vectors, queries, attended,
     log_totals, key_rows, key_turned, value_rows, mask, w_query_all, w_out_all, w_kv, up_parts,
-    grad_up, batch_size, head_count,
+    batch_size, head_count,
 ):
     tok, width = tokens.shape
     seq_len, head_size = key_rows.shape
@@ -760,7 +865,6 @@
     n = head_count // 2
     tiles = width // TILE
     cols_out = width // batch_size
-    owned = tiles // batch_size
     half_rows = slab // 2
     kv_cols = 2 * head_size
     kv_rows = width // head_count // batch_size
@@ -771,8 +875,8 @@
 
     def kernel(
         owner_ref, gm_ref, cot_ref, tok_ref, n2_ref, i2_ref, vec_ref, q_ref, att_ref, log_ref,
-        k_ref, kt_ref, v_ref, mask_ref, wq_ref, wo_ref, wkv_ref, up_ref, gu_ref,
-        tokens_out, query_out, out_out, kv_out, vec_out, up_out, gu_out,
+        k_ref, kt_ref, v_ref, mask_ref, wq_ref, wo_ref, wkv_ref, up_ref,
+        tokens_out, query_out, out_out, kv_out, vec_out, up_out,
         branch, wide_tiles, normed_owned, branch_owned, grad_in, wq_buf, wo_buf, dk, dv,
         give, mine, pair_in, land, hop, z_land,
         dkv, dkv_pair, dkv_here, dkv_land,
@@ -781,7 +885,7 @@
         gm_sem, n2_sem, cot_sem, free_sem, wq_sem, wo_sem, pair_send, pair_recv, hop_send, hop_recv, land_send, land_recv,
         z_send, z_recv, dkv_s, dkv_r, dkz_s, dkz_r,
         s_pair, r_pair, s_kvb, r_kvb, s_kvz, r_kvz, s_kva, r_kva,
-        s_vh, r_vh, s_vb, r_vb, s_va, r_va, s_up, r_up, gu_send, gu_recv, gu_sem,
+        s_vh, r_vh, s_vb, r_vb, s_va, r_va, s_up, r_up,
     ):
         b = lax.axis_index("batch")
         h = lax.axis_index("head")
@@ -811,22 +915,6 @@
             for k in range(1, batch_size)
         ]
         for copy in up_copies:
-            copy.start()
-
-        gu_own = pltpu.make_async_copy(gu_ref.at[b], gu_out.at[0], gu_sem)
-        gu_own.start()
-
-        def gu_copies(p):
-            part = pl.ds(p * TILE, TILE)
-            return [
-                remote(
-                    gu_ref.at[b ^ k, part], gu_out.at[k, part], gu_send.at[k, p], gu_recv.at[k, p],
-                    peer(k),
-                )
-                for k in range(1, batch_size)
-            ]
-
-        for copy in gu_copies(0):
             copy.start()
 
         def slab_at(s):
@@ -1093,9 +1181,6 @@
         normed_one, inverse_one = norm_stats(tok_ref[...].astype(F32))
         normed_in = (normed_one * vec_ref[0:1, :] + vec_ref[1:2, :]).astype(BF16)
         plane_hop(2 * n - 1)
-        for p in range(1, owned):
-            for copy in gu_copies(p):
-                copy.start()
         grad_kv = dkv_here[z].astype(F32)
         for copy in dkv_copies:
             copy.wait_recv()
@@ -1210,10 +1295,6 @@
             copy.wait_send()
         pair_copy(2 * n - 2).wait_send()
         pair_copy(2 * n - 1).wait_send()
-        for p in range(owned):
-            for copy in gu_copies(p):
-                copy.wait()
-        gu_own.wait()
 
         def finish(q, carry):
             @pl.when(q % n < n - 1)
@@ -1246,12 +1327,11 @@
             jax.ShapeDtypeStruct((nb, kv_rows, kv_cols), F32),
             jax.ShapeDtypeStruct((nh, 8, slab), F32),
             jax.ShapeDtypeStruct(up_parts.shape, F32),
-            jax.ShapeDtypeStruct(grad_up.shape, grad_up.dtype),
         ),
         in_specs=[pl.BlockSpec(memory_space=pltpu.SMEM), ANY, ANY, WHOLE, ANY]
         + [WHOLE] * 9
-        + [ANY, ANY, WHOLE, WHOLE, ANY],
-        out_specs=(WHOLE,) * 6 + (ANY,),
+        + [ANY, ANY, WHOLE, WHOLE],
+        out_specs=(WHOLE,) * 6,
         scratch_shapes=[
             vm((tok, width), BF16),
             vm((tiles, tok, TILE), BF16),
@@ -1288,7 +1368,7 @@
             dma((2 * n, nb, 2)), dma((2 * n, nb, 2)), dma((2 * n,)), dma((2 * n,)), dma, dma, dma((n,)), dma((n,)),
             dma, dma, dma((nb,)), dma((nb,)), dma((n,)), dma((n,)), dma((nb,)), dma((nb,)),
             dma((nh,)), dma((nh,)), dma((nb,)), dma((nb,)), dma((nh,)), dma((nh,)),
-            dma((nb,)), dma((nb,)), dma((nb, owned)), dma((nb, owned)), dma,
+            dma((nb,)), dma((nb,)),
         ],
         compiler_params=pltpu.CompilerParams(
             collective_id=4, has_side_effects=True, vmem_limit_bytes=VMEM_LIMIT + 2 * 1024 * 1024
@@ -1302,7 +1382,6 @@
     )(
         owner, grad_mixer, cotangent, tokens, normed_two, inverse_two, vectors, queries, attended,
         log_totals, key_rows, key_turned, value_rows, mask, w_query_all, w_out_all, w_kv, up_parts,
-        grad_up,
     )
 
 
@@ -1322,39 +1401,43 @@
 
 
 def shampoo(
-    first, second, first_weight, second_weight, owned, left, right, root_left, root_right, wide_rows
+    first, second, first_weight, second_weight, owned, left, right, root_left, root_right, wide_rows,
+    per_step,
 ):
     _, owned_count, columns, _, _ = left.shape
 
+    steps = owned_count // per_step
+
     def kernel(ids_ref, *refs):
         del ids_ref
-        one, two, w_one, w_two, l_ref, r_ref, p_ref, q_ref, g_out, l_out, r_out, w_out = refs
+        one, two = refs[:2]
+        w_one, w_two = refs[2 : 2 + per_step], refs[2 + per_step : 2 + 2 * per_step]
+        l_ref, r_ref, p_ref, q_ref, g_out, l_out, r_out, w_out = refs[2 + 2 * per_step :]
 
         def update(turned):
-            for t in range(columns):
-                spot = slice(t * TILE, (t + 1) * TILE)
-                shares = two if turned else one
-                part = (slice(None), spot) if wide_rows else (spot, slice(None))
-                grad = shares[(0,) + part].astype(F32)
-                for i in range(1, shares.shape[0]):
-                    grad += shares[(i,) + part].astype(F32)
-                if turned == wide_rows:
-                    grad = grad.T
-                if turned:
-                    weight = w_two[spot, :].astype(F32)
-                else:
-                    weight = w_one[:, spot].astype(F32)
-                high = grad.astype(BF16)
-                g_out[0, 0, t] = grad
-                l_out[0, 0, t] = DECAY_RATE * l_ref[0, 0, t] + (1.0 - DECAY_RATE) * matmul_nt(
-                    high, high
-                )
-                r_out[0, 0, t] = DECAY_RATE * r_ref[0, 0, t] + (1.0 - DECAY_RATE) * matmul_t(
-                    high, high
-                )
-                stepped = matmul_three(p_ref[0, 0, t], grad)
-                stepped = matmul_three(stepped, q_ref[0, 0, t])
-                w_out[0, 0, t] = weight - MATRIX_RATE * stepped
+            shares = two if turned else one
+            for p in range(per_step):
+                for t in range(columns):
+                    wide = slice(p * TILE, (p + 1) * TILE)
+                    spot = slice(t * TILE, (t + 1) * TILE)
+                    part = (wide, spot) if wide_rows else (spot, wide)
+                    grad = shares[(0,) + part].astype(F32)
+                    for i in range(1, shares.shape[0]):
+                        grad += shares[(i,) + part].astype(F32)
+                    if turned == wide_rows:
+                        grad = grad.T
+                    weight = w_two[p][spot, :] if turned else w_one[p][:, spot]
+                    high = grad.astype(BF16)
+                    g_out[0, p, t] = grad
+                    l_out[0, p, t] = DECAY_RATE * l_ref[0, p, t] + (1.0 - DECAY_RATE) * matmul_nt(
+                        high, high
+                    )
+                    r_out[0, p, t] = DECAY_RATE * r_ref[0, p, t] + (1.0 - DECAY_RATE) * matmul_t(
+                        high, high
+                    )
+                    stepped = matmul_three(p_ref[0, p, t], grad)
+                    stepped = matmul_three(stepped, q_ref[0, p, t])
+                    w_out[0, p, t] = weight.astype(F32) - MATRIX_RATE * stepped
 
         @pl.when(pl.program_id(0) == 0)
         def _():
@@ -1364,32 +1447,46 @@
         def _():
             update(True)
 
-    last = owned_count - 1
+    last = steps - 1
+
+    def place_one(m, i):
+        return jnp.where(m == 0, i, last)
+
+    def place_two(m, i):
+        return jnp.where(m == 1, i, 0)
+
     def share(array, place):
         if wide_rows:
             return pl.BlockSpec(
-                (array.shape[0], TILE, columns * TILE), lambda m, p, ids: (0, place(m, p), 0)
+                (array.shape[0], per_step * TILE, columns * TILE),
+                lambda m, i, ids: (0, place(m, i), 0),
             )
         return pl.BlockSpec(
-            (array.shape[0], columns * TILE, TILE), lambda m, p, ids: (0, 0, place(m, p))
+            (array.shape[0], columns * TILE, per_step * TILE),
+            lambda m, i, ids: (0, 0, place(m, i)),
         )
 
-    share_one = share(first, lambda m, p: jnp.where(m == 0, p, last))
-    share_two = share(second, lambda m, p: jnp.where(m == 1, p, 0))
-    weight_one = pl.BlockSpec(
-        (TILE, columns * TILE), lambda m, p, ids: (ids[jnp.where(m == 0, p, last)], 0)
-    )
-    weight_two = pl.BlockSpec(
-        (columns * TILE, TILE), lambda m, p, ids: (0, ids[jnp.where(m == 1, p, 0)])
-    )
-    stat = pl.BlockSpec((1, 1, columns, TILE, TILE), lambda m, p, ids: (m, p, 0, 0, 0))
+    def weight_one(p):
+        return pl.BlockSpec(
+            (TILE, columns * TILE), lambda m, i, ids: (ids[place_one(m, i) * per_step + p], 0)
+        )
+
+    def weight_two(p):
+        return pl.BlockSpec(
+            (columns * TILE, TILE), lambda m, i, ids: (0, ids[place_two(m, i) * per_step + p])
+        )
+
+    stat = pl.BlockSpec((1, per_step, columns, TILE, TILE), lambda m, i, ids: (m, i, 0, 0, 0))
     shape = jax.ShapeDtypeStruct(left.shape, F32)
     return pl.pallas_call(
         kernel,
         grid_spec=pltpu.PrefetchScalarGridSpec(
             num_scalar_prefetch=1,
-            grid=(2, owned_count),
-            in_specs=[share_one, share_two, weight_one, weight_two] + [stat] * 4,
+            grid=(2, steps),
+            in_specs=[share(first, place_one), share(second, place_two)]
+            + [weight_one(p) for p in range(per_step)]
+            + [weight_two(p) for p in range(per_step)]
+            + [stat] * 4,
             out_specs=[stat] * 4,
         ),
         out_shape=[shape] * 4,
@@ -1398,7 +1495,17 @@
             flops=left.size * TILE * 16, bytes_accessed=left.size * 40, transcendentals=0
         ),
         name="shampoo",
-    )(owned, first, second, first_weight, second_weight, left, right, root_left, root_right)
+    )(
+        owned,
+        first,
+        second,
+        *([first_weight] * per_step),
+        *([second_weight] * per_step),
+        left,
+        right,
+        root_left,
+        root_right,
+    )
 
 
 def shampoo_update(grad_tiles, left_old, right_old, root_left, root_right, weight_tiles):
@@ -1481,22 +1588,22 @@
     allowed = (documents[:, None] == row_docs[None, :]) & (positions[:, None] <= row_ids[None, :])
     mask = jnp.where(allowed, 0.0, MASKED).astype(F32)
 
-    rows_own = tokens.astype(F32)
+    w_query_all, w_out_part, bias_all = gather_weights(
+        w_query, w_out, bias_query.reshape(1, slab), batch_size, head_count
+    )
+    w_out_part, cotangent_later, tokens_later = lax.optimization_barrier(
+        (w_out_part, cotangent, tokens)
+    )
+    cot_all = lax.all_gather(cotangent_later, "head", axis=0, tiled=True)
+    rows_own = tokens_later.astype(F32)
     normed_one, inverse_one = norm_stats(rows_own)
     normed_in = (normed_one * gain_one + shift_one).astype(BF16)
     w_kv = jnp.concatenate([w_key, w_value], axis=1)
     kv_bias = jnp.concatenate([jnp.zeros_like(bias_value), bias_value])
     kv_own = (matmul(normed_in, w_kv) + kv_bias).astype(BF16)
-    kv_all = lax.all_gather(kv_own, "head", axis=0, tiled=True)
+    w_out_all, kv_all = gather_rest(w_out_part, kv_own, batch_size, head_count)
     key_rows = kv_all[:, :head_size]
     value_rows = kv_all[:, head_size:]
-
-    w_query_all, w_out_part, bias_all = gather_weights(
-        w_query, w_out, bias_query.reshape(1, slab), batch_size, head_count
-    )
-    w_out_part, cotangent_later = lax.optimization_barrier((w_out_part, cotangent))
-    w_out_all = gather_rest(w_out_part, batch_size, head_count)
-    cot_all = lax.all_gather(cotangent_later, "head", axis=0, tiled=True)
 
     queries = (matmul(normed_in, w_query_all) + bias_all.reshape(1, width)).astype(BF16)
     attended, log_totals = attention_forward(queries, key_rows, value_rows.T, mask, head_count)
@@ -1504,13 +1611,14 @@
         attended, w_out_all, tokens, vectors
     )
 
-    mix_part, grad_up, down_shares, grad_mixer_in, grad_up_bias = mixer_pass(
+    mix_a, mix_b, grad_up, down_shares, grad_mixer_in, grad_up_bias = mixer_pass(
         mixer_in, cot_all, w_up, w_down, bias_up, owner, batch_size, head_count, 2
     )
-    mix_one = lax.psum_scatter(mix_part, "head", scatter_dimension=0, tiled=True)
+    mix_first = lax.psum_scatter(mix_a, "head", scatter_dimension=0, tiled=True)
+    up_shares = lax.psum_scatter(grad_up, "batch", scatter_dimension=0, tiled=True)
 
     kv_rows = width // head_count // batch_size
-    grad_tokens, query_share, out_share, kv_total, vector_wide, up_bias_total, up_shares = backward_pass(
+    grad_tokens, query_share, out_share, kv_total, vector_wide, up_bias_total = backward_pass(
         owner,
         grad_mixer_in,
         cotangent,
@@ -1529,10 +1637,12 @@
         w_out_all,
         w_kv,
         grad_up_bias.reshape(8, -1),
-        grad_up,
         batch_size,
         head_count,
     )
+    kv_total, mix_first, mix_b = lax.optimization_barrier((kv_total, mix_first, mix_b))
+    up_shares, mix_first = lax.optimization_barrier((up_shares, mix_first))
+    mix_second = lax.psum_scatter(mix_b, "head", scatter_dimension=0, tiled=True)
     kv_total = kv_total.reshape(batch_size * kv_rows, 2 * head_size)
     up_bias_total = up_bias_total.reshape(-1)
     vector_all = vector_wide.transpose(1, 0, 2).reshape(8, width)
@@ -1553,6 +1663,7 @@
         mixer_root_left,
         mixer_root_right,
         True,
+        1,
     )
     attn_out = shampoo(
         query_share,
@@ -1565,6 +1676,7 @@
         attn_root_left,
         attn_root_right,
         False,
+        attn_left.shape[1],
     )
     kv_count = width // head_count
 
@@ -1580,7 +1692,7 @@
         kv_root_right,
         jnp.stack([kv_tiles(kv_slab[:, :head_size]), kv_tiles(kv_slab[:, head_size:])]),
     )
-    _, mix_one = lax.optimization_barrier((kv_total, mix_one))
+    mix_one = jnp.concatenate([mix_first, mix_second], axis=0)
     output = resid + mix_one.astype(F32) + bias_down
     vec_out = diagonal_update(vector_total, vector_second, vectors)
     query_out = diagonal_update(query_bias_total, query_second, bias_query)

time: 533 us -> 514 us (0.964)
  Pallas kernels: 462 us -> 443 us
    pallas_call x1, Pallas kernels: 156 us -> 145 us  [backward_pass(): pl.pallas_call(kernel, out_shape=(jax.ShapeDtypeStruct((tok, width), F32)...]
    pallas_call x1, Pallas kernels: 60.6 us -> 51.7 us  [gather_weights(): pl.pallas_call(kernel, out_shape=(jax.ShapeDtypeStruct((rows, cols * head...]
    all_gather x1, waiting for transfers between devices: 11.6 us -> 4.11 us  [body(): cot_all = lax.all_gather(cotangent_later, 'head', axis=0, tiled=True)]
    reduce_scatter x1 -> x2, waiting for transfers between devices: 0.01 us -> 6.49 us  [the longest x1 6.47 us: body(): lax.psum_scatter(mix_b, 'head', scatter_dimension=0, tiled=True)]
  transfers between devices with their start and end apart: 3 -> 4, of which waited for: 1 -> 2; matrix products, arithmetic and copies ran while one was open for 5% -> 6% of each run, Pallas kernels for 60% -> 48%
where the time goes in v4:
time: 514 us; the launch traced here: 505 us
  Pallas kernels  443 us (86%)
  between operations  14.6 us (3%)
  local copies, waits for them, and re-layouts  13.5 us (3%)
  matrix products  12.4 us (2%)
  waiting for transfers between devices  11.3 us (2%)
  other arithmetic  10.1 us (2%)
    pallas_call x1, Pallas kernels, mixer_pass(): pl.pallas_call(kernel, out_shape=(jax.ShapeDtypeStruct(block + (width,),...  149 us
    pallas_call x1, Pallas kernels, backward_pass(): pl.pallas_call(kernel, out_shape=(jax.ShapeDtypeStruct((tok, width), F32)...  145 us
    pallas_call x1, Pallas kernels, gather_weights(): pl.pallas_call(kernel, out_shape=(jax.ShapeDtypeStruct((rows, cols * head...  51.7 us
    pallas_call x1, Pallas kernels, gather_rest(): pl.pallas_call(kernel, out_shape=(jax.ShapeDtypeStruct(w_all.shape, w_all...  33 us
    pallas_call x2, Pallas kernels, shampoo(): pl.pallas_call(kernel, grid_spec=pltpu.PrefetchScalarGridSpec(num_scalar_...  30.7 us
    pallas_call x1, Pallas kernels, attention_forward(): pl.pallas_call(kernel, grid=(slabs,), out_shape=(jax.ShapeDtypeStruct((to...  24 us
  transfers between devices with their start and end apart: 4, of which 2 were waited for; matrix products, arithmetic and copies ran while one was open for 6% of the time, Pallas kernels for 48%

profile of v4, /device:TPU:0, one launch (start us, length us, event | category | flops | bytes accessed | tf_op | source)
XLA Modules:
  0.0 505.2 jit_solution(2760596444554487554)
XLA Ops:
  7.2 0.0 copy-start
  7.2 0.0 copy-start.1
  7.2 0.0 all-gather.2.cloned.1.call-start
  7.3 51.7 %gather_weights.1 = (bf16[2048,2048]{1,0:T(8,128)(2,1)}, bf16[2048,2048]{1,0:T(8,128)(2,1)}, f32[8,1,256]{2,1,0:T(1,128)}) custom-call(bf16[2048,256]{1,0:T(8,128)(2,1)} %refs_5_.2, bf16[256,2048]{1,0:T(8,128)(2,1)} %refs_9_.1, f32[1,256]{1,0:T(1,128)} %bitcast.108), custom_call_target="tpu_custom_call" | custom-call | bytes 125829120 | tf_op jit(solution)/shard_map/gather_weights/pallas_call | solution.py:288
  59.1 0.0 all-gather.2.cloned.1.call-update
  59.1 0.0 reduce-scatter.6.cloned.1.call-start
  59.2 0.2 convert_reduce_fusion
  59.4 0.4 fusion.3
  59.8 0.2 copy-done.6
  60.1 0.1 constant_dynamic-update-slice_fusion.1
  60.2 0.1 copy-done.7
  60.2 0.1 constant_dynamic-update-slice_fusion.wkv_ref
  60.4 0.0 copy-start.8
  60.4 1.1 fusion.41
  61.5 1.3 fusion.17.kv_ref
  62.8 33.0 %gather_rest.1 = (bf16[2048,2048]{1,0:T(8,128)(2,1)}, bf16[2048,256]{1,0:T(8,128)(2,1)}) custom-call(bf16[2048,2048]{1,0:T(8,128)(2,1)} %get-tuple-element.70.in_ref, bf16[256,256]{1,0:T(8,128)(2,1)} %fusion.17.kv_ref), custom_call_target="tpu_custom_call", output_to_operand_aliasing={{0}: (0, {})} | custom-call | bytes 104857600 | tf_op jit(solution)/shard_map/gather_rest/pallas_call | solution.py:358
  95.8 1.6 copy.80
  97.4 1.1 slice_bitcast_fusion.1
  98.5 2.1 copy.81.k_ref
  100.6 0.9 fusion.38
  101.4 1.0 copy.82.v_ref
  102.5 0.1 convert_reduce_fusion.1
  102.6 0.1 dynamic_slice.12
  102.6 1.9 fusion.18
  104.5 7.0 %fusion.q_ref = bf16[256,2048]{1,0:T(8,128)(2,1)} fusion(bf16[2048,2048]{1,0:T(8,128)(2,1)} %get-tuple-element.68.wq_ref, f32[2048]{0:T(1024)S(1)} %bitcast.114, bf16[256,2048]{1,0:T(8,128)(2,1)S(1)} %copy-done.1, f32[2048]{0:T(1024)S(1)} %bitcast.105, f32[2048]{0:T(1024)S(1)} %bitcast.107, f32[256]{0:T(256)S(1)} %add_rsqrt_fusion, ...), kind=kOutput, calls=%fused_computation.3 | convolution fusion | flops 2151677952 | bytes 10512384 | tf_op jit(solution)/shard_map/dot_general | solution.py:29
  111.5 24.0 %attention_forward.1 = (bf16[256,2048]{1,0:T(8,128)(2,1)}, f32[8,2,256]{2,1,0:T(2,128)}) custom-call(bf16[256,2048]{1,0:T(8,128)(2,1)} %fusion.q_ref, bf16[2048,128]{1,0:T(8,128)(2,1)} %copy.81.k_ref, bf16[128,2048]{1,0:T(8,128)(2,1)} %copy.82.v_ref, f32[2048,256]{1,0:T(8,128)} %get-tuple-element.208.mask_ref), custom_call_target="tpu_custom_call" | custom-call | flops 8589934592 | bytes 2097152 | tf_op jit(solution)/shard_map/attention_forward/pallas_call | solution.py:829
  135.5 8.8 %project_out.1 = (f32[256,2048]{1,0:T(8,128)}, bf16[256,2048]{1,0:T(8,128)(2,1)}, f32[256,2048]{1,0:T(8,128)}, f32[256,128]{1,0:T(8,128)}) custom-call(bf16[256,2048]{1,0:T(8,128)(2,1)} %get-tuple-element.72.att_ref, bf16[256,2048]{1,0:T(8,128)(2,1)} %tok_ref.3, f32[6,2048]{1,0:T(8,128)} %vec_ref.3, bf16[2048,2048]{1,0:T(8,128)(2,1)} %get-tuple-element.73.w_ref.wo_ref), custom_call_target="tpu_custom_call" | custom-call | flops 2147483648 | bytes 58720256 | tf_op jit(solution)/shard_map/project_out/pallas_call | solution.py:387
  144.3 4.1 all-gather.2.cloned.1.call-done
  148.4 149.4 %mixer_pass.1 = (bf16[4,2,2,128,2048]{4,3,2,1,0:T(8,128)(2,1)}, bf16[4,2,2,128,1024]{4,3,2,1,0:T(8,128)(2,1)}, bf16[4,2,2,128,1024]{4,3,2,1,0:T(8,128)(2,1)}, bf...) custom-call(s32[16]{0:T(128)} %owner_ref.3, ...), custom_call_target="tpu_custom_call" | custom-call | flops 51539607552 | bytes 314572800 | tf_op jit(solution)/shard_map/mixer_pass/pallas_call | solution.py:753
  297.8 0.0 reduce-scatter.6.cloned.1.call-update
  297.8 0.0 reduce-scatter.10.cloned.1.call-start
  297.8 0.7 reduce-scatter.10.cloned.1.call-update
  298.5 0.0 reduce-scatter.8.cloned.1.call-start
  298.6 0.0 copy-done.16
  298.6 0.6 reduce_sum.39
  299.2 145.4 %backward_pass.1 = (f32[256,2048]{1,0:T(8,128)}, bf16[1,256,512]{2,1,0:T(8,128)(2,1)}, bf16[1,256,512]{2,1,0:T(8,128)(2,1)}, f32[4,64,256]{2,1,0:T(8,128)}, f32[8,8,256]{2,1,0:T(8,128)}, /*index=5*/f32[8,128]{1,0:T(8,128)}) custom-call(s32[16]{0:T(128)} %owner_ref.3, f32[256,2048]{1,0:T(8,128)} %bitcast.115, bf16[256,2048]{1,0:T(8,128)(2,1)} %cot_ref.1, ...), custom_call_target="tpu_custom_call" | custom-call | flops 30064771072 | bytes 209715200 | tf_op jit(solution)/shard_map/backward_pass/pallas_call | solution.py:1321
  444.7 0.0 reduce-scatter.6.cloned.1.call-done
  444.7 0.0 copy-start.9
  444.7 0.0 copy-start.15
  444.7 0.0 reduce-scatter.8.cloned.1.call-update
  444.8 0.6 copy-done.26
  445.3 0.6 dynamic_slice.14.ids_ref
  445.9 0.9 dynamic-slice_convert_fusion
  446.9 0.7 divide_subtract_fusion
  447.6 0.6 slice.63
  448.2 0.6 slice.64
  448.8 0.0 copy-start.18
  448.8 0.0 copy-start.22
  448.9 0.0 copy-start.20
  448.9 8.2 %shampoo.2 = (f32[2,4,2,128,128]{4,3,2,1,0:T(8,128)}, f32[2,4,2,128,128]{4,3,2,1,0:T(8,128)}, f32[2,4,2,128,128]{4,3,2,1,0:T(8,128)}, f32[2,4,2,128,128]{4,3,2,1,0:T(8,128)}) custom-call(s32[4]{0:T(128)} %dynamic_slice.14.ids_ref, bf16[1,256,512]{2,1,0:T(8,128)(2,1)} %get-tuple-element.92.refs_0_, bf16[1,256,512]{2,1,0:T(8,128)(2,1)} %get-tuple-element.93.refs_1_, ...), custom_call_target="tpu_custom_call" | custom-call | flops 536870912 | bytes 10485760 | tf_op jit(solution)/shard_map/shampoo/pallas_call | solution.py:1481
  457.1 0.7 divide_subtract_fusion.2
  457.8 0.5 divide_subtract_fusion.3
  458.4 0.6 divide_subtract_fusion.1
  459.0 0.7 fusion.25
  459.7 0.4 fusion.20
  460.1 1.1 fusion.10
  461.2 22.5 %shampoo.3 = (f32[2,4,8,128,128]{4,3,2,1,0:T(8,128)}, f32[2,4,8,128,128]{4,3,2,1,0:T(8,128)}, f32[2,4,8,128,128]{4,3,2,1,0:T(8,128)}, f32[2,4,8,128,128]{4,3,2,1,0:T(8,128)}) custom-call(s32[4]{0:T(128)} %dynamic_slice.14.ids_ref, bf16[1,512,1024]{2,1,0:T(8,128)(2,1)} %reduce-scatter.10.cloned.1.call-done.refs_0_, bf16[4,512,1024]{2,1,0:T(8,128)(2,1)} %bitcast.85, ...), custom_call_target="tpu_custom_call" | custom-call | flops 2147483648 | bytes 41943040 | tf_op jit(solution)/shard_map/shampoo/pallas_call | solution.py:1481
  483.8 1.3 fusion.16
  485.1 1.4 fusion.13
  486.5 6.5 %reduce-scatter.8.cloned.1.call-done = bf16[128,2048]{1,0:T(8,128)(2,1)} async-done(((bf16[1024,2048]{1,0:T(8,128)(2,1)}), bf16[128,2048]{1,0:T(8,128)(2,1)}) %reduce-scatter.8.cloned.1.call-update) | async-done | bytes 524304 | tf_op jit(solution)/shard_map/reduce_scatter | solution.py:1645
  492.9 2.8 add_add_fusion
  495.7 1.3 copy.101
  497.1 0.6 copy.102
  497.7 0.6 copy.103
  (50 shorter events, 0.2 us)
Async XLA Ops:
  7.2 452.5 %copy-start = (f32[2,2,1,128,128]{4,3,2,1,0:T(8,128)S(1)}, f32[2,2,1,128,128]{4,3,2,1,0:T(8,128)}, u32[]{:S(2)}) copy-start(f32[2,2,1,128,128]{4,3,2,1,0:T(8,128)} %param.54) | copy-start | bytes 786436
  7.2 52.0 %copy-start.1 = (bf16[256,2048]{1,0:T(8,128)(2,1)S(1)}, bf16[256,2048]{1,0:T(8,128)(2,1)}, u32[]{:S(2)}) copy-start(bf16[256,2048]{1,0:T(8,128)(2,1)} %tok_ref.3) | copy-start | bytes 3145732
  7.2 51.9 %copy-start.21 = (f32[128]{0:T(128)S(1)}, f32[128]{0:T(128)}, u32[]{:S(2)}) copy-start(f32[128]{0:T(128)} %param.36) | copy-start | bytes 1540
  7.2 141.1 %all-gather.2.cloned.1.call-start = ((), (), s32[]{:S(2)}) async-start(), calls=%async_computation.3 | async-start | bytes 9437184 | tf_op jit(solution)/shard_map/all_gather | solution.py:1597
  59.0 1.0 copy-start.6
  59.1 1.2 copy-start.7
  59.1 385.6 %reduce-scatter.6.cloned.1.call-start = ((), (), s32[]{:S(2)}) async-start(), calls=%async_computation.4 | async-start | bytes 4718592 | tf_op jit(solution)/shard_map/reduce_scatter | solution.py:1617
  60.4 1.2 copy-start.8
  95.8 4.7 copy-start.2
  98.5 3.9 copy-start.23
  101.4 3.1 copy-start.25
  297.8 161.2 %reduce-scatter.10.cloned.1.call-start = ((), (), s32[]{:S(2)}) async-start(), calls=%async_computation.6 | async-start | bytes 5242880
  297.8 0.8 copy-start.16
  298.5 194.4 %reduce-scatter.8.cloned.1.call-start = ((), (), s32[]{:S(2)}) async-start(), calls=%async_computation.5 | async-start | bytes 4718592 | tf_op jit(solution)/shard_map/reduce_scatter | solution.py:1645
  444.7 0.7 copy-start.26
  444.7 2.2 copy-start.9
  444.7 2.2 copy-start.10
  444.7 2.2 copy-start.15
  448.8 8.3 %copy-start.18 = (f32[256]{0:T(256)S(1)}, f32[256]{0:T(256)}, u32[]{:S(2)}) copy-start(f32[256]{0:T(256)} %param.35) | copy-start | bytes 3076
  448.8 8.3 %copy-start.22 = (f32[256]{0:T(256)S(1)}, f32[256]{0:T(256)}, u32[]{:S(2)}) copy-start(f32[256]{0:T(256)} %param.57) | copy-start | bytes 3076
  448.9 8.9 %copy-start.24 = (f32[128]{0:T(128)S(1)}, f32[128]{0:T(128)}, u32[]{:S(2)}) copy-start(f32[128]{0:T(128)} %param.58) | copy-start | bytes 1540
  448.9 9.5 %copy-start.17 = (f32[8,128]{1,0:T(8,128)S(1)}, f32[8,128]{1,0:T(8,128)}, u32[]{:S(2)}) copy-start(f32[8,128]{1,0:T(8,128)} %get-tuple-element.91) | copy-start | bytes 12292
  448.9 9.5 %copy-start.19 = (f32[1024]{0:T(1024)S(1)}, f32[1024]{0:T(1024)}, u32[]{:S(2)}) copy-start(f32[1024]{0:T(1024)} %param.37) | copy-start | bytes 12292
  448.9 9.5 %copy-start.20 = (f32[1024]{0:T(1024)S(1)}, f32[1024]{0:T(1024)}, u32[]{:S(2)}) copy-start(f32[1024]{0:T(1024)} %param.59) | copy-start | bytes 12292
  448.9 10.1 %copy-start.13 = (f32[4,64,256]{2,1,0:T(8,128)S(1)}, f32[4,64,256]{2,1,0:T(8,128)}, u32[]{:S(2)}) copy-start(f32[4,64,256]{2,1,0:T(8,128)} %get-tuple-element.104) | copy-start | bytes 786436
  448.9 11.2 %copy-start.14 = (f32[2,2,1,128,128]{4,3,2,1,0:T(8,128)S(1)}, f32[2,2,1,128,128]{4,3,2,1,0:T(8,128)}, u32[]{:S(2)}) copy-start(f32[2,2,1,128,128]{4,3,2,1,0:T(8,128)} %param.55) | copy-start | bytes 786436
  461.2 22.6 %copy-start.11 = (f32[2,2,1,128,128]{4,3,2,1,0:T(8,128)S(1)}, f32[2,2,1,128,128]{4,3,2,1,0:T(8,128)}, u32[]{:S(2)}) copy-start(f32[2,2,1,128,128]{4,3,2,1,0:T(8,128)} %param.53) | copy-start | bytes 786436
  461.2 23.9 %copy-start.12 = (f32[2,2,1,128,128]{4,3,2,1,0:T(8,128)S(1)}, f32[2,2,1,128,128]{4,3,2,1,0:T(8,128)}, u32[]{:S(2)}) copy-start(f32[2,2,1,128,128]{4,3,2,1,0:T(8,128)} %param.52) | copy-start | bytes 786436
  461.2 31.7 %copy-start.3 = (f32[256,2048]{1,0:T(8,128)S(1)}, f32[256,2048]{1,0:T(8,128)}, u32[]{:S(2)}) copy-start(f32[256,2048]{1,0:T(8,128)} %get-tuple-element.74) | copy-start | bytes 6291460
  461.2 31.7 %copy-start.5 = (bf16[128,2048]{1,0:T(8,128)(2,1)S(1)}, bf16[128,2048]{1,0:T(8,128)(2,1)}, u32[]{:S(2)}) copy-start(bf16[128,2048]{1,0:T(8,128)(2,1)} %reduce-scatter.6.cloned.1.call-done) | copy-start | bytes 1572868
  492.9 2.8 copy-start.4
Sparse Core Ops, SparseCore 0:
  59.2 89.1 all-gather.1
  297.9 47.1 reduce-scatter.5
  348.1 76.8 reduce-scatter.9
  444.9 48.0 reduce-scatter.7

commit v5 on v4

--- a/solution.py
+++ b/solution.py
@@ -808,21 +808,25 @@
     )
 
 
-def attention_forward(queries, key_rows, value_turned, mask, slabs):
+def attention_forward(queries, kv_all, mask, slabs):
     tok, width = queries.shape
-    seq_len, head_size = key_rows.shape
+    seq_len, head_size = kv_all.shape[0], kv_all.shape[1] // 2
     slab = width // slabs
     heads = slab // head_size
     scale = LOG2E / math.sqrt(head_size)
 
-    def kernel(q_ref, k_ref, v_ref, mask_ref, o_ref, log_ref):
+    def kernel(q_ref, k_ref, v_ref, mask_ref, o_ref, log_ref, turned):
+        @pl.when(pl.program_id(0) == 0)
+        def _():
+            turned[...] = v_ref[...].astype(F32).T.astype(BF16)
+
         for j in range(heads):
             spot = slice(j * head_size, (j + 1) * head_size)
             scores = matmul_nt(k_ref[...], q_ref[:, spot]) * scale + mask_ref[...]
             highest = jnp.max(scores, axis=0, keepdims=True)
             raised = jnp.exp2(scores - highest)
             total = jnp.sum(raised, axis=0, keepdims=True)
-            out = matmul(v_ref[...], raised.astype(BF16)) / total
+            out = matmul(turned[...], raised.astype(BF16)) / total
             o_ref[:, spot] = out.T.astype(BF16)
             log_ref[0, j : j + 1, :] = highest + jnp.log2(total)
 
@@ -836,13 +840,14 @@
         in_specs=[
             pl.BlockSpec((tok, slab), lambda i: (0, i)),
             pl.BlockSpec((seq_len, head_size), lambda i: (0, 0)),
-            pl.BlockSpec((head_size, seq_len), lambda i: (0, 0)),
+            pl.BlockSpec((seq_len, head_size), lambda i: (0, 1)),
             pl.BlockSpec((seq_len, tok), lambda i: (0, 0)),
         ],
         out_specs=(
             pl.BlockSpec((tok, slab), lambda i: (0, i)),
             pl.BlockSpec((1, heads, tok), lambda i: (i, 0, 0)),
         ),
+        scratch_shapes=[pltpu.VMEM((head_size, seq_len), BF16)],
         compiler_params=pltpu.CompilerParams(vmem_limit_bytes=VMEM_LIMIT),
         cost_estimate=pl.CostEstimate(
             flops=8 * tok * seq_len * width,
@@ -850,16 +855,16 @@
             transcendentals=tok * seq_len * slabs * heads,
         ),
         name="attention_forward",
-    )(queries, key_rows, value_turned, mask)
+    )(queries, kv_all, kv_all, mask)
 
 
 def backward_pass(
     owner, grad_mixer, cotangent, tokens, normed_two, inverse_two, vectors, queries, attended,
-    log_totals, key_rows, key_turned, value_rows, mask, w_query_all, w_out_all, w_kv, up_parts,
+    log_totals, kv_all, mask, w_query_all, w_out_all, w_kv, up_parts,
     batch_size, head_count,
 ):
     tok, width = tokens.shape
-    seq_len, head_size = key_rows.shape
+    seq_len, head_size = kv_all.shape[0], kv_all.shape[1] // 2
     slab = width // head_count
     heads = slab // head_size
     n = head_count // 2
@@ -875,9 +880,9 @@
 
     def kernel(
         owner_ref, gm_ref, cot_ref, tok_ref, n2_ref, i2_ref, vec_ref, q_ref, att_ref, log_ref,
-        k_ref, kt_ref, v_ref, mask_ref, wq_ref, wo_ref, wkv_ref, up_ref,
+        keys_ref, mask_ref, wq_ref, wo_ref, wkv_ref, up_ref,
         tokens_out, query_out, out_out, kv_out, vec_out, up_out,
-        branch, wide_tiles, normed_owned, branch_owned, grad_in, wq_buf, wo_buf, dk, dv,
+        branch, kt_ref, wide_tiles, normed_owned, branch_owned, grad_in, wq_buf, wo_buf, dk, dv,
         give, mine, pair_in, land, hop, z_land,
         dkv, dkv_pair, dkv_here, dkv_land,
         kv_part, kv_pair, kv_sum, kv_land, kv_half, kv_zland,
@@ -976,6 +981,7 @@
 
         for p in range(tiles):
             normed_owned[:, p * TILE : (p + 1) * TILE] = wide_tiles[owner_ref[p]]
+        kt_ref[...] = keys_ref[:, :head_size].astype(F32).T.astype(BF16)
         dk[...] = jnp.zeros_like(dk)
         dv[...] = jnp.zeros_like(dv)
         grad_in[...] = jnp.zeros_like(grad_in)
@@ -1110,9 +1116,9 @@
                 total = jnp.zeros((head_size, tok), F32)
                 for start in range(0, seq_len, block):
                     part = slice(start, start + block)
-                    scores = matmul_nt(k_ref[part, :], query) * scale
+                    scores = matmul_nt(keys_ref[part, :head_size], query) * scale
                     probs = jnp.exp2(scores + (mask_ref[part, :].astype(F32) - logs))
-                    grad_probs = matmul_nt(v_ref[part, :], grad)
+                    grad_probs = matmul_nt(keys_ref[part, head_size:], grad)
                     grad_scores = (probs * (grad_probs - delta)).astype(BF16)
                     dv[part, :] += matmul(probs.astype(BF16), grad)
                     dk[part, :] += matmul(grad_scores, query)
@@ -1329,11 +1335,12 @@
             jax.ShapeDtypeStruct(up_parts.shape, F32),
         ),
         in_specs=[pl.BlockSpec(memory_space=pltpu.SMEM), ANY, ANY, WHOLE, ANY]
-        + [WHOLE] * 9
+        + [WHOLE] * 7
         + [ANY, ANY, WHOLE, WHOLE],
         out_specs=(WHOLE,) * 6,
         scratch_shapes=[
             vm((tok, width), BF16),
+            vm((head_size, seq_len), BF16),
             vm((tiles, tok, TILE), BF16),
             vm((tok, width), BF16),
             vm((tok, width), BF16),
@@ -1381,7 +1388,7 @@
         name="backward_pass",
     )(
         owner, grad_mixer, cotangent, tokens, normed_two, inverse_two, vectors, queries, attended,
-        log_totals, key_rows, key_turned, value_rows, mask, w_query_all, w_out_all, w_kv, up_parts,
+        log_totals, kv_all, mask, w_query_all, w_out_all, w_kv, up_parts,
     )
 
 
@@ -1416,28 +1423,35 @@
 
         def update(turned):
             shares = two if turned else one
-            for p in range(per_step):
-                for t in range(columns):
+            tiles = [(p, t) for p in range(per_step) for t in range(columns)]
+            group = 4 if len(tiles) % 4 == 0 else 1
+            for first in range(0, len(tiles), group):
+                here = tiles[first : first + group]
+                grads = []
+                for p, t in here:
                     wide = slice(p * TILE, (p + 1) * TILE)
                     spot = slice(t * TILE, (t + 1) * TILE)
                     part = (wide, spot) if wide_rows else (spot, wide)
                     grad = shares[(0,) + part].astype(F32)
                     for i in range(1, shares.shape[0]):
                         grad += shares[(i,) + part].astype(F32)
-                    if turned == wide_rows:
-                        grad = grad.T
+                    grads.append(grad.T if turned == wide_rows else grad)
+                highs = [grad.astype(BF16) for grad in grads]
+                halfway = [matmul_three(p_ref[0, p, t], g) for (p, t), g in zip(here, grads)]
+                lefts = [matmul_nt(high, high) for high in highs]
+                steps_here = [matmul_three(m, q_ref[0, p, t]) for (p, t), m in zip(here, halfway)]
+                rights = [matmul_t(high, high) for high in highs]
+                for i, (p, t) in enumerate(here):
+                    spot = slice(t * TILE, (t + 1) * TILE)
                     weight = w_two[p][spot, :] if turned else w_one[p][:, spot]
-                    high = grad.astype(BF16)
-                    g_out[0, p, t] = grad
-                    l_out[0, p, t] = DECAY_RATE * l_ref[0, p, t] + (1.0 - DECAY_RATE) * matmul_nt(
-                        high, high
+                    g_out[0, p, t] = grads[i]
+                    l_out[0, p, t] = (
+                        DECAY_RATE * l_ref[0, p, t] + (1.0 - DECAY_RATE) * lefts[i]
                     )
-                    r_out[0, p, t] = DECAY_RATE * r_ref[0, p, t] + (1.0 - DECAY_RATE) * matmul_t(
-                        high, high
+                    r_out[0, p, t] = (
+                        DECAY_RATE * r_ref[0, p, t] + (1.0 - DECAY_RATE) * rights[i]
                     )
-                    stepped = matmul_three(p_ref[0, p, t], grad)
-                    stepped = matmul_three(stepped, q_ref[0, p, t])
-                    w_out[0, p, t] = weight.astype(F32) - MATRIX_RATE * stepped
+                    w_out[0, p, t] = weight.astype(F32) - MATRIX_RATE * steps_here[i]
 
         @pl.when(pl.program_id(0) == 0)
         def _():
@@ -1602,11 +1616,9 @@
     kv_bias = jnp.concatenate([jnp.zeros_like(bias_value), bias_value])
     kv_own = (matmul(normed_in, w_kv) + kv_bias).astype(BF16)
     w_out_all, kv_all = gather_rest(w_out_part, kv_own, batch_size, head_count)
-    key_rows = kv_all[:, :head_size]
-    value_rows = kv_all[:, head_size:]
 
     queries = (matmul(normed_in, w_query_all) + bias_all.reshape(1, width)).astype(BF16)
-    attended, log_totals = attention_forward(queries, key_rows, value_rows.T, mask, head_count)
+    attended, log_totals = attention_forward(queries, kv_all, mask, head_count)
     resid, mixer_in, normed_two, inverse_wide = project_out(
         attended, w_out_all, tokens, vectors
     )
@@ -1629,9 +1641,7 @@
         queries,
         attended,
         log_totals,
-        key_rows,
-        key_rows.T,
-        value_rows,
+        kv_all,
         mask.astype(BF16),
         w_query_all,
         w_out_all,
@@ -1640,7 +1650,7 @@
         batch_size,
         head_count,
     )
-    kv_total, mix_first, mix_b = lax.optimization_barrier((kv_total, mix_first, mix_b))
+    kv_total, mix_first = lax.optimization_barrier((kv_total, mix_first))
     up_shares, mix_first = lax.optimization_barrier((up_shares, mix_first))
     mix_second = lax.psum_scatter(mix_b, "head", scatter_dimension=0, tiled=True)
     kv_total = kv_total.reshape(batch_size * kv_rows, 2 * head_size)
@@ -1663,7 +1673,7 @@
         mixer_root_left,
         mixer_root_right,
         True,
-        1,
+        2 if owned_count % 2 == 0 else 1,
     )
     attn_out = shampoo(
         query_share,
@@ -1692,6 +1702,7 @@
         kv_root_right,
         jnp.stack([kv_tiles(kv_slab[:, :head_size]), kv_tiles(kv_slab[:, head_size:])]),
     )
+    _, mix_second = lax.optimization_barrier((mixer_out[0], mix_second))
     mix_one = jnp.concatenate([mix_first, mix_second], axis=0)
     output = resid + mix_one.astype(F32) + bias_down
     vec_out = diagonal_update(vector_total, vector_second, vectors)

time: 514 us -> 504 us (0.981)
  local copies, waits for them, and re-layouts: 13.5 us -> 7.24 us
  Pallas kernels: 443 us -> 437 us
    pallas_call x2, Pallas kernels: 30.7 us -> 22.9 us  [shampoo(): pl.pallas_call(kernel, grid_spec=pltpu.PrefetchScalarGridSpec(num_scalar_...]
    all_gather x1, waiting for transfers between devices: 4.11 us -> 10.4 us  [body(): cot_all = lax.all_gather(cotangent_later, 'head', axis=0, tiled=True)]
    reduce_scatter x1, waiting for transfers between devices: 6.47 us -> 0.78 us  [body(): lax.psum_scatter(mix_b, 'head', scatter_dimension=0, tiled=True)]
  transfers between devices with their start and end apart: 4 -> 4, of which waited for: 2 -> 2; matrix products, arithmetic and copies ran while one was open for 6% -> 5% of each run, Pallas kernels for 48% -> 48%
where the time goes in v5:
time: 504 us; the launch traced here: 496 us
  Pallas kernels  437 us (87%)
  between operations  14.4 us (3%)
  matrix products  14.2 us (3%)
  waiting for transfers between devices  12.4 us (2%)
  other arithmetic  10.1 us (2%)
  local copies, waits for them, and re-layouts  7.24 us (1%)
    pallas_call x1, Pallas kernels, mixer_pass(): pl.pallas_call(kernel, out_shape=(jax.ShapeDtypeStruct(block + (width,),...  149 us
    pallas_call x1, Pallas kernels, backward_pass(): pl.pallas_call(kernel, out_shape=(jax.ShapeDtypeStruct((tok, width), F32)...  148 us
    pallas_call x1, Pallas kernels, gather_weights(): pl.pallas_call(kernel, out_shape=(jax.ShapeDtypeStruct((rows, cols * head...  51.7 us
    pallas_call x1, Pallas kernels, gather_rest(): pl.pallas_call(kernel, out_shape=(jax.ShapeDtypeStruct(w_all.shape, w_all...  33 us
    pallas_call x1, Pallas kernels, attention_forward(): pl.pallas_call(kernel, grid=(slabs,), out_shape=(jax.ShapeDtypeStruct((to...  24.3 us
    pallas_call x2, Pallas kernels, shampoo(): pl.pallas_call(kernel, grid_spec=pltpu.PrefetchScalarGridSpec(num_scalar_...  22.9 us
    all_gather x1, waiting for transfers between devices, body(): cot_all = lax.all_gather(cotangent_later, 'head', axis=0, tiled=True)  10.4 us
  transfers between devices with their start and end apart: 4, of which 2 were waited for; matrix products, arithmetic and copies ran while one was open for 5% of the time, Pallas kernels for 48%

profile of v5, /device:TPU:0, one launch (start us, length us, event | category | flops | bytes accessed | tf_op | source)
XLA Modules:
  0.0 495.8 jit_solution(8738749562773519363)
XLA Ops:
  7.2 0.0 copy-start
  7.2 0.0 copy-start.1
  7.2 0.0 all-gather.2.cloned.1.call-start
  7.3 51.7 %gather_weights.1 = (bf16[2048,2048]{1,0:T(8,128)(2,1)}, bf16[2048,2048]{1,0:T(8,128)(2,1)}, f32[8,1,256]{2,1,0:T(1,128)}) custom-call(bf16[2048,256]{1,0:T(8,128)(2,1)} %refs_5_.3, bf16[256,2048]{1,0:T(8,128)(2,1)} %refs_9_.3, f32[1,256]{1,0:T(1,128)} %bitcast.104), custom_call_target="tpu_custom_call" | custom-call | bytes 125829120 | tf_op jit(solution)/shard_map/gather_weights/pallas_call | solution.py:288
  59.0 0.0 copy-start.5
  59.1 0.0 copy-start.6
  59.1 0.0 all-gather.2.cloned.1.call-update
  59.1 0.0 reduce-scatter.6.cloned.1.call-start
  59.2 0.0 copy-done.1
  59.2 0.2 convert_reduce_fusion
  59.4 0.4 fusion.3
  59.8 0.2 copy-done.5
  60.1 0.1 constant_dynamic-update-slice_fusion.1
  60.2 0.1 copy-done.6
  60.2 0.1 constant_dynamic-update-slice_fusion.wkv_ref
  60.4 0.0 copy-start.7
  60.4 1.1 fusion.40
  61.5 1.2 fusion.17.kv_ref
  62.8 33.0 %gather_rest.1 = (bf16[2048,2048]{1,0:T(8,128)(2,1)}, bf16[2048,256]{1,0:T(8,128)(2,1)}) custom-call(bf16[2048,2048]{1,0:T(8,128)(2,1)} %get-tuple-element.70.in_ref, bf16[256,256]{1,0:T(8,128)(2,1)} %fusion.17.kv_ref), custom_call_target="tpu_custom_call", output_to_operand_aliasing={{0}: (0, {})} | custom-call | bytes 104857600 | tf_op jit(solution)/shard_map/gather_rest/pallas_call | solution.py:358
  95.8 0.0 copy-start.22
  95.8 0.0 copy-done.20
  95.8 0.1 convert_reduce_fusion.1
  95.9 0.1 dynamic_slice.12
  96.0 1.9 fusion.18
  97.9 0.0 copy-done.22
  97.9 6.9 %fusion.q_ref = bf16[256,2048]{1,0:T(8,128)(2,1)} fusion(bf16[2048,2048]{1,0:T(8,128)(2,1)} %get-tuple-element.68.wq_ref, f32[2048]{0:T(1024)S(1)} %bitcast.110, bf16[256,2048]{1,0:T(8,128)(2,1)S(1)} %copy-done.1, f32[2048]{0:T(1024)S(1)} %bitcast.101, f32[2048]{0:T(1024)S(1)} %bitcast.103, f32[256]{0:T(256)S(1)} %add_rsqrt_fusion, ...), kind=kOutput, calls=%fused_computation.3 | convolution fusion | flops 2151677952 | bytes 10512384 | tf_op jit(solution)/shard_map/dot_general | solution.py:29
  104.8 24.3 %attention_forward.1 = (bf16[256,2048]{1,0:T(8,128)(2,1)}, f32[8,2,256]{2,1,0:T(2,128)}) custom-call(bf16[256,2048]{1,0:T(8,128)(2,1)} %fusion.q_ref, bf16[2048,256]{1,0:T(8,128)(2,1)} %get-tuple-element.71.k_ref.v_ref.keys_ref, bf16[2048,256]{1,0:T(8,128)(2,1)} %get-tuple-element.71.k_ref.v_ref.keys_ref, f32[2048,256]{1,0:T(8,128)} %get-tuple-element.204.mask_ref), custom_call_target="tpu_custom_call" | custom-call | flops 8589934592 | bytes 2097152 | tf_op jit(solution)/shard_map/attention_forward/pallas_call | solution.py:833
  129.1 8.8 %project_out.1 = (f32[256,2048]{1,0:T(8,128)}, bf16[256,2048]{1,0:T(8,128)(2,1)}, f32[256,2048]{1,0:T(8,128)}, f32[256,128]{1,0:T(8,128)}) custom-call(bf16[256,2048]{1,0:T(8,128)(2,1)} %get-tuple-element.72.att_ref, bf16[256,2048]{1,0:T(8,128)(2,1)} %tok_ref.3, f32[6,2048]{1,0:T(8,128)} %vec_ref.3, bf16[2048,2048]{1,0:T(8,128)(2,1)} %get-tuple-element.73.w_ref.wo_ref), custom_call_target="tpu_custom_call" | custom-call | flops 2147483648 | bytes 58720256 | tf_op jit(solution)/shard_map/project_out/pallas_call | solution.py:387
  137.9 10.4 %all-gather.2.cloned.1.call-done = bf16[2048,2048]{1,0:T(8,128)(2,1)} async-done(((bf16[256,2048]{1,0:T(8,128)(2,1)}), bf16[2048,2048]{1,0:T(8,128)(2,1)}) %all-gather.2.cloned.1.call-update) | async-done | bytes 8388624 | tf_op jit(solution)/shard_map/all_gather | solution.py:1611
  148.4 149.0 %mixer_pass.1 = (bf16[4,2,2,128,2048]{4,3,2,1,0:T(8,128)(2,1)}, bf16[4,2,2,128,1024]{4,3,2,1,0:T(8,128)(2,1)}, bf16[4,2,2,128,1024]{4,3,2,1,0:T(8,128)(2,1)}, bf...) custom-call(s32[16]{0:T(128)} %owner_ref.3, ...), custom_call_target="tpu_custom_call" | custom-call | flops 51539607552 | bytes 314572800 | tf_op jit(solution)/shard_map/mixer_pass/pallas_call | solution.py:753
  297.3 0.0 reduce-scatter.6.cloned.1.call-update
  297.4 0.0 reduce-scatter.10.cloned.1.call-start
  297.4 0.7 reduce-scatter.10.cloned.1.call-update
  298.1 0.0 reduce-scatter.8.cloned.1.call-start
  298.1 0.0 copy-start.23
  298.2 0.5 reduce-scatter.8.cloned.1.call-update
  298.7 0.1 copy-done.23
  298.8 0.6 dynamic_slice.13.ids_ref
  299.4 0.6 reduce_sum.39
  300.1 147.6 %backward_pass.1 = (f32[256,2048]{1,0:T(8,128)}, bf16[1,256,512]{2,1,0:T(8,128)(2,1)}, bf16[1,256,512]{2,1,0:T(8,128)(2,1)}, f32[4,64,256]{2,1,0:T(8,128)}, f32[8,8,256]{2,1,0:T(8,128)}, /*index=5*/f32[8,128]{1,0:T(8,128)}) custom-call(s32[16]{0:T(128)} %owner_ref.3, f32[256,2048]{1,0:T(8,128)} %bitcast.111, bf16[256,2048]{1,0:T(8,128)(2,1)} %cot_ref.1, ...), custom_call_target="tpu_custom_call" | custom-call | flops 30064771072 | bytes 209715200 | tf_op jit(solution)/shard_map/backward_pass/pallas_call | solution.py:1327
  447.7 1.5 divide_subtract_fusion
  449.2 0.6 slice.54
  449.8 0.6 slice.55
  450.4 0.8 slice.56
  451.3 0.0 copy-start.19
  451.3 0.0 copy-start.21
  451.3 0.0 copy-start.16
  451.3 0.0 copy-start.17
  451.4 6.1 %shampoo.3 = (f32[2,4,2,128,128]{4,3,2,1,0:T(8,128)}, f32[2,4,2,128,128]{4,3,2,1,0:T(8,128)}, f32[2,4,2,128,128]{4,3,2,1,0:T(8,128)}, f32[2,4,2,128,128]{4,3,2,1,0:T(8,128)}) custom-call(s32[4]{0:T(128)} %dynamic_slice.13.ids_ref, bf16[1,256,512]{2,1,0:T(8,128)(2,1)} %get-tuple-element.95.refs_0_, bf16[1,256,512]{2,1,0:T(8,128)(2,1)} %get-tuple-element.96.refs_1_, ...), custom_call_target="tpu_custom_call" | custom-call | flops 536870912 | bytes 10485760 | tf_op jit(solution)/shard_map/shampoo/pallas_call | solution.py:1495
  457.5 0.7 divide_subtract_fusion.2
  458.1 0.5 divide_subtract_fusion.3
  458.7 0.6 divide_subtract_fusion.1
  459.3 0.7 fusion.25
  460.0 16.8 %shampoo.2 = (f32[2,4,8,128,128]{4,3,2,1,0:T(8,128)}, f32[2,4,8,128,128]{4,3,2,1,0:T(8,128)}, f32[2,4,8,128,128]{4,3,2,1,0:T(8,128)}, f32[2,4,8,128,128]{4,3,2,1,0:T(8,128)}) custom-call(s32[4]{0:T(128)} %dynamic_slice.13.ids_ref, bf16[1,512,1024]{2,1,0:T(8,128)(2,1)} %reduce-scatter.10.cloned.1.call-done.refs_0_, bf16[4,512,1024]{2,1,0:T(8,128)(2,1)} %bitcast.78, ...), custom_call_target="tpu_custom_call" | custom-call | flops 2147483648 | bytes 41943040 | tf_op jit(solution)/shard_map/shampoo/pallas_call | solution.py:1495
  476.8 0.0 copy-start.2
  476.9 0.4 fusion.20
  477.3 1.3 fusion.16
  478.6 2.3 fusion.13
  480.9 0.8 reduce-scatter.8.cloned.1.call-done
  481.7 2.0 fusion.10
  483.7 2.8 add_add_fusion
  486.5 1.3 copy.89
  487.8 0.6 copy.90
  488.5 0.6 copy.91
  (39 shorter events, 0.1 us)
Async XLA Ops:
  7.2 469.6 %copy-start = (f32[2,2,1,128,128]{4,3,2,1,0:T(8,128)S(1)}, f32[2,2,1,128,128]{4,3,2,1,0:T(8,128)}, u32[]{:S(2)}) copy-start(f32[2,2,1,128,128]{4,3,2,1,0:T(8,128)} %param.54) | copy-start | bytes 786436
  7.2 52.0 %copy-start.1 = (bf16[256,2048]{1,0:T(8,128)(2,1)S(1)}, bf16[256,2048]{1,0:T(8,128)(2,1)}, u32[]{:S(2)}) copy-start(bf16[256,2048]{1,0:T(8,128)(2,1)} %tok_ref.3) | copy-start | bytes 3145732
  7.2 51.9 %copy-start.18 = (f32[128]{0:T(128)S(1)}, f32[128]{0:T(128)}, u32[]{:S(2)}) copy-start(f32[128]{0:T(128)} %param.36) | copy-start | bytes 1540
  7.2 141.1 %all-gather.2.cloned.1.call-start = ((), (), s32[]{:S(2)}) async-start(), calls=%async_computation.3 | async-start | bytes 9437184 | tf_op jit(solution)/shard_map/all_gather | solution.py:1611
  59.0 1.0 copy-start.5
  59.1 1.2 copy-start.6
  59.1 400.2 %reduce-scatter.6.cloned.1.call-start = ((), (), s32[]{:S(2)}) async-start(), calls=%async_computation.4 | async-start | bytes 4718592 | tf_op jit(solution)/shard_map/reduce_scatter | solution.py:1629
  60.4 239.0 %copy-start.7 = (bf16[2048,256]{1,0:T(8,128)(2,1)}, bf16[2048,256]{1,0:T(8,128)(2,1)S(1)}, u32[]{:S(2)}) copy-start(bf16[2048,256]{1,0:T(8,128)(2,1)S(1)} %constant_dynamic-update-slice_fusion.wkv_ref) | copy-start | bytes 3145732
  62.8 33.1 %copy-start.20 = (s32[1,4]{1,0:T(1,128)S(1)}, s32[1,4]{1,0:T(1,128)}, u32[]{:S(2)}) copy-start(s32[1,4]{1,0:T(1,128)} %param.32) | copy-start | bytes 52
  95.8 2.1 copy-start.22
  297.4 161.9 %reduce-scatter.10.cloned.1.call-start = ((), (), s32[]{:S(2)}) async-start(), calls=%async_computation.6 | async-start | bytes 5242880
  298.1 183.6 %reduce-scatter.8.cloned.1.call-start = ((), (), s32[]{:S(2)}) async-start(), calls=%async_computation.5 | async-start | bytes 4718592 | tf_op jit(solution)/shard_map/reduce_scatter | solution.py:1655
  298.1 0.7 copy-start.23
  298.2 1.3 copy-start.13
  300.1 147.6 %copy-start.8 = (f32[6,2048]{1,0:T(8,128)S(1)}, f32[6,2048]{1,0:T(8,128)}, u32[]{:S(2)}) copy-start(f32[6,2048]{1,0:T(8,128)} %vec_ref.3) | copy-start | bytes 147460
  300.1 147.6 %copy-start.12 = (f32[6,2048]{1,0:T(8,128)S(1)}, f32[6,2048]{1,0:T(8,128)}, u32[]{:S(2)}) copy-start(f32[6,2048]{1,0:T(8,128)} %param.56) | copy-start | bytes 147460
  451.3 6.2 %copy-start.15 = (f32[256]{0:T(256)S(1)}, f32[256]{0:T(256)}, u32[]{:S(2)}) copy-start(f32[256]{0:T(256)} %param.35) | copy-start | bytes 3076
  451.3 6.2 %copy-start.19 = (f32[256]{0:T(256)S(1)}, f32[256]{0:T(256)}, u32[]{:S(2)}) copy-start(f32[256]{0:T(256)} %param.57) | copy-start | bytes 3076
  451.3 6.8 %copy-start.9 = (f32[8,8,256]{2,1,0:T(8,128)S(1)}, f32[8,8,256]{2,1,0:T(8,128)}, u32[]{:S(2)}) copy-start(f32[8,8,256]{2,1,0:T(8,128)} %get-tuple-element.93) | copy-start | bytes 196612
  451.3 6.8 %copy-start.21 = (f32[128]{0:T(128)S(1)}, f32[128]{0:T(128)}, u32[]{:S(2)}) copy-start(f32[128]{0:T(128)} %param.58) | copy-start | bytes 1540
  451.3 7.4 %copy-start.14 = (f32[8,128]{1,0:T(8,128)S(1)}, f32[8,128]{1,0:T(8,128)}, u32[]{:S(2)}) copy-start(f32[8,128]{1,0:T(8,128)} %get-tuple-element.94) | copy-start | bytes 12292
  451.3 7.3 %copy-start.16 = (f32[1024]{0:T(1024)S(1)}, f32[1024]{0:T(1024)}, u32[]{:S(2)}) copy-start(f32[1024]{0:T(1024)} %param.37) | copy-start | bytes 12292
  451.3 7.3 %copy-start.17 = (f32[1024]{0:T(1024)S(1)}, f32[1024]{0:T(1024)}, u32[]{:S(2)}) copy-start(f32[1024]{0:T(1024)} %param.59) | copy-start | bytes 12292
  451.3 8.0 %copy-start.11 = (f32[4,64,256]{2,1,0:T(8,128)S(1)}, f32[4,64,256]{2,1,0:T(8,128)}, u32[]{:S(2)}) copy-start(f32[4,64,256]{2,1,0:T(8,128)} %get-tuple-element.104) | copy-start | bytes 786436
  460.0 17.2 %copy-start.10 = (f32[2,2,1,128,128]{4,3,2,1,0:T(8,128)S(1)}, f32[2,2,1,128,128]{4,3,2,1,0:T(8,128)}, u32[]{:S(2)}) copy-start(f32[2,2,1,128,128]{4,3,2,1,0:T(8,128)} %param.53) | copy-start | bytes 786436
  476.8 6.9 %copy-start.2 = (f32[256,2048]{1,0:T(8,128)S(1)}, f32[256,2048]{1,0:T(8,128)}, u32[]{:S(2)}) copy-start(f32[256,2048]{1,0:T(8,128)} %get-tuple-element.74) | copy-start | bytes 6291460
  476.9 6.9 %copy-start.4 = (bf16[128,2048]{1,0:T(8,128)(2,1)S(1)}, bf16[128,2048]{1,0:T(8,128)(2,1)}, u32[]{:S(2)}) copy-start(bf16[128,2048]{1,0:T(8,128)(2,1)} %reduce-scatter.6.cloned.1.call-done) | copy-start | bytes 1572868
  483.7 2.8 copy-start.3
Sparse Core Ops, SparseCore 0:
  59.2 89.1 all-gather.1
  297.5 47.2 reduce-scatter.5
  347.8 76.1 reduce-scatter.9
  426.2 55.3 reduce-scatter.7

commit v6 on v5

--- a/solution.py
+++ b/solution.py
@@ -411,7 +411,7 @@
     tiles = width // TILE
     owned = tiles // batch_size
     total_events = n * cuts
-    pieces = 2
+    pieces = 4
     piece = sub // pieces
 
     def kernel(

time: 504 us -> 504 us (level)
  no operation moved by 1% of the time
where the time goes in v6:
time: 504 us; the launch traced here: 496 us
  Pallas kernels  437 us (87%)
  between operations  14.4 us (3%)
  matrix products  14.2 us (3%)
  waiting for transfers between devices  13.4 us (3%)
  other arithmetic  10.1 us (2%)
  local copies, waits for them, and re-layouts  7.24 us (1%)
    pallas_call x1, Pallas kernels, mixer_pass(): pl.pallas_call(kernel, out_shape=(jax.ShapeDtypeStruct(block + (width,),...  149 us
    pallas_call x1, Pallas kernels, backward_pass(): pl.pallas_call(kernel, out_shape=(jax.ShapeDtypeStruct((tok, width), F32)...  147 us
    pallas_call x1, Pallas kernels, gather_weights(): pl.pallas_call(kernel, out_shape=(jax.ShapeDtypeStruct((rows, cols * head...  51.7 us
    pallas_call x1, Pallas kernels, gather_rest(): pl.pallas_call(kernel, out_shape=(jax.ShapeDtypeStruct(w_all.shape, w_all...  33 us
    pallas_call x1, Pallas kernels, attention_forward(): pl.pallas_call(kernel, grid=(slabs,), out_shape=(jax.ShapeDtypeStruct((to...  24.3 us
    pallas_call x2, Pallas kernels, shampoo(): pl.pallas_call(kernel, grid_spec=pltpu.PrefetchScalarGridSpec(num_scalar_...  22.9 us
    all_gather x1, waiting for transfers between devices, body(): cot_all = lax.all_gather(cotangent_later, 'head', axis=0, tiled=True)  10.4 us
  transfers between devices with their start and end apart: 4, of which 2 were waited for; matrix products, arithmetic and copies ran while one was open for 5% of the time, Pallas kernels for 48%

profile of v6, /device:TPU:0, one launch (start us, length us, event | category | flops | bytes accessed | tf_op | source)
XLA Modules:
  0.0 496.1 jit_solution(4847150600950706860)
XLA Ops:
  7.2 0.0 copy-start
  7.2 0.0 copy-start.1
  7.2 0.0 all-gather.2.cloned.1.call-start
  7.3 51.7 %gather_weights.1 = (bf16[2048,2048]{1,0:T(8,128)(2,1)}, bf16[2048,2048]{1,0:T(8,128)(2,1)}, f32[8,1,256]{2,1,0:T(1,128)}) custom-call(bf16[2048,256]{1,0:T(8,128)(2,1)} %refs_5_.3, bf16[256,2048]{1,0:T(8,128)(2,1)} %refs_9_.3, f32[1,256]{1,0:T(1,128)} %bitcast.104), custom_call_target="tpu_custom_call" | custom-call | bytes 125829120 | tf_op jit(solution)/shard_map/gather_weights/pallas_call | solution.py:288
  59.0 0.0 copy-start.5
  59.1 0.0 copy-start.6
  59.1 0.0 all-gather.2.cloned.1.call-update
  59.1 0.0 reduce-scatter.6.cloned.1.call-start
  59.2 0.2 convert_reduce_fusion
  59.4 0.4 fusion.3
  59.8 0.2 copy-done.5
  60.1 0.1 constant_dynamic-update-slice_fusion.1
  60.2 0.1 copy-done.6
  60.2 0.1 constant_dynamic-update-slice_fusion.wkv_ref
  60.4 0.0 copy-start.7
  60.4 1.1 fusion.40
  61.5 1.2 fusion.17.kv_ref
  62.8 33.0 %gather_rest.1 = (bf16[2048,2048]{1,0:T(8,128)(2,1)}, bf16[2048,256]{1,0:T(8,128)(2,1)}) custom-call(bf16[2048,2048]{1,0:T(8,128)(2,1)} %get-tuple-element.70.in_ref, bf16[256,256]{1,0:T(8,128)(2,1)} %fusion.17.kv_ref), custom_call_target="tpu_custom_call", output_to_operand_aliasing={{0}: (0, {})} | custom-call | bytes 104857600 | tf_op jit(solution)/shard_map/gather_rest/pallas_call | solution.py:358
  95.8 0.1 convert_reduce_fusion.1
  95.9 0.1 dynamic_slice.12
  96.0 1.9 fusion.18
  97.9 6.9 %fusion.q_ref = bf16[256,2048]{1,0:T(8,128)(2,1)} fusion(bf16[2048,2048]{1,0:T(8,128)(2,1)} %get-tuple-element.68.wq_ref, f32[2048]{0:T(1024)S(1)} %bitcast.110, bf16[256,2048]{1,0:T(8,128)(2,1)S(1)} %copy-done.1, f32[2048]{0:T(1024)S(1)} %bitcast.101, f32[2048]{0:T(1024)S(1)} %bitcast.103, f32[256]{0:T(256)S(1)} %add_rsqrt_fusion, ...), kind=kOutput, calls=%fused_computation.3 | convolution fusion | flops 2151677952 | bytes 10512384 | tf_op jit(solution)/shard_map/dot_general | solution.py:29
  104.8 24.3 %attention_forward.1 = (bf16[256,2048]{1,0:T(8,128)(2,1)}, f32[8,2,256]{2,1,0:T(2,128)}) custom-call(bf16[256,2048]{1,0:T(8,128)(2,1)} %fusion.q_ref, bf16[2048,256]{1,0:T(8,128)(2,1)} %get-tuple-element.71.k_ref.v_ref.keys_ref, bf16[2048,256]{1,0:T(8,128)(2,1)} %get-tuple-element.71.k_ref.v_ref.keys_ref, f32[2048,256]{1,0:T(8,128)} %get-tuple-element.204.mask_ref), custom_call_target="tpu_custom_call" | custom-call | flops 8589934592 | bytes 2097152 | tf_op jit(solution)/shard_map/attention_forward/pallas_call | solution.py:833
  129.1 8.8 %project_out.1 = (f32[256,2048]{1,0:T(8,128)}, bf16[256,2048]{1,0:T(8,128)(2,1)}, f32[256,2048]{1,0:T(8,128)}, f32[256,128]{1,0:T(8,128)}) custom-call(bf16[256,2048]{1,0:T(8,128)(2,1)} %get-tuple-element.72.att_ref, bf16[256,2048]{1,0:T(8,128)(2,1)} %tok_ref.3, f32[6,2048]{1,0:T(8,128)} %vec_ref.3, bf16[2048,2048]{1,0:T(8,128)(2,1)} %get-tuple-element.73.w_ref.wo_ref), custom_call_target="tpu_custom_call" | custom-call | flops 2147483648 | bytes 58720256 | tf_op jit(solution)/shard_map/project_out/pallas_call | solution.py:387
  137.9 10.4 %all-gather.2.cloned.1.call-done = bf16[2048,2048]{1,0:T(8,128)(2,1)} async-done(((bf16[256,2048]{1,0:T(8,128)(2,1)}), bf16[2048,2048]{1,0:T(8,128)(2,1)}) %all-gather.2.cloned.1.call-update) | async-done | bytes 8388624 | tf_op jit(solution)/shard_map/all_gather | solution.py:1611
  148.4 149.0 %mixer_pass.1 = (bf16[4,2,2,128,2048]{4,3,2,1,0:T(8,128)(2,1)}, bf16[4,2,2,128,1024]{4,3,2,1,0:T(8,128)(2,1)}, bf16[4,2,2,128,1024]{4,3,2,1,0:T(8,128)(2,1)}, bf...) custom-call(s32[16]{0:T(128)} %owner_ref.3, ...), custom_call_target="tpu_custom_call" | custom-call | flops 51539607552 | bytes 314572800 | tf_op jit(solution)/shard_map/mixer_pass/pallas_call | solution.py:753
  297.4 0.0 reduce-scatter.6.cloned.1.call-update
  297.4 0.0 reduce-scatter.10.cloned.1.call-start
  297.5 0.7 reduce-scatter.10.cloned.1.call-update
  298.1 0.0 reduce-scatter.8.cloned.1.call-start
  298.2 0.0 copy-start.23
  298.2 0.5 reduce-scatter.8.cloned.1.call-update
  298.7 0.1 copy-done.23
  298.8 0.6 dynamic_slice.13.ids_ref
  299.5 0.0 copy-done.13
  299.5 0.6 reduce_sum.39
  300.1 146.8 %backward_pass.1 = (f32[256,2048]{1,0:T(8,128)}, bf16[1,256,512]{2,1,0:T(8,128)(2,1)}, bf16[1,256,512]{2,1,0:T(8,128)(2,1)}, f32[4,64,256]{2,1,0:T(8,128)}, f32[8,8,256]{2,1,0:T(8,128)}, /*index=5*/f32[8,128]{1,0:T(8,128)}) custom-call(s32[16]{0:T(128)} %owner_ref.3, f32[256,2048]{1,0:T(8,128)} %bitcast.111, bf16[256,2048]{1,0:T(8,128)(2,1)} %cot_ref.1, ...), custom_call_target="tpu_custom_call" | custom-call | flops 30064771072 | bytes 209715200 | tf_op jit(solution)/shard_map/backward_pass/pallas_call | solution.py:1327
  446.9 1.5 divide_subtract_fusion
  448.5 0.6 slice.54
  449.1 0.6 slice.55
  449.7 0.8 slice.56
  450.6 0.0 copy-start.19
  450.6 0.0 copy-start.9
  450.6 0.0 copy-start.21
  450.6 0.0 copy-start.16
  450.6 0.0 copy-start.17
  450.6 0.0 copy-start.11
  450.6 6.1 %shampoo.3 = (f32[2,4,2,128,128]{4,3,2,1,0:T(8,128)}, f32[2,4,2,128,128]{4,3,2,1,0:T(8,128)}, f32[2,4,2,128,128]{4,3,2,1,0:T(8,128)}, f32[2,4,2,128,128]{4,3,2,1,0:T(8,128)}) custom-call(s32[4]{0:T(128)} %dynamic_slice.13.ids_ref, bf16[1,256,512]{2,1,0:T(8,128)(2,1)} %get-tuple-element.95.refs_0_, bf16[1,256,512]{2,1,0:T(8,128)(2,1)} %get-tuple-element.96.refs_1_, ...), custom_call_target="tpu_custom_call" | custom-call | flops 536870912 | bytes 10485760 | tf_op jit(solution)/shard_map/shampoo/pallas_call | solution.py:1495
  456.8 0.7 divide_subtract_fusion.2
  457.4 0.5 divide_subtract_fusion.3
  458.0 0.0 copy-done.17
  458.0 0.6 divide_subtract_fusion.1
  458.6 0.7 fusion.25
  459.4 16.8 %shampoo.2 = (f32[2,4,8,128,128]{4,3,2,1,0:T(8,128)}, f32[2,4,8,128,128]{4,3,2,1,0:T(8,128)}, f32[2,4,8,128,128]{4,3,2,1,0:T(8,128)}, f32[2,4,8,128,128]{4,3,2,1,0:T(8,128)}) custom-call(s32[4]{0:T(128)} %dynamic_slice.13.ids_ref, bf16[1,512,1024]{2,1,0:T(8,128)(2,1)} %reduce-scatter.10.cloned.1.call-done.refs_0_, bf16[4,512,1024]{2,1,0:T(8,128)(2,1)} %bitcast.78, ...), custom_call_target="tpu_custom_call" | custom-call | flops 2147483648 | bytes 41943040 | tf_op jit(solution)/shard_map/shampoo/pallas_call | solution.py:1495
  476.1 0.0 copy-start.2
  476.1 0.4 fusion.20
  476.5 1.3 fusion.16
  477.8 2.3 fusion.13
  480.1 1.8 reduce-scatter.8.cloned.1.call-done
  481.9 2.0 fusion.10
  484.0 2.8 add_add_fusion
  486.8 1.3 copy.89
  488.1 0.6 copy.90
  488.7 0.6 copy.91
  (39 shorter events, 0.1 us)
Async XLA Ops:
  7.2 468.9 %copy-start = (f32[2,2,1,128,128]{4,3,2,1,0:T(8,128)S(1)}, f32[2,2,1,128,128]{4,3,2,1,0:T(8,128)}, u32[]{:S(2)}) copy-start(f32[2,2,1,128,128]{4,3,2,1,0:T(8,128)} %param.54) | copy-start | bytes 786436
  7.2 52.0 %copy-start.1 = (bf16[256,2048]{1,0:T(8,128)(2,1)S(1)}, bf16[256,2048]{1,0:T(8,128)(2,1)}, u32[]{:S(2)}) copy-start(bf16[256,2048]{1,0:T(8,128)(2,1)} %tok_ref.3) | copy-start | bytes 3145732
  7.2 51.9 %copy-start.18 = (f32[128]{0:T(128)S(1)}, f32[128]{0:T(128)}, u32[]{:S(2)}) copy-start(f32[128]{0:T(128)} %param.36) | copy-start | bytes 1540
  7.2 141.1 %all-gather.2.cloned.1.call-start = ((), (), s32[]{:S(2)}) async-start(), calls=%async_computation.3 | async-start | bytes 9437184 | tf_op jit(solution)/shard_map/all_gather | solution.py:1611
  59.0 1.0 copy-start.5
  59.1 1.2 copy-start.6
  59.1 399.5 %reduce-scatter.6.cloned.1.call-start = ((), (), s32[]{:S(2)}) async-start(), calls=%async_computation.4 | async-start | bytes 4718592 | tf_op jit(solution)/shard_map/reduce_scatter | solution.py:1629
  60.4 239.1 %copy-start.7 = (bf16[2048,256]{1,0:T(8,128)(2,1)}, bf16[2048,256]{1,0:T(8,128)(2,1)S(1)}, u32[]{:S(2)}) copy-start(bf16[2048,256]{1,0:T(8,128)(2,1)S(1)} %constant_dynamic-update-slice_fusion.wkv_ref) | copy-start | bytes 3145732
  62.8 33.1 %copy-start.20 = (s32[1,4]{1,0:T(1,128)S(1)}, s32[1,4]{1,0:T(1,128)}, u32[]{:S(2)}) copy-start(s32[1,4]{1,0:T(1,128)} %param.32) | copy-start | bytes 52
  95.8 2.1 copy-start.22
  297.4 161.2 %reduce-scatter.10.cloned.1.call-start = ((), (), s32[]{:S(2)}) async-start(), calls=%async_computation.6 | async-start | bytes 5242880
  298.1 183.8 %reduce-scatter.8.cloned.1.call-start = ((), (), s32[]{:S(2)}) async-start(), calls=%async_computation.5 | async-start | bytes 4718592 | tf_op jit(solution)/shard_map/reduce_scatter | solution.py:1655
  298.2 0.7 copy-start.23
  298.2 1.3 copy-start.13
  300.1 146.8 %copy-start.8 = (f32[6,2048]{1,0:T(8,128)S(1)}, f32[6,2048]{1,0:T(8,128)}, u32[]{:S(2)}) copy-start(f32[6,2048]{1,0:T(8,128)} %vec_ref.3) | copy-start | bytes 147460
  300.1 146.8 %copy-start.12 = (f32[6,2048]{1,0:T(8,128)S(1)}, f32[6,2048]{1,0:T(8,128)}, u32[]{:S(2)}) copy-start(f32[6,2048]{1,0:T(8,128)} %param.56) | copy-start | bytes 147460
  450.6 6.2 %copy-start.15 = (f32[256]{0:T(256)S(1)}, f32[256]{0:T(256)}, u32[]{:S(2)}) copy-start(f32[256]{0:T(256)} %param.35) | copy-start | bytes 3076
  450.6 6.2 %copy-start.19 = (f32[256]{0:T(256)S(1)}, f32[256]{0:T(256)}, u32[]{:S(2)}) copy-start(f32[256]{0:T(256)} %param.57) | copy-start | bytes 3076
  450.6 6.9 %copy-start.9 = (f32[8,8,256]{2,1,0:T(8,128)S(1)}, f32[8,8,256]{2,1,0:T(8,128)}, u32[]{:S(2)}) copy-start(f32[8,8,256]{2,1,0:T(8,128)} %get-tuple-element.93) | copy-start | bytes 196612
  450.6 6.9 %copy-start.21 = (f32[128]{0:T(128)S(1)}, f32[128]{0:T(128)}, u32[]{:S(2)}) copy-start(f32[128]{0:T(128)} %param.58) | copy-start | bytes 1540
  450.6 7.4 %copy-start.14 = (f32[8,128]{1,0:T(8,128)S(1)}, f32[8,128]{1,0:T(8,128)}, u32[]{:S(2)}) copy-start(f32[8,128]{1,0:T(8,128)} %get-tuple-element.94) | copy-start | bytes 12292
  450.6 7.4 %copy-start.16 = (f32[1024]{0:T(1024)S(1)}, f32[1024]{0:T(1024)}, u32[]{:S(2)}) copy-start(f32[1024]{0:T(1024)} %param.37) | copy-start | bytes 12292
  450.6 7.4 %copy-start.17 = (f32[1024]{0:T(1024)S(1)}, f32[1024]{0:T(1024)}, u32[]{:S(2)}) copy-start(f32[1024]{0:T(1024)} %param.59) | copy-start | bytes 12292
  450.6 8.0 %copy-start.11 = (f32[4,64,256]{2,1,0:T(8,128)S(1)}, f32[4,64,256]{2,1,0:T(8,128)}, u32[]{:S(2)}) copy-start(f32[4,64,256]{2,1,0:T(8,128)} %get-tuple-element.104) | copy-start | bytes 786436
  459.4 17.2 %copy-start.10 = (f32[2,2,1,128,128]{4,3,2,1,0:T(8,128)S(1)}, f32[2,2,1,128,128]{4,3,2,1,0:T(8,128)}, u32[]{:S(2)}) copy-start(f32[2,2,1,128,128]{4,3,2,1,0:T(8,128)} %param.53) | copy-start | bytes 786436
  476.1 7.9 %copy-start.2 = (f32[256,2048]{1,0:T(8,128)S(1)}, f32[256,2048]{1,0:T(8,128)}, u32[]{:S(2)}) copy-start(f32[256,2048]{1,0:T(8,128)} %get-tuple-element.74) | copy-start | bytes 6291460
  476.1 7.8 %copy-start.4 = (bf16[128,2048]{1,0:T(8,128)(2,1)S(1)}, bf16[128,2048]{1,0:T(8,128)(2,1)}, u32[]{:S(2)}) copy-start(bf16[128,2048]{1,0:T(8,128)(2,1)} %reduce-scatter.6.cloned.1.call-done) | copy-start | bytes 1572868
  484.0 2.8 copy-start.3
Sparse Core Ops, SparseCore 0:
  59.2 89.1 all-gather.1
  297.5 47.5 reduce-scatter.5
  348.1 76.3 reduce-scatter.9
  426.7 55.2 reduce-scatter.7
